TPU v7x, 256 devices: a whole 4x4x8 slice. The times are simulated.
256 devices in a mesh: grp: 8 (over z), seq: 16 (over y, x), resp: 2 (over core).
Axes of the slice: x: 4, y: 4, z: 8, core: 2. Of those that a mesh axis runs over, the one named last changes fastest.
Arguments:
- prompt_xbc: bfloat16 [65536, 5376], P(('grp', 'seq', 'resp')), parts along dimension 0, may hold values from -6 to 6
- prompt_z: bfloat16 [65536, 5120], P(('grp', 'seq', 'resp')), parts along dimension 0, may hold values from -6 to 6
- prompt_step: float32 [80, 65536], P(None, ('grp', 'seq', 'resp')), parts along dimension 1, may hold values from 0 to 0.2
- prompt_keep: float32 [80, 65536], P(None, ('grp', 'seq', 'resp')), parts along dimension 1, may hold values from -0.6 to 0
- resp_xbc: bfloat16 [256, 128, 5376], P(('grp', 'seq', 'resp')), parts along dimension 0, may hold values from -6 to 6
- resp_z: bfloat16 [256, 128, 5120], P(('grp', 'seq', 'resp')), parts along dimension 0, may hold values from -6 to 6
- resp_step: float32 [80, 256, 128], P(None, ('grp', 'seq', 'resp')), parts along dimension 1, may hold values from 0 to 0.2
- resp_keep: float32 [80, 256, 128], P(None, ('grp', 'seq', 'resp')), parts along dimension 1, may hold values from -0.6 to 0
- resp_len: int32 [256], P(('grp', 'seq', 'resp')), parts along dimension 0, may hold values from 32 to 128, as said below
- conv_weight: float32 [4, 5376], replicated, may hold values from -3 to 3
- conv_bias: float32 [5376], replicated, may hold values from -3 to 3
- skip: float32 [80], replicated, may hold values from 0.5 to 1.5
- gain: float32 [5120], replicated, may hold values from 0.25 to 1.75
Outputs:
- prompt_out: bfloat16 [65536, 5120], P(('grp', 'seq', 'resp')), parts along dimension 0
- resp_out: bfloat16 [256, 128, 5120], P(('grp', 'seq', 'resp')), parts along dimension 0
There are 8 independent parts, one for each index of `grp`. A program takes and returns all parts, laid end to end along the dimension named above; an argument that names none is the same for every part. Nothing has to cross between parts.
Inputs may be any that keep to these rules, and one draw needn't show every extreme that they name: `resp_len`: some response fills all 128 positions.
All inputs are finite; a program needn't handle non-finite values.
Results may differ from a plain program's by a relative error of at most 0.0034.
Values may be sent and summed in bfloat16 or wider, within the bound.
No kernel may reach another device: no remote copies, remote signals or barrier semaphores. Data moves between devices by JAX's collectives and lax.ppermute only.
A program may use at most 256 MiB of HBM per device.

v0:
```python
import jax
import jax.numpy as jnp
from jax import lax
from jax.sharding import PartitionSpec as P

HEADS = 80
HEAD_DIM = 64
STATE = 128
KERNEL = 4
BLOCK = 128
D_INNER = 5120


EPS = 1e-05


def shifted(shard, axis, by):
    count = lax.axis_size(axis)
    pairs = [(i, i + by) for i in range(count) if 0 <= i + by < count]
    return lax.ppermute(shard, axis, pairs)


def prefix(value, axis, join, neutral):
    count, mine = (lax.axis_size(axis), lax.axis_index(axis))
    pieces = jax.tree.map(lambda part: lax.all_gather(part, axis), value)
    running = jax.tree.map(
        lambda part, zero: jnp.full_like(part, 0) + jnp.asarray(zero, part.dtype), value, neutral
    )

    def lap(position, running):
        longer = join(running, jax.tree.map(lambda part: part[position], pieces))
        return jax.tree.map(lambda new, old: jnp.where(position < mine, new, old), longer, running)

    return lax.fori_loop(0, count - 1, lap, running)


def from_root(block, axis, source):
    block = jnp.where(lax.axis_index(axis) == source, block, jnp.zeros_like(block))
    return lax.psum(block, axis)


def conv_silu(input_rows, history, conv_weight, conv_bias):
    row_count = input_rows.shape[0]
    padded = jnp.concatenate([history, input_rows], axis=0).astype(jnp.float32)
    conv_total = jnp.broadcast_to(conv_bias[None, :], (row_count, conv_bias.shape[0]))
    for offset in range(KERNEL):
        conv_total = conv_total + conv_weight[offset][None, :] * padded[offset : offset + row_count]
    return jax.nn.silu(conv_total).astype(jnp.bfloat16)


def block_local(activations, step_rows, keep_rows, want_state):
    row_count = activations.shape[0]
    values = activations[:, :D_INNER].reshape(row_count, HEADS, HEAD_DIM)
    key_rows = activations[:, D_INNER : D_INNER + STATE]
    queries = activations[:, D_INNER + STATE :]
    log_cum = jnp.cumsum(keep_rows, axis=1)
    scores = jnp.dot(queries, key_rows.T, preferred_element_type=jnp.float32)
    token_places = jnp.arange(row_count)
    causal = token_places[:, None] >= token_places[None, :]
    row_factor = jnp.exp(log_cum)
    col_factor = jnp.exp(-log_cum) * step_rows
    product_rows = row_factor[:, :, None] * scores[None] * col_factor[:, None, :]
    mixing = jnp.where(causal[None], product_rows, 0.0).astype(jnp.bfloat16)
    within = jnp.einsum("hts,shp->thp", mixing, values, preferred_element_type=jnp.float32)
    added_state = None
    if want_state:
        tail_weight = jnp.exp(log_cum[:, -1:] - log_cum) * step_rows
        weighted = (values.astype(jnp.float32) * tail_weight.T[:, :, None]).astype(jnp.bfloat16)
        added_state = jnp.einsum(
            "thp,tn->hpn", weighted, key_rows, preferred_element_type=jnp.float32
        )
    return (within, added_state, log_cum)


def carried(queries, carry_state, log_cum):
    carried_part = jnp.einsum(
        "tn,hpn->thp",
        queries,
        carry_state,
        precision=lax.Precision.HIGHEST,
        preferred_element_type=jnp.float32,
    )
    return carried_part * jnp.exp(log_cum).T[:, :, None]


def run_device(activations, step_rows, keep_rows, block, want_state):
    row_count = activations.shape[0]
    block_count = row_count // block
    queries = activations[:, D_INNER + STATE :].astype(jnp.float32)
    block_outs = []
    carry_state = None
    for index in range(block_count):
        row_start = index * block
        needed = want_state or index + 1 < block_count
        within, added_state, log_cum = block_local(
            activations[row_start : row_start + block],
            step_rows[:, row_start : row_start + block],
            keep_rows[:, row_start : row_start + block],
            needed,
        )
        if carry_state is not None:
            within = within + carried(queries[row_start : row_start + block], carry_state, log_cum)
            carry_state = jnp.exp(log_cum[:, -1])[:, None, None] * carry_state + added_state
        else:
            carry_state = added_state
        block_outs.append(within)
    return (jnp.concatenate(block_outs, axis=0), carry_state)


def finish(pre_norm, activations, gate_rows, skip, gain):
    row_count = pre_norm.shape[0]
    values = activations[:, :D_INNER].astype(jnp.float32).reshape(row_count, HEADS, HEAD_DIM)
    mixed_sum = (pre_norm + skip[None, :, None] * values).reshape(row_count, D_INNER)
    gated_rows = mixed_sum * jax.nn.silu(gate_rows.astype(jnp.float32))
    inv_rms = lax.rsqrt(jnp.mean(gated_rows * gated_rows, axis=1, keepdims=True) + EPS)
    return (gated_rows * inv_rms * gain[None, :]).astype(jnp.bfloat16)


def compose(earlier, latter):
    return (earlier[0] * latter[0], latter[0][:, None, None] * earlier[1] + latter[1])


def shards(
    prompt_xbc,
    prompt_z,
    prompt_step,
    prompt_keep,
    resp_xbc,
    resp_z,
    resp_step,
    resp_keep,
    resp_len,
    conv_weight,
    conv_bias,
    skip,
    gain,
):
    device_count = lax.axis_size(("seq", "resp"))
    own_rows = prompt_xbc[prompt_xbc.shape[0] - (KERNEL - 1) :]
    history = shifted(own_rows, ("seq", "resp"), 1)
    prompt_acts = conv_silu(prompt_xbc, history, conv_weight, conv_bias)
    within, local_state = run_device(prompt_acts, prompt_step, prompt_keep, BLOCK, True)
    running = jnp.cumsum(prompt_keep, axis=1)
    through = jnp.exp(running[:, -1])
    identity = (jnp.ones_like(through), jnp.zeros_like(local_state))
    before, entering = prefix((through, local_state), ("seq", "resp"), compose, identity)
    queries = prompt_acts[:, D_INNER + STATE :].astype(jnp.float32)
    pre_norm = within + carried(queries, entering, running)
    prompt_out = finish(pre_norm, prompt_acts, prompt_z, skip, gain)
    ending = through[:, None, None] * entering + local_state
    final_state, tail_wide = (
        from_root(ending, ("seq", "resp"), device_count - 1),
        from_root(own_rows.astype(jnp.float32), ("seq", "resp"), device_count - 1),
    )
    last_rows = tail_wide.astype(jnp.bfloat16)
    resp_positions = resp_xbc.shape[1]
    response_block = min(BLOCK, resp_positions)
    token_places = jnp.arange(resp_positions)

    def respond(pieces):
        input_rows, gate_rows, step_rows, keep_rows, length = pieces
        activations = conv_silu(input_rows, last_rows, conv_weight, conv_bias)
        within_resp, unused = run_device(activations, step_rows, keep_rows, response_block, False)
        resp_running = jnp.cumsum(keep_rows, axis=1)
        resp_queries = activations[:, D_INNER + STATE :].astype(jnp.float32)
        pre_resp = within_resp + carried(resp_queries, final_state, resp_running)
        finished = finish(pre_resp, activations, gate_rows, skip, gain)
        return jnp.where((token_places < length)[:, None], finished, jnp.zeros_like(finished))

    resp_out = lax.map(
        respond,
        (
            resp_xbc,
            resp_z,
            jnp.transpose(resp_step, (1, 0, 2)),
            jnp.transpose(resp_keep, (1, 0, 2)),
            resp_len,
        ),
    )
    return (prompt_out, resp_out)


def solution(mesh):
    return jax.shard_map(
        shards,
        mesh=mesh,
        in_specs=(
            P(("grp", "seq", "resp"), None),
            P(("grp", "seq", "resp"), None),
            P(None, ("grp", "seq", "resp")),
            P(None, ("grp", "seq", "resp")),
            P(("grp", "seq", "resp"), None, None),
            P(("grp", "seq", "resp"), None, None),
            P(None, ("grp", "seq", "resp"), None),
            P(None, ("grp", "seq", "resp"), None),
            P(("grp", "seq", "resp")),
            P(),
            P(),
            P(),
            P(),
        ),
        out_specs=(P(("grp", "seq", "resp"), None), P(("grp", "seq", "resp"), None, None)),
        check_vma=False,
    )
```

profile of v0, /device:TPU:1, one launch (start us, length us, event | category | flops | bytes accessed | tf_op | source)
XLA Modules:
  0.0 508.1 jit_solution(13911984617777442369)
XLA Ops:
  8.1 4.5 collective-permute-start
  16.7 2.3 maximum_convert_fusion
  19.0 3.5 multiply_convert_fusion
  22.6 2.0 fusion.61
  24.6 2.4 copy.63
  27.0 2.4 copy.64
  29.4 1.9 fusion.34
  31.4 1.5 copy-done.2
  32.9 2.1 multiply_add_fusion
  39.3 123.8 %all-reduce.1 = (f32[2560]{0:T(1024)S(1)}, bf16[3,5376]{1,0:T(4,128)(2,1)S(1)}) all-reduce(f32[2560]{0:T(1024)S(1)} %dynamic-update-slice, f32[3,5376]{1,0:T(4,128)S(1)} %convert_select_fusion), channel_id=2, replica_groups=mesh['grp'=8,'seq'=16,'resp'=2] {'seq','resp'}, use_global_device_ids=true, to_apply=%add | all-reduce | flops 18688 | bytes 117248
  163.2 1.7 maximum_convert_fusion.1
  164.9 1.8 multiply_convert_fusion.2
  169.0 2.4 copy.73
  171.8 3.0 copy.78
  176.6 4.8 slice_convert_fusion
  181.3 6.0 %copy.71 = f32[256,5120]{0,1:T(8,128)} copy(f32[256,5120]{1,0:T(8,128)} %slice_convert_fusion) | data formatting | bytes 10485760 | tf_op jit(solution)/shard_map/reshape | solution.py:112
  189.2 4.0 fusion.15
  193.2 3.6 fusion.33
  196.8 3.9 bitcast_add_fusion.2
  200.7 87.5 %all-gather.4.cloned.1.call-done = f32[2560,64,128]{2,1,0:T(8,128)} async-done(((f32[80,64,128]{2,1,0:T(8,128)}), f32[2560,64,128]{2,1,0:T(8,128)}) %all-gather.4.cloned.1.call-update) | async-done | bytes 83886096 | tf_op jit(solution)/shard_map/all_gather | solution.py:25
  288.2 74.3 %while.18 = (s32[]{:T(128)}, f32[80,64,128]{2,1,0:T(8,128)S(1)}, s32[]{:T(128)}, f32[32,80]{1,0:T(8,128)S(1)}, f32[32,80,64,128]{3,2,1,0:T(8,128)}, /*index=5*/s32[]{:T(128)}, s32[]{:T(128)}) while((s32[]{:T(128)}, f32[80,64,128]{2,1,0:T(8,128)S(1)}, s32[]{:T(128)}, f32[32,80]{1,0:T(8,128)S(1)}, f32[32,80,64,128]{3,2,1,0:T(8,128)}, ...), condition=%wide.region_5.6_spmd.clone, body=%wide.region_4.5_spmd.clone.sunk | while | flops 2621444 | bytes 7865385 | solution.py:34
  288.2 2.3 fusion.71
  290.6 2.4 fusion.71
  293.0 2.4 fusion.71
  295.4 2.4 fusion.71
  297.8 2.4 fusion.71
  300.2 2.4 fusion.71
  302.6 2.4 fusion.71
  305.0 2.4 fusion.71
  307.4 2.4 fusion.71
  309.8 2.4 fusion.71
  312.2 2.4 fusion.71
  314.6 2.4 fusion.71
  317.0 2.4 fusion.71
  319.4 2.4 fusion.71
  321.8 2.4 fusion.71
  324.2 2.4 fusion.71
  326.6 2.4 fusion.71
  329.0 2.4 fusion.71
  331.4 2.4 fusion.71
  333.8 2.4 fusion.71
  336.2 2.4 fusion.71
  338.6 2.4 fusion.71
  341.0 2.4 fusion.71
  343.4 2.4 fusion.71
  345.8 2.4 fusion.71
  348.2 2.4 fusion.71
  350.6 2.4 fusion.71
  353.0 2.4 fusion.71
  355.4 2.4 fusion.71
  357.8 2.4 fusion.71
  360.2 2.4 fusion.71
  362.6 3.5 add_select_fusion
  366.1 5.4 %fusion.37 = f32[256,80,64]{0,2,1:T(8,128)} fusion(f32[80,64,128]{2,1,0:T(8,128)S(1)} %get-tuple-element.138, bf16[256,5376]{1,0:T(8,128)(2,1)} %copy-done.1), kind=kOutput, calls=%fused_computation.76 | convolution fusion | flops 2013265920 | bytes 7929856 | tf_op jit(solution)/shard_map/tn,hpn->thp/dot_general | solution.py:76
  371.5 1.7 copy-done.5
  373.2 7.4 %fusion.9 = f32[256,80,64]{0,2,1:T(8,128)} fusion(f32[128,80,64]{0,2,1:T(8,128)S(1)} %copy-done.5, f32[128,80,64]{0,2,1:T(8,128)} %fusion.33, f32[256,80,64]{0,2,1:T(8,128)} %bitcast.82, f32[256,80,64]{0,2,1:T(8,128)} %fusion.37, f32[80]{0:T(128)S(1)} %copy-done.16, f32[256,80]{0,1:T(8,128)S(1)} %exponential_bitcast_fusion), kind=kLoop, calls=%fused_computation.19 | loop fusion | flops 6553600 | bytes 21053760 | tf_op jit(solution)/shard_map/add | solution.py:113
  380.6 6.1 %copy.72 = f32[256,5120]{1,0:T(8,128)} copy(f32[256,5120]{0,1:T(8,128)} %bitcast.83) | data formatting | bytes 10485760 | tf_op jit(solution)/shard_map/reshape | solution.py:113
  386.8 4.3 multiply_reduce_fusion
  391.1 3.2 multiply_convert_fusion.1
  394.4 94.0 %all-reduce.4.cloned.1.call-done = f32[80,64,128]{2,1,0:T(8,128)} async-done(((f32[80,64,128]{2,1,0:T(8,128)}), f32[80,64,128]{2,1,0:T(8,128)}) %all-reduce.4.cloned.1.call-update) | async-done | bytes 2621456 | tf_op jit(solution)/shard_map/psum | solution.py:39
  488.4 3.1 fusion.44
  491.6 4.1 multiply_reduce_fusion.1
  495.7 2.1 copy.77
  497.9 3.4 broadcast_select_fusion
  (104 shorter events, 14.7 us)
Async XLA Ops:
  7.2 281.1 %all-gather.4.cloned.1.call-start = ((), (), s32[]{:S(2)}) async-start(), calls=%async_computation.1 | async-start | bytes 86507520 | tf_op jit(solution)/shard_map/all_gather | solution.py:25
  8.1 8.6 %collective-permute-start = (bf16[3,5376]{1,0:T(4,128)(2,1)S(1)}, bf16[3,5376]{1,0:T(4,128)(2,1)S(1)}, u32[]{:S(2)}, u32[]{:S(2)}) collective-permute-start(bf16[3,5376]{1,0:T(4,128)(2,1)S(1)} %slice.129), channel_id=1, source_target_pairs={{0,1},{1,2},{2,3},{3,4},{4,5},{5,6},{6,7},{7,8},{8,9},{9,10},{10,1... | collective-permute-start | bytes 96776 | tf_op jit(solution)/shard_map/ppermute | solution.py:20
  16.7 2.4 copy-start.12
  22.6 8.8 %copy-start.1 = (bf16[256,5376]{1,0:T(8,128)(2,1)}, bf16[256,5376]{1,0:T(8,128)(2,1)S(1)}, u32[]{:S(2)}) copy-start(bf16[256,5376]{1,0:T(8,128)(2,1)S(1)} %multiply_convert_fusion) | copy-start | bytes 8257540
  29.4 3.4 copy-start.8
  31.4 1.5 copy-start.2
  34.9 0.9 copy-start.11
  34.9 1.8 copy-start.17
  35.0 453.4 %all-reduce.4.cloned.1.call-start = ((), (), s32[]{:S(2)}) async-start(), calls=%async_computation | async-start | bytes 5242880 | tf_op jit(solution)/shard_map/psum | solution.py:39
  166.7 1.1 copy-start.6
  167.8 3.6 copy-start.14
  171.5 4.0 copy-start.15
  189.2 4.0 copy-start.7
  193.2 3.6 copy-start.3
  371.5 1.7 copy-start.5
  371.5 1.7 copy-start.16
  380.6 6.2 %copy-start.4 = (bf16[256,5120]{1,0:T(8,128)(2,1)S(1)}, bf16[256,5120]{1,0:T(8,128)(2,1)}, u32[]{:S(2)}) copy-start(bf16[256,5120]{1,0:T(8,128)(2,1)} %param.16) | copy-start | bytes 7864324
  386.8 4.3 copy-start
  386.8 4.3 copy-start.13
  394.4 97.2 %copy-start.9 = (f32[1,128,5120]{1,2,0:T(8,128)S(1)}, f32[1,128,5120]{1,2,0:T(8,128)}, u32[]{:S(2)}) copy-start(f32[1,128,5120]{1,2,0:T(8,128)} %copy.78) | copy-start | bytes 7864324
  488.4 3.2 copy-start.10
Sparse Core Ops, SparseCore 0:
  35.1 253.1 all-gather.3
  371.6 116.7 all-reduce.3
where the time goes:
time: 511 us; the launch traced here: 508 us
  waiting for transfers between devices  182 us (36%)
  blocking collectives  124 us (24%)
  other arithmetic  113 us (22%)
  local copies, waits for them, and re-layouts  37.9 us (7%)
  matrix products  30.9 us (6%)
  between operations  15.6 us (3%)
    unnamed x1, blocking collectives  124 us
    psum x1, waiting for transfers between devices, from_root(): return lax.psum(block, axis)  94 us
    all_gather x1, waiting for transfers between devices, prefix(): pieces = jax.tree.map(lambda part: lax.all_gather(part, axis), value)  87.5 us
    select_n x31, other arithmetic, lap(): jnp.where(position < mine, new, old)  72.9 us
    dot_general x3, matrix products, carried(): jnp.einsum('tn,hpn->thp', queries, carry_state, precision=lax.Precision.H...  12.4 us
    dot_general x3, matrix products, block_local(): jnp.einsum('hts,shp->thp', mixing, values, preferred_element_type=jnp.flo...  11.8 us
    slice x5, local copies, waits for them, and re-layouts, block_local(): values = activations[:, :D_INNER].reshape(row_count, HEADS, HEAD_DIM)  10.5 us
  transfers between devices with their start and end apart: 3, of which 2 were waited for; matrix products, arithmetic and copies ran while one was open for 13% of the time, Pallas kernels for 0%

commit v1 on v0

v1 whole, which is shorter than its diff:
```python
import functools

import jax
import jax.numpy as jnp
from jax import lax
from jax.experimental import pallas as pl
from jax.experimental.pallas import tpu as pltpu
from jax.sharding import PartitionSpec as P

HEADS = 80
HEAD_DIM = 64
STATE = 128
KERNEL = 4
BLOCK = 128
D_INNER = 5120
SLABS = 8
SLAB = D_INNER // SLABS
SLAB_HEADS = HEADS // SLABS
PAIRS = SLAB // 128
EXTRA = 16
HIST = 8
HALF_TAIL = (D_INNER + 2 * STATE) // 2
PIECES = -(-HALF_TAIL // SLAB)
EPS = 1e-05
GROUP = ("seq", "resp")
SIDE = 4

F32 = jnp.float32
BF16 = jnp.bfloat16


SMEM = pl.BlockSpec(memory_space=pltpu.SMEM)
VMEM = pl.BlockSpec(memory_space=pltpu.VMEM)


def ordered(kernel, inputs, extra):
    def body(*refs):
        kernel(*refs[:inputs], *refs[inputs + extra :])

    return body


def params(mib=12):
    return pltpu.CompilerParams(vmem_limit_bytes=mib * 2**20)


def whole(kernel, where, arrays, shapes, name, after=(), scratch=(), cost=None):
    return pl.pallas_call(
        ordered(kernel, 1 + len(arrays), len(after)),
        in_specs=[SMEM] + [VMEM] * (len(arrays) + len(after)),
        out_specs=[VMEM] * len(shapes),
        out_shape=[jax.ShapeDtypeStruct(shape, dtype) for shape, dtype in shapes],
        scratch_shapes=list(scratch),
        compiler_params=params(),
        name=name,
    )(where, *arrays, *after)


def silu(value):
    return 0.5 * value * (1.0 + jnp.tanh(0.5 * value))


def spread(table, pair):
    lane = lax.broadcasted_iota(jnp.int32, table.shape, 1)
    return jnp.take_along_axis(table, 2 * pair + lane // HEAD_DIM, axis=1, mode="promise_in_bounds")


def lanes(slab, count=SLAB):
    return pl.ds(pl.multiple_of(slab * SLAB, 128), count)


def first_part(shape):
    return lax.broadcasted_iota(jnp.int32, shape, 1) % HEAD_DIM < HEAD_DIM // 2


def extra_rows(decay, tail):
    wide = jnp.broadcast_to(decay, tail.shape)
    high = wide.astype(BF16).astype(F32)
    coded = jnp.where(first_part(tail.shape), high, wide - high)
    return jnp.where(lax.broadcasted_iota(jnp.int32, tail.shape, 0) == 0, coded, tail).astype(BF16)


def decay_of(rows):
    wide = rows.astype(F32)
    half = HEAD_DIM // 2
    other = jnp.where(first_part(wide.shape), pltpu.roll(wide, SLAB - half, 1), pltpu.roll(wide, half, 1))
    return (wide + other)[0:1]


def tail_rows(rows_ref, half):
    block = jnp.zeros((EXTRA, SLAB), F32)
    place = lax.broadcasted_iota(jnp.int32, block.shape, 0)
    for piece in range(PIECES):
        width = min(SLAB, HALF_TAIL - piece * SLAB)
        start = pl.multiple_of(half * HALF_TAIL + piece * SLAB, 128)
        wide = rows_ref[:, pl.ds(start, width)].astype(F32)
        if width < SLAB:
            wide = jnp.concatenate([wide, jnp.zeros((HIST, SLAB - width), F32)], axis=1)
        for row in range(KERNEL - 1):
            line = wide[HIST - (KERNEL - 1) + row : HIST - (KERNEL - 1) + row + 1]
            block = jnp.where(place == 1 + PIECES * row + piece, line, block)
    return block


def block_table(keep, step):
    lane = lax.broadcasted_iota(jnp.int32, (HEADS, BLOCK), 1)
    cum = keep
    for by in (1, 2, 4, 8, 16, 32, 64):
        cum = cum + jnp.where(lane >= by, pltpu.roll(cum, by, 1), 0.0)
    gap = cum - 0.5 * cum[:, BLOCK - 1 : BLOCK]
    col = jnp.exp(-gap) * step
    blank = jnp.zeros((128 - HEADS, BLOCK), F32)
    return col, jnp.concatenate([jnp.exp(gap), blank], axis=0).T, jnp.concatenate([col, blank], axis=0).T


def tables_kernel(where_ref, keep_ref, step_ref, skip_ref, col_ref, rowt_ref, colt_ref, hcol_ref):
    place = lax.broadcasted_iota(jnp.int32, (8, 128), 0)
    stack = jnp.zeros((8, 128), F32)
    for block in range(2):
        here = slice(block * BLOCK, (block + 1) * BLOCK)
        col_ref[block], rowt, colt_ref[block] = block_table(keep_ref[:, here], step_ref[:, here])
        rowt_ref[block] = rowt
        stack = jnp.where(place == block, rowt[BLOCK - 1 : BLOCK], stack)
    stack = jnp.where(place == 3, jnp.concatenate([skip_ref[...], jnp.zeros((1, 128 - HEADS), F32)], axis=1), stack)
    for pair in range(HEADS // 2):
        at = (pair % PAIRS) * 128
        hcol_ref[pair // PAIRS, :, at : at + 128] = spread(stack, pair)


def conv_columns(rows, hist, weight, bias):
    wide = jnp.concatenate([hist, rows.astype(F32)], axis=0)
    total = bias + weight[KERNEL - 1 : KERNEL] * wide
    for back in range(1, KERNEL):
        total = total + weight[KERNEL - 1 - back : KERNEL - back] * pltpu.roll(wide, back, 0)
    return silu(total[HIST:]).astype(BF16)


def states_kernel(
    where_ref, x_ref, hist_ref, w_ref, b_ref, rows_ref, colt_ref, hcol_ref,
    acts_ref, kq_ref, high_ref, msg_ref, own_ref, weighted_ref, keyt_ref,
):
    core = where_ref[2]
    keep_history = where_ref[3].astype(F32)

    def conv(cols):
        hist = hist_ref[:, cols].astype(F32) * keep_history
        return conv_columns(x_ref[:, cols], hist, w_ref[:, cols], b_ref[:, cols])

    key = conv(slice(D_INNER, D_INNER + STATE))
    kq_ref[:, 0:STATE] = key
    kq_ref[:, STATE : 2 * STATE] = conv(slice(D_INNER + STATE, D_INNER + 2 * STATE))
    keyt_ref[...] = key.astype(F32).T.astype(BF16)

    def slab_states(slab, put):
        shift = lax.rem(128 - SLAB_HEADS * slab, 128)
        colts = [pltpu.roll(colt_ref[block], shift, 1) for block in range(2)]
        for pair in range(PAIRS):
            cols = slice(pair * 128, pair * 128 + 128)
            acts = conv(pl.ds(pl.multiple_of(slab * SLAB + pair * 128, 128), 128))
            acts_ref[slab, :, cols] = acts
            for block in range(2):
                here = slice(block * BLOCK, (block + 1) * BLOCK)
                weight = spread(colts[block], pair) * hcol_ref[slab, block : block + 1, cols]
                weighted_ref[here, cols] = (acts[here].astype(F32) * weight).astype(BF16)
        first = jnp.dot(keyt_ref[:, 0:BLOCK], weighted_ref[0:BLOCK], preferred_element_type=F32)
        second = jnp.dot(keyt_ref[:, BLOCK:], weighted_ref[BLOCK:], preferred_element_type=F32)
        high_ref[slab] = first.astype(BF16)
        put(hcol_ref[slab, 1:2] ** 2 * first + second)

    def sent(at, carry):
        slab = (1 - core) * 4 + at

        def put(state):
            msg_ref[at, 0:STATE] = state.astype(BF16)

        slab_states(slab, put)
        decay = (hcol_ref[slab, 0:1] * hcol_ref[slab, 1:2]) ** 2
        msg_ref[at, STATE:] = extra_rows(decay, jnp.zeros((EXTRA, SLAB), F32))
        return carry

    def kept(at, carry):
        def put(state):
            own_ref[at] = state

        slab_states(core * 4 + at, put)
        return carry

    lax.fori_loop(0, 4, sent, 0)
    slab = (1 - core) * 4
    decay = (hcol_ref[slab, 0:1] * hcol_ref[slab, 1:2]) ** 2
    msg_ref[0, STATE:] = extra_rows(decay, tail_rows(rows_ref, 1 - core))
    lax.fori_loop(0, 4, kept, 0)


def masked_scores(key_query):
    scores = lax.dot_general(
        key_query[:, STATE:], key_query[:, :STATE], (((1,), (1,)), ((), ())), preferred_element_type=F32
    )
    row = lax.broadcasted_iota(jnp.int32, (BLOCK, BLOCK), 0)
    col = lax.broadcasted_iota(jnp.int32, (BLOCK, BLOCK), 1)
    return jnp.where(row >= col, scores, 0.0)


def within_pair(scores, col_rows, values):
    mixes = [(scores * row).astype(BF16) for row in col_rows]
    first = lax.broadcasted_iota(jnp.int32, (BLOCK, 128), 1) < HEAD_DIM
    wide = values.astype(F32)
    stacked = jnp.concatenate(
        [jnp.where(first, wide, 0.0).astype(BF16), jnp.where(first, 0.0, wide).astype(BF16)], axis=0
    )
    return jnp.dot(jnp.concatenate(mixes, axis=1), stacked, preferred_element_type=F32)


def prompt_within_kernel(
    where_ref, acts_ref, z_ref, kq_ref, high_ref, col_ref, rowt_ref, hcol_ref, part_ref, gate_ref, scores_ref
):
    for block in range(2):
        scores_ref[block] = masked_scores(kq_ref[block * BLOCK : (block + 1) * BLOCK, :])

    def step(slab, carry):
        shift = lax.rem(128 - SLAB_HEADS * slab, 128)
        rowts = [pltpu.roll(rowt_ref[block], shift, 1) for block in range(2)]
        earlier = jnp.dot(kq_ref[BLOCK : 2 * BLOCK, STATE:], high_ref[slab], preferred_element_type=F32)
        for pair in range(PAIRS):
            cols = slice(pair * 128, pair * 128 + 128)
            gate_cols = pl.ds(pl.multiple_of(slab * SLAB + pair * 128, 128), 128)
            first_half = hcol_ref[slab, 0:1, cols]
            second_half = hcol_ref[slab, 1:2, cols]
            skip = hcol_ref[slab, 3:4, cols]
            head = slab * SLAB_HEADS + 2 * pair
            for block in range(2):
                here = slice(block * BLOCK, (block + 1) * BLOCK)
                values = acts_ref[slab, here, cols]
                col_rows = [col_ref[block, pl.ds(head + which, 1), :] for which in range(2)]
                mixed = within_pair(scores_ref[block], col_rows, values)
                scale = first_half
                if block == 1:
                    mixed += second_half * earlier[:, cols]
                    scale = second_half * first_half * first_half
                gate = silu(z_ref[here, gate_cols].astype(F32))
                row = spread(rowts[block], pair)
                part_ref[slab, here, cols] = (row * mixed + skip * values.astype(F32)) * gate
                gate_ref[slab, here, cols] = row * scale * gate
        return carry

    lax.fori_loop(0, SLABS, step, 0)


def resp_within_kernel(
    where_ref, x_ref, mine_ref, other_ref, w_ref, b_ref, z_ref, keep_ref, step_ref, hcol_ref,
    part_ref, gate_ref, kq_ref, hist_ref, scores_ref, col_ref, rowt_ref,
):
    core = where_ref[2]
    for half in range(2):
        flag = (core == half).astype(F32)
        tail = mine_ref[...].astype(F32) * flag + other_ref[...].astype(F32) * (1.0 - flag)
        for piece in range(PIECES):
            width = min(SLAB, HALF_TAIL - piece * SLAB)
            start = half * HALF_TAIL + piece * SLAB
            block = jnp.zeros((HIST, SLAB), F32)
            place = lax.broadcasted_iota(jnp.int32, block.shape, 0)
            for row in range(KERNEL - 1):
                at = 1 + PIECES * row + piece
                block = jnp.where(place == HIST - (KERNEL - 1) + row, tail[at : at + 1], block)
            hist_ref[:, start : start + width] = block[:, 0:width]
    col_ref[...], rowt_ref[...], _ = block_table(keep_ref[...], step_ref[...])

    def conv(cols):
        return conv_columns(x_ref[:, cols], hist_ref[:, cols], w_ref[:, cols], b_ref[:, cols])

    for at in (0, STATE):
        kq_ref[:, at : at + STATE] = conv(slice(D_INNER + at, D_INNER + at + STATE))
    scores_ref[...] = masked_scores(kq_ref[...])

    def step(slab, carry):
        rowt = pltpu.roll(rowt_ref[...], lax.rem(128 - SLAB_HEADS * slab, 128), 1)
        for pair in range(PAIRS):
            cols = slice(pair * 128, pair * 128 + 128)
            wide_cols = pl.ds(pl.multiple_of(slab * SLAB + pair * 128, 128), 128)
            values = conv(wide_cols)
            head = slab * SLAB_HEADS + 2 * pair
            col_rows = [col_ref[pl.ds(head + which, 1), :] for which in range(2)]
            mixed = within_pair(scores_ref[...], col_rows, values)
            gate = silu(z_ref[:, wide_cols].astype(F32))
            row = spread(rowt, pair)
            half = row[BLOCK - 1 : BLOCK]
            part_ref[slab, :, cols] = (row * mixed + hcol_ref[slab, 3:4, cols] * values.astype(F32)) * gate
            gate_ref[slab, :, cols] = row * half * gate
        return carry

    lax.fori_loop(0, SLABS, step, 0)


def at_shift(place, by):
    return lax.rem(place + by + SIDE, SIDE)


def pick(condition, value):
    flag = condition.astype(F32)
    return value * flag + (1.0 - flag)


def chip_kernel(where_ref, own_ref, recv_ref, hcol_ref, rows_ref, *out_refs):
    x, core = where_ref[0], where_ref[2]
    first = (core == 0).astype(F32)
    tail = tail_rows(rows_ref, core) * (1.0 - first) + recv_ref[0, STATE:, :].astype(F32) * first
    for shift in range(SIDE):
        slab = at_shift(x, shift)
        half = hcol_ref[core * 4 + slab]
        mine = (half[0:1] * half[1:2]) ** 2
        theirs = decay_of(recv_ref[slab, STATE:, :])
        own_scale = theirs * first + (1.0 - first)
        recv_scale = mine * (1.0 - first) + first
        state = own_scale * own_ref[slab] + recv_scale * recv_ref[slab, 0:STATE, :].astype(F32)
        out_refs[shift][0:STATE] = state.astype(BF16)
        out_refs[shift][STATE:] = extra_rows(mine * theirs, tail)


def row_kernel(where_ref, r0, r1, r2, r3, out_ref):
    x = where_ref[0]
    refs = (r0, r1, r2, r3)
    places = [at_shift(x, -i) for i in range(SIDE)]
    decays = [decay_of(ref[STATE:]) for ref in refs]
    total = jnp.zeros((STATE, SLAB), F32)
    through = jnp.ones((1, SLAB), F32)
    tail = jnp.zeros((EXTRA, SLAB), F32)
    for i in range(SIDE):
        scale = jnp.ones((1, SLAB), F32)
        for k in range(SIDE):
            if k != i:
                scale = scale * pick(places[k] > places[i], decays[k])
        total = total + scale * refs[i][0:STATE].astype(F32)
        through = through * decays[i]
        tail = tail + refs[i][STATE:].astype(F32) * (places[i] == SIDE - 1).astype(F32)
    out_ref[0:STATE] = total.astype(BF16)
    out_ref[STATE:] = extra_rows(through, tail)


def entering_kernel(where_ref, r0, r1, r2, r3, t0, t1, t2, t3, e0, e1, e2, e3, tail_ref):
    x, y = where_ref[0], where_ref[1]
    refs, totals, outs = (r0, r1, r2, r3), (t0, t1, t2, t3), (e0, e1, e2, e3)
    rows = [at_shift(y, -i) for i in range(SIDE)]
    row_decays = [decay_of(ref[STATE:]) for ref in totals]
    final = jnp.zeros((STATE, SLAB), F32)
    row_in = jnp.zeros((STATE, SLAB), F32)
    tail = jnp.zeros((EXTRA, SLAB), F32)
    for i in range(SIDE):
        scale = jnp.ones((1, SLAB), F32)
        before = (rows[i] < y).astype(F32) * jnp.ones((1, SLAB), F32)
        for k in range(SIDE):
            if k != i:
                scale = scale * pick(rows[k] > rows[i], row_decays[k])
                before = before * pick(jnp.logical_and(rows[k] > rows[i], rows[k] < y), row_decays[k])
        wide = totals[i][0:STATE].astype(F32)
        final = final + scale * wide
        row_in = row_in + before * wide
        tail = tail + totals[i][STATE:].astype(F32) * (rows[i] == SIDE - 1).astype(F32)
    tail_ref[...] = tail.astype(BF16)
    final = final.astype(BF16)
    places = [at_shift(x, -i) for i in range(SIDE)]
    decays = [decay_of(ref[STATE:]) for ref in refs]
    for shift in range(SIDE):
        target = at_shift(x, shift)
        carry = jnp.ones((1, SLAB), F32)
        for k in range(SIDE):
            carry = carry * pick(places[k] < target, decays[k])
        total = carry * row_in
        for i in range(SIDE):
            scale = (places[i] < target).astype(F32) * jnp.ones((1, SLAB), F32)
            for k in range(SIDE):
                if k != i:
                    scale = scale * pick(
                        jnp.logical_and(places[k] > places[i], places[k] < target), decays[k]
                    )
            total = total + scale * refs[i][0:STATE].astype(F32)
        outs[shift][0:STATE] = total.astype(BF16)
        outs[shift][STATE:] = final


def cores_kernel(where_ref, g0, g1, g2, g3, own_ref, recv_ref, hcol_ref, mine_ref, send_ref, final_ref):
    x, core = where_ref[0], where_ref[2]
    first = (core == 0).astype(F32)
    for i, ref in enumerate((g0, g1, g2, g3)):
        slab = at_shift(x, -i)
        half = hcol_ref[core * 4 + slab]
        mine = (half[0:1] * half[1:2]) ** 2
        theirs = decay_of(recv_ref[slab, STATE:, :])
        decay = mine * first + theirs * (1.0 - first)
        earlier = own_ref[slab] * first + recv_ref[slab, 0:STATE, :].astype(F32) * (1.0 - first)
        start = ref[0:STATE].astype(F32)
        later = decay * start + earlier
        mine_ref[slab] = (start * first + later * (1.0 - first)).astype(BF16)
        send_ref[slab] = (later * first + start * (1.0 - first)).astype(BF16)
        final_ref[slab] = ref[STATE:]


def finish_kernel(tile, length_at, where_ref, part_ref, gate_ref, kq_ref, mine_ref, other_ref, gain_ref, out_ref, gated_ref):
    core = where_ref[2]
    start = pl.program_id(0) * tile
    here = pl.ds(pl.multiple_of(start, tile), tile)
    query = kq_ref[here, STATE:]
    squares = jnp.zeros((tile, 128), F32)
    for held_ref, half in ((mine_ref, core), (other_ref, 1 - core)):
        for s in range(4):
            slab = half * 4 + s
            carried = jnp.dot(query, held_ref[s], preferred_element_type=F32)
            gated = part_ref[slab, here, :] + gate_ref[slab, here, :] * carried
            gated_ref[slab] = gated
            square = gated * gated
            for pair in range(PAIRS):
                squares = squares + square[:, pair * 128 : pair * 128 + 128]
    mean = jnp.sum(squares, axis=1, keepdims=True) * (1.0 / D_INNER)
    row = lax.broadcasted_iota(jnp.int32, (tile, 1), 0) + start
    inv = jnp.where(row < where_ref[length_at], lax.rsqrt(mean + EPS), 0.0)
    for slab in range(SLABS):
        cols = slice(slab * SLAB, (slab + 1) * SLAB)
        out_ref[:, cols] = (gated_ref[slab] * inv * gain_ref[:, cols]).astype(BF16)


def finish(where, part, gate, kq, mine, other, gain, length_at, name, tile=64):
    rows = part.shape[1]
    return pl.pallas_call(
        functools.partial(finish_kernel, tile, length_at),
        grid=(rows // tile,),
        in_specs=[SMEM] + [VMEM] * 6,
        out_specs=pl.BlockSpec((tile, D_INNER), lambda i: (i, 0)),
        scratch_shapes=[pltpu.VMEM((SLABS, tile, SLAB), F32)],
        out_shape=jax.ShapeDtypeStruct((rows, D_INNER), BF16),
        compiler_params=params(),
        name=name,
    )(where, part, gate, kq, mine, other, gain)


def number(y, x, core):
    return (y % SIDE) * 2 * SIDE + (x % SIDE) * 2 + core


def moved(value, move):
    pairs = [
        (number(y, x, core), number(*move(y, x, core)))
        for y in range(SIDE)
        for x in range(SIDE)
        for core in range(2)
    ]
    return lax.ppermute(value, GROUP, pairs)


def swap_cores(value):
    return moved(value, lambda y, x, core: (y, x, 1 - core))


def along_x(value, by):
    return moved(value, lambda y, x, core: (y, x + by, core))


def along_y(value, by):
    return moved(value, lambda y, x, core: (y + by, x, core))


def make_tables(where, keep, step, skip, after):
    shapes = [((2, HEADS, BLOCK), F32), ((2, BLOCK, 128), F32), ((2, BLOCK, 128), F32), ((SLABS, 8, SLAB), F32)]
    return whole(tables_kernel, where, (keep, step, skip[None, :]), shapes, "tables", after)


def make_states(where, xbc, hist, weight, bias, own_rows, colt, hcol):
    rows = xbc.shape[0]
    shapes = [
        ((SLABS, rows, SLAB), BF16),
        ((rows, 2 * STATE), BF16),
        ((SLABS, STATE, SLAB), BF16),
        ((4, STATE + EXTRA, SLAB), BF16),
        ((4, STATE, SLAB), F32),
    ]
    scratch = [pltpu.VMEM((rows, SLAB), BF16), pltpu.VMEM((STATE, rows), BF16)]
    return whole(states_kernel, where, (xbc, hist, weight, bias, own_rows, colt, hcol), shapes, "states", scratch=scratch)


def prompt_within(where, acts, z, kq, high, col, rowt, hcol, after):
    shapes = [((SLABS, z.shape[0], SLAB), F32)] * 2
    scratch = [pltpu.VMEM((2, BLOCK, BLOCK), F32)]
    return whole(prompt_within_kernel, where, (acts, z, kq, high, col, rowt, hcol), shapes, "prompt_within", after, scratch)


def resp_within(where, xbc, mine, other, weight, bias, z, keep, step, hcol, after):
    rows = z.shape[0]
    shapes = [((SLABS, rows, SLAB), F32)] * 2 + [((rows, 2 * STATE), BF16)]
    scratch = [
        pltpu.VMEM((HIST, D_INNER + 2 * STATE), F32),
        pltpu.VMEM((BLOCK, BLOCK), F32),
        pltpu.VMEM((HEADS, BLOCK), F32),
        pltpu.VMEM((BLOCK, 128), F32),
    ]
    arrays = (xbc, mine, other, weight, bias, z, keep, step, hcol)
    return whole(resp_within_kernel, where, arrays, shapes, "resp_within", after, scratch)


def shards(
    prompt_xbc,
    prompt_z,
    prompt_step,
    prompt_keep,
    resp_xbc,
    resp_z,
    resp_step,
    resp_keep,
    resp_len,
    conv_weight,
    conv_bias,
    skip,
    gain,
):
    rows = prompt_xbc.shape[0]
    seq, core = lax.axis_index("seq"), lax.axis_index("resp")
    fixed = [seq % SIDE, seq // SIDE, core, jnp.where(lax.axis_index(GROUP) == 0, 0, 1)]
    where = jnp.stack([jnp.asarray(v, jnp.int32) for v in fixed + [rows, resp_len[0]]])
    bias_row, gain_row = conv_bias[None, :], gain[None, :]

    own_rows = prompt_xbc[rows - HIST :]
    count = 2 * SIDE * SIDE
    hist = lax.ppermute(own_rows, GROUP, [(i, i + 1) for i in range(count - 1)])
    col, rowt, colt, hcol = make_tables(
        where, prompt_keep, prompt_step, skip, after=(prompt_xbc, conv_weight, bias_row)
    )
    acts, kq, high, msg, own = make_states(where, prompt_xbc, hist, conv_weight, bias_row, own_rows, colt, hcol)
    recv = swap_cores(msg)
    with_extra, both = ((STATE + EXTRA, SLAB), BF16), ((2 * STATE, SLAB), BF16)
    c0, c1, c2, c3 = whole(chip_kernel, where, (own, recv, hcol, own_rows), [with_extra] * 4, "chip")
    pieces = (c0, along_x(c1, 1), along_x(c2, 2), along_x(c3, 3))
    part, gate = prompt_within(where, acts, prompt_z, kq, high, col, rowt, hcol, after=(c1, c2, c3))
    (total,) = whole(row_kernel, where, pieces, [with_extra], "row", after=(part, gate))
    totals = (total, along_y(total, 1), along_y(total, 2), along_y(total, 3))
    e0, e1, e2, e3, tail = whole(
        entering_kernel, where, pieces + totals, [both] * 4 + [((EXTRA, SLAB), BF16)], "entering", after=(part, gate)
    )
    tail_other = swap_cores(tail)
    back = (e0, along_x(e1, 1), along_x(e2, 2), along_x(e3, 3))
    resp_part, resp_gate, resp_kq = resp_within(
        where, resp_xbc[0], tail, tail_other, conv_weight, bias_row, resp_z[0],
        resp_keep.reshape(HEADS, BLOCK), resp_step.reshape(HEADS, BLOCK), hcol, after=(e1, e2, e3),
    )
    four = ((4, STATE, SLAB), BF16)
    mine, send, final = whole(
        cores_kernel, where, back + (own, recv, hcol), [four] * 3, "cores",
        after=(resp_part, resp_gate, part, gate),
    )
    other, final_other = swap_cores(send), swap_cores(final)
    prompt_out = finish(where, part, gate, kq, mine, other, gain_row, 4, "prompt_finish")
    resp_out = finish(where, resp_part, resp_gate, resp_kq, final, final_other, gain_row, 5, "resp_finish")
    return (prompt_out, resp_out[None])


def solution(mesh):
    return jax.shard_map(
        shards,
        mesh=mesh,
        in_specs=(
            P(("grp", "seq", "resp"), None),
            P(("grp", "seq", "resp"), None),
            P(None, ("grp", "seq", "resp")),
            P(None, ("grp", "seq", "resp")),
            P(("grp", "seq", "resp"), None, None),
            P(("grp", "seq", "resp"), None, None),
            P(None, ("grp", "seq", "resp"), None),
            P(None, ("grp", "seq", "resp"), None),
            P(("grp", "seq", "resp")),
            P(),
            P(),
            P(),
            P(),
        ),
        out_specs=(P(("grp", "seq", "resp"), None), P(("grp", "seq", "resp"), None, None)),
        check_vma=False,
    )
```

time: 511 us -> 85.4 us (0.17)
  waiting for transfers between devices: 182 us -> 24.4 us
  blocking collectives: 124 us -> 0 us
  other arithmetic: 113 us -> 0 us
  Pallas kernels: 0 us -> 31.3 us
  matrix products: 30.9 us -> 0 us
  local copies, waits for them, and re-layouts: 37.9 us -> 7.26 us
  starting transfers between devices: 4.59 us -> 20.7 us
  between operations: 15.6 us -> 1.47 us
    unnamed x1 -> x0, blocking collectives: 124 us -> none
    psum x1 -> x0, waiting for transfers between devices: 94 us -> none  [from_root(): return lax.psum(block, axis)]
    all_gather x1 -> x0, waiting for transfers between devices: 87.5 us -> none  [prefix(): pieces = jax.tree.map(lambda part: lax.all_gather(part, axis), value)]
    select_n x34 -> x0, other arithmetic: 80.8 us -> none  [the longest x31 72.9 us: lap(): jnp.where(position < mine, new, old)]
    pallas_call x0 -> x10, Pallas kernels: none -> 31.3 us  [the longest x8 24.8 us: whole(): pl.pallas_call(ordered(kernel, 1 + len(arrays), len(after)), in_specs=[SM...]
    dot_general x11 -> x0, matrix products: 30.9 us -> none  [the longest x3 12.4 us: carried(): jnp.einsum('tn,hpn->thp', queries, carry_state, precision=lax.Precision.H...]
    ppermute x1 -> x14, waiting for transfers between devices: 0.01 us -> 24.4 us  [the longest x13 24.4 us: moved(): return lax.ppermute(value, GROUP, pairs)]
    ppermute x1 -> x14, starting transfers between devices: 4.51 us -> 20.7 us  [the longest x13 16.2 us: moved(): return lax.ppermute(value, GROUP, pairs)]
  transfers between devices with their start and end apart: 3 -> 14, of which waited for: 2 -> 8; matrix products, arithmetic and copies ran while one was open for 13% -> 1% of each run, Pallas kernels for 0% -> 18%
where the time goes in v1:
time: 85.4 us; the launch traced here: 85 us
  Pallas kernels  31.3 us (37%)
  waiting for transfers between devices  24.4 us (29%)
  starting transfers between devices  20.7 us (24%)
  local copies, waits for them, and re-layouts  7.26 us (9%)
  between operations  1.47 us (2%)
    pallas_call x8, Pallas kernels, whole(): pl.pallas_call(ordered(kernel, 1 + len(arrays), len(after)), in_specs=[SM...  24.8 us
    ppermute x13, waiting for transfers between devices, moved(): return lax.ppermute(value, GROUP, pairs)  24.4 us
    ppermute x13, starting transfers between devices, moved(): return lax.ppermute(value, GROUP, pairs)  16.2 us
    pallas_call x2, Pallas kernels, finish(): pl.pallas_call(functools.partial(finish_kernel, tile, length_at), grid=(r...  6.5 us
    unnamed x26, local copies, waits for them, and re-layouts  5.49 us
    ppermute x1, starting transfers between devices, shards(): hist = lax.ppermute(own_rows, GROUP, [(i, i + 1) for i in range(count - 1)])  4.5 us
  transfers between devices with their start and end apart: 14, of which 8 were waited for; matrix products, arithmetic and copies ran while one was open for 1% of the time, Pallas kernels for 18%

profile of v1, /device:TPU:1, one launch (start us, length us, event | category | flops | bytes accessed | tf_op | source)
XLA Modules:
  0.0 85.0 jit_solution(14031681636738395205)
XLA Ops:
  0.6 0.0 copy-start.6
  0.6 0.9 %slice.3.refs_5_.refs_4_ = bf16[8,5376]{1,0:T(8,128)(2,1)S(1)} slice(bf16[256,5376]{1,0:T(8,128)(2,1)} %refs_1_.3), slice={[248:256], [0:5376]} | slice | bytes 172032 | tf_op jit(solution)/shard_map/slice | solution.py:518
  1.6 4.5 %collective-permute-start = (bf16[8,5376]{1,0:T(8,128)(2,1)S(1)}, bf16[8,5376]{1,0:T(8,128)(2,1)S(1)}, u32[]{:S(2)}, u32[]{:S(2)}) collective-permute-start(bf16[8,5376]{1,0:T(8,128)(2,1)S(1)} %slice.3.refs_5_.refs_4_), channel_id=1, source_target_pairs={{0,1},{1,2},{2,3},{3,4},{4,5},{5,6},{6,7},{7,8},{8,9},{9,10},{10,1... | collective-permute-start | bytes 258056 | tf_op jit(solution)/shard_map/ppermute | solution.py:520
  6.8 0.8 broadcast_in_dim.12.refs_6_.refs_4_.refs_5_
  7.5 0.1 stack.19.refs_0_.where_ref
  7.6 0.0 copy-start
  7.6 1.8 %copy-done = bf16[256,5376]{1,0:T(8,128)(2,1)S(1)} copy-done((bf16[256,5376]{1,0:T(8,128)(2,1)S(1)}, bf16[256,5376]{1,0:T(8,128)(2,1)}, u32[]{:S(2)}) %copy-start) | copy-done | bytes 2752536
  9.4 0.0 copy-start.5
  9.4 0.9 %copy-done.5 = f32[4,5376]{1,0:T(4,128)S(1)} copy-done((f32[4,5376]{1,0:T(4,128)S(1)}, f32[4,5376]{1,0:T(4,128)}, u32[]{:S(2)}) %copy-start.5) | copy-done | bytes 86040
  10.3 0.9 %copy-done.8 = f32[80,256]{1,0:T(8,128)S(1)} copy-done((f32[80,256]{1,0:T(8,128)S(1)}, f32[80,256]{1,0:T(8,128)}, u32[]{:S(2)}) %copy-start.8) | copy-done | bytes 81944
  11.2 0.0 copy-start.9
  11.2 0.9 %copy-done.9 = f32[80,256]{1,0:T(8,128)S(1)} copy-done((f32[80,256]{1,0:T(8,128)S(1)}, f32[80,256]{1,0:T(8,128)}, u32[]{:S(2)}) %copy-start.9) | copy-done | bytes 81944
  12.1 0.0 copy-start.12
  12.1 0.7 copy-done.12
  12.7 0.0 copy-start.1
  12.7 1.4 %tables.1 = (f32[2,80,128]{2,1,0:T(8,128)S(1)}, f32[2,128,128]{2,1,0:T(8,128)S(1)}, f32[2,128,128]{2,1,0:T(8,128)S(1)}, f32[8,8,640]{2,1,0:T(8,128)S(1)}) custom-call(s32[6]{0:T(128)S(1)} %stack.19.refs_0_.where_ref, f32[80,256]{1,0:T(8,128)S(1)} %copy-done.8, f32[80,256]{1,0:T(8,128)S(1)} %copy-done.9, f32[1,80]{1,0:T(1,128)S(1)} %bitcast.17, ...), custom_call_target="tpu_custom_call" | custom-call | tf_op jit(solution)/shard_map/tables/pallas_call | solution.py:48
  14.1 0.0 collective-permute-done.refs_2_
  14.1 0.0 copy-done.6
  14.1 0.4 copy-done.1
  14.5 7.5 %states.1 = (bf16[8,256,640]{2,1,0:T(8,128)(2,1)S(1)}, bf16[256,256]{1,0:T(8,128)(2,1)S(1)}, bf16[8,128,640]{2,1,0:T(8,128)(2,1)S(1)}, bf16[4,144,640]{2,1,0:T(8,128)(2,1)S(1)}, f32[4,128,640]{2,1,0:T(8,128)S(1)}) custom-call(s32[6]{0:T(128)S(1)} %stack.19.refs_0_.where_ref, bf16[256,5376]{1,0:T(8,128)(2,1)S(1)} %copy-done.1, ...), custom_call_target="tpu_custom_call" | custom-call | tf_op jit(solution)/shard_map/states/pallas_call | solution.py:48
  22.0 0.1 collective-permute-start.1
  22.1 2.2 %collective-permute-done.1.refs_2_.refs_6_ = bf16[4,144,640]{2,1,0:T(8,128)(2,1)S(1)} collective-permute-done((bf16[4,144,640]{2,1,0:T(8,128)(2,1)S(1)}, bf16[4,144,640]{2,1,0:T(8,128)(2,1)S(1)}, u32[]{:S(2)}, u32[]{:S(2)}) %collective-permute-start.1) | collective-permute-done | bytes 737312 | tf_op jit(solution)/shard_map/ppermute | solution.py:445
  24.3 0.9 %chip.1 = (bf16[144,640]{1,0:T(8,128)(2,1)S(1)}, bf16[144,640]{1,0:T(8,128)(2,1)S(1)}, bf16[144,640]{1,0:T(8,128)(2,1)S(1)}, bf16[144,640]{1,0:T(8,128)(2,1)S(1)}) custom-call(s32[6]{0:T(128)S(1)} %stack.19.refs_0_.where_ref, f32[4,128,640]{2,1,0:T(8,128)S(1)} %get-tuple-element.35.refs_1_.refs_5_, ...), custom_call_target="tpu_custom_call" | custom-call | tf_op jit(solution)/shard_map/chip/pallas_call | solution.py:48
  25.2 1.3 %collective-permute-start.2 = (bf16[144,640]{1,0:T(8,128)(2,1)S(1)}, bf16[144,640]{1,0:T(8,128)(2,1)S(1)}, u32[]{:S(2)}, u32[]{:S(2)}) collective-permute-start(bf16[144,640]{1,0:T(8,128)(2,1)S(1)} %get-tuple-element.37.refs_8_), channel_id=1, source_target_pairs={{0,2},{1,3},{2,4},{3,5},{4,6},{5,7},{6,0},{7,1},{8,10},{9,11},{10,... | collective-permute-start | bytes 552968 | tf_op jit(solution)/shard_map/ppermute | solution.py:445
  26.5 2.5 %collective-permute-start.3 = (bf16[144,640]{1,0:T(8,128)(2,1)S(1)}, bf16[144,640]{1,0:T(8,128)(2,1)S(1)}, u32[]{:S(2)}, u32[]{:S(2)}) collective-permute-start(bf16[144,640]{1,0:T(8,128)(2,1)S(1)} %get-tuple-element.38.refs_9_), channel_id=1, source_target_pairs={{0,4},{1,5},{2,6},{3,7},{4,0},{5,1},{6,2},{7,3},{8,12},{9,13},{10,... | collective-permute-start | bytes 552968 | tf_op jit(solution)/shard_map/ppermute | solution.py:445
  29.0 0.9 %collective-permute-start.4 = (bf16[144,640]{1,0:T(8,128)(2,1)S(1)}, bf16[144,640]{1,0:T(8,128)(2,1)S(1)}, u32[]{:S(2)}, u32[]{:S(2)}) collective-permute-start(bf16[144,640]{1,0:T(8,128)(2,1)S(1)} %get-tuple-element.39.refs_10_), channel_id=1, source_target_pairs={{0,6},{1,7},{2,0},{3,1},{4,2},{5,3},{6,4},{7,5},{8,14},{9,15},{10,... | collective-permute-start | bytes 552968 | tf_op jit(solution)/shard_map/ppermute | solution.py:445
  29.8 0.0 copy-done.2
  29.8 5.2 %prompt_within.1 = (f32[8,256,640]{2,1,0:T(8,128)S(1)}, f32[8,256,640]{2,1,0:T(8,128)S(1)}) custom-call(s32[6]{0:T(128)S(1)} %stack.19.refs_0_.where_ref, bf16[8,256,640]{2,1,0:T(8,128)(2,1)S(1)} %get-tuple-element.30.refs_1_, bf16[256,5120]{1,0:T(8,128)(2,1)S(1)} %copy-done.2, bf16[256,256]{1,0:T(8,128)(2,1)S(1)} %get-tuple-element.31.refs_3_.kq_ref, ...), custom_call_target="tpu_custom_call" | custom-call | tf_op jit(solution)/shard_map/prompt_within/pallas_call | solution.py:48
  35.1 0.0 collective-permute-done.2.refs_2_
  35.1 2.5 %collective-permute-done.3.refs_3_ = bf16[144,640]{1,0:T(8,128)(2,1)S(1)} collective-permute-done((bf16[144,640]{1,0:T(8,128)(2,1)S(1)}, bf16[144,640]{1,0:T(8,128)(2,1)S(1)}, u32[]{:S(2)}, u32[]{:S(2)}) %collective-permute-start.3) | collective-permute-done | bytes 184352 | tf_op jit(solution)/shard_map/ppermute | solution.py:445
  37.6 0.0 collective-permute-done.4.refs_4_
  37.6 0.8 row.1.refs_5_
  38.4 0.0 copy-start.3
  38.4 0.0 copy-start.4
  38.4 0.0 copy-start.10
  38.4 0.0 copy-start.11
  38.4 2.1 %collective-permute-start.7 = (bf16[144,640]{1,0:T(8,128)(2,1)S(1)}, bf16[144,640]{1,0:T(8,128)(2,1)S(1)}, u32[]{:S(2)}, u32[]{:S(2)}) collective-permute-start(bf16[144,640]{1,0:T(8,128)(2,1)S(1)} %row.1.refs_5_), channel_id=1, source_target_pairs={{0,24},{1,25},{2,26},{3,27},{4,28},{5,29},{6,30},{7,31},{8,0},{9,1... | collective-permute-start | bytes 552968 | tf_op jit(solution)/shard_map/ppermute | solution.py:445
  40.5 1.1 %collective-permute-start.6 = (bf16[144,640]{1,0:T(8,128)(2,1)S(1)}, bf16[144,640]{1,0:T(8,128)(2,1)S(1)}, u32[]{:S(2)}, u32[]{:S(2)}) collective-permute-start(bf16[144,640]{1,0:T(8,128)(2,1)S(1)} %row.1.refs_5_), channel_id=1, source_target_pairs={{0,16},{1,17},{2,18},{3,19},{4,20},{5,21},{6,22},{7,23},{8,24},{9,... | collective-permute-start | bytes 552968 | tf_op jit(solution)/shard_map/ppermute | solution.py:445
  41.6 0.4 collective-permute-start.5
  42.0 1.7 %collective-permute-done.7.refs_8_ = bf16[144,640]{1,0:T(8,128)(2,1)S(1)} collective-permute-done((bf16[144,640]{1,0:T(8,128)(2,1)S(1)}, bf16[144,640]{1,0:T(8,128)(2,1)S(1)}, u32[]{:S(2)}, u32[]{:S(2)}) %collective-permute-start.7) | collective-permute-done | bytes 184352 | tf_op jit(solution)/shard_map/ppermute | solution.py:445
  43.7 2.8 %collective-permute-done.6.refs_7_ = bf16[144,640]{1,0:T(8,128)(2,1)S(1)} collective-permute-done((bf16[144,640]{1,0:T(8,128)(2,1)S(1)}, bf16[144,640]{1,0:T(8,128)(2,1)S(1)}, u32[]{:S(2)}, u32[]{:S(2)}) %collective-permute-start.6) | collective-permute-done | bytes 184352 | tf_op jit(solution)/shard_map/ppermute | solution.py:445
  46.5 5.6 %collective-permute-done.5.refs_6_ = bf16[144,640]{1,0:T(8,128)(2,1)S(1)} collective-permute-done((bf16[144,640]{1,0:T(8,128)(2,1)S(1)}, bf16[144,640]{1,0:T(8,128)(2,1)S(1)}, u32[]{:S(2)}, u32[]{:S(2)}) %collective-permute-start.5) | collective-permute-done | bytes 184352 | tf_op jit(solution)/shard_map/ppermute | solution.py:445
  52.1 2.4 %entering.1 = (bf16[256,640]{1,0:T(8,128)(2,1)S(1)}, bf16[256,640]{1,0:T(8,128)(2,1)S(1)}, bf16[256,640]{1,0:T(8,128)(2,1)S(1)}, bf16[256,640]{1,0:T(8,128)(2,1)S(1)}, bf16[16,640]{1,0:T(8,128)(2,1)S(1)}) custom-call(s32[6]{0:T(128)S(1)} %stack.19.refs_0_.where_ref, bf16[144,640]{1,0:T(8,128)(2,1)S(1)} %get-tuple-element.42.refs_1_, ...), custom_call_target="tpu_custom_call" | custom-call | tf_op jit(solution)/shard_map/entering/pallas_call | solution.py:48
  54.5 2.3 %collective-permute-start.8 = (bf16[256,640]{1,0:T(8,128)(2,1)S(1)}, bf16[256,640]{1,0:T(8,128)(2,1)S(1)}, u32[]{:S(2)}, u32[]{:S(2)}) collective-permute-start(bf16[256,640]{1,0:T(8,128)(2,1)S(1)} %get-tuple-element.44.refs_10_), channel_id=1, source_target_pairs={{0,2},{1,3},{2,4},{3,5},{4,6},{5,7},{6,0},{7,1},{8,10},{9,11},{10,... | collective-permute-start | bytes 983048 | tf_op jit(solution)/shard_map/ppermute | solution.py:445
  56.8 2.5 %collective-permute-start.9 = (bf16[256,640]{1,0:T(8,128)(2,1)S(1)}, bf16[256,640]{1,0:T(8,128)(2,1)S(1)}, u32[]{:S(2)}, u32[]{:S(2)}) collective-permute-start(bf16[256,640]{1,0:T(8,128)(2,1)S(1)} %get-tuple-element.45.refs_11_), channel_id=1, source_target_pairs={{0,4},{1,5},{2,6},{3,7},{4,0},{5,1},{6,2},{7,3},{8,12},{9,13},{10,... | collective-permute-start | bytes 983048 | tf_op jit(solution)/shard_map/ppermute | solution.py:445
  59.4 0.1 collective-permute-start.10
  59.4 1.5 %collective-permute-start.11 = (bf16[16,640]{1,0:T(8,128)(2,1)S(1)}, bf16[16,640]{1,0:T(8,128)(2,1)S(1)}, u32[]{:S(2)}, u32[]{:S(2)}) collective-permute-start(bf16[16,640]{1,0:T(8,128)(2,1)S(1)} %get-tuple-element.47.refs_2_), channel_id=1, source_target_pairs={{0,1},{1,0},{2,3},{3,2},{4,5},{5,4},{6,7},{7,6},{8,9},{9,8},{10,11... | collective-permute-start | bytes 61448 | tf_op jit(solution)/shard_map/ppermute | solution.py:445
  60.9 0.8 collective-permute-done.11.refs_3_
  61.8 0.0 copy-done.3
  61.8 0.0 copy-done.4
  61.8 0.0 copy-done.10
  61.8 0.0 copy-done.11
  61.8 4.9 %resp_within.1 = (f32[8,128,640]{2,1,0:T(8,128)S(1)}, f32[8,128,640]{2,1,0:T(8,128)S(1)}, bf16[128,256]{1,0:T(8,128)(2,1)S(1)}) custom-call(s32[6]{0:T(128)S(1)} %stack.19.refs_0_.where_ref, bf16[128,5376]{1,0:T(8,128)(2,1)S(1)} %bitcast.11, bf16[16,640]{1,0:T(8,128)(2,1)S(1)} %get-tuple-element.47.refs_2_, ...), custom_call_target="tpu_custom_call" | custom-call | tf_op jit(solution)/shard_map/resp_within/pallas_call | solution.py:48
  66.6 0.0 collective-permute-done.8.refs_2_
  66.6 7.1 %collective-permute-done.9.refs_3_ = bf16[256,640]{1,0:T(8,128)(2,1)S(1)} collective-permute-done((bf16[256,640]{1,0:T(8,128)(2,1)S(1)}, bf16[256,640]{1,0:T(8,128)(2,1)S(1)}, u32[]{:S(2)}, u32[]{:S(2)}) %collective-permute-start.9) | collective-permute-done | bytes 327712 | tf_op jit(solution)/shard_map/ppermute | solution.py:445
  73.7 0.0 collective-permute-done.10.refs_4_
  73.7 1.7 %cores.1 = (bf16[4,128,640]{2,1,0:T(8,128)(2,1)S(1)}, bf16[4,128,640]{2,1,0:T(8,128)(2,1)S(1)}, bf16[4,128,640]{2,1,0:T(8,128)(2,1)S(1)}) custom-call(s32[6]{0:T(128)S(1)} %stack.19.refs_0_.where_ref, bf16[256,640]{1,0:T(8,128)(2,1)S(1)} %get-tuple-element.43.refs_1_, bf16[256,640]{1,0:T(8,128)(2,1)S(1)} %collective-permute-done.8.refs_2_, ...), custom_call_target="tpu_custom_call" | custom-call | tf_op jit(solution)/shard_map/cores/pallas_call | solution.py:48
  75.4 1.4 %collective-permute-start.12 = (bf16[4,128,640]{2,1,0:T(8,128)(2,1)S(1)}, bf16[4,128,640]{2,1,0:T(8,128)(2,1)S(1)}, u32[]{:S(2)}, u32[]{:S(2)}) collective-permute-start(bf16[4,128,640]{2,1,0:T(8,128)(2,1)S(1)} %get-tuple-element.51), channel_id=1, source_target_pairs={{0,1},{1,0},{2,3},{3,2},{4,5},{5,4},{6,7},{7,6},{8,9},{9,8},{10,11... | collective-permute-start | bytes 1966088 | tf_op jit(solution)/shard_map/ppermute | solution.py:445
  76.8 0.1 collective-permute-start.13
  76.9 1.6 %collective-permute-done.12.other_ref = bf16[4,128,640]{2,1,0:T(8,128)(2,1)S(1)} collective-permute-done((bf16[4,128,640]{2,1,0:T(8,128)(2,1)S(1)}, bf16[4,128,640]{2,1,0:T(8,128)(2,1)S(1)}, u32[]{:S(2)}, u32[]{:S(2)}) %collective-permute-start.12) | collective-permute-done | bytes 655392 | tf_op jit(solution)/shard_map/ppermute | solution.py:445
  78.5 0.0 copy-done.7
  78.5 4.0 %prompt_finish.1 = bf16[256,5120]{1,0:T(8,128)(2,1)} custom-call(s32[6]{0:T(128)S(1)} %stack.19.refs_0_.where_ref, f32[8,256,640]{2,1,0:T(8,128)S(1)} %get-tuple-element.40.refs_5_.refs_9_.refs_10_.part_ref, f32[8,256,640]{2,1,0:T(8,128)S(1)} %get-tuple-element.41.refs_6_.refs_10_.refs_11_.gate_ref, bf16[256,256]{1,0:T(8,128)(2,1)S(1)} %get-tuple-element.31.refs_3_.kq_ref, ...), custom_call_target="tpu_custom_call" | custom-call | tf_op jit(solution)/shard_map/prompt_finish/pallas_call | solution.py:422
  82.5 0.0 collective-permute-done.13.other_ref
  82.5 2.5 %resp_finish.1 = bf16[128,5120]{1,0:T(8,128)(2,1)} custom-call(s32[6]{0:T(128)S(1)} %stack.19.refs_0_.where_ref, f32[8,128,640]{2,1,0:T(8,128)S(1)} %get-tuple-element.48.refs_8_.part_ref, f32[8,128,640]{2,1,0:T(8,128)S(1)} %get-tuple-element.49.refs_9_.gate_ref, bf16[128,256]{1,0:T(8,128)(2,1)S(1)} %get-tuple-element.52.kq_ref, ...), custom_call_target="tpu_custom_call" | custom-call | tf_op jit(solution)/shard_map/resp_finish/pallas_call | solution.py:422
  (3 shorter events, 0.0 us)
Async XLA Ops:
  0.6 13.5 %copy-start.6 = (f32[4,5376]{1,0:T(4,128)S(1)}, f32[4,5376]{1,0:T(4,128)}, u32[]{:S(2)}) copy-start(f32[4,5376]{1,0:T(4,128)} %refs_4_.3) | copy-start | bytes 258052
  1.6 12.6 %collective-permute-start = (bf16[8,5376]{1,0:T(8,128)(2,1)S(1)}, bf16[8,5376]{1,0:T(8,128)(2,1)S(1)}, u32[]{:S(2)}, u32[]{:S(2)}) collective-permute-start(bf16[8,5376]{1,0:T(8,128)(2,1)S(1)} %slice.3.refs_5_.refs_4_), channel_id=1, source_target_pairs={{0,1},{1,2},{2,3},{3,4},{4,5},{5,6},{6,7},{7,8},{8,9},{9,10},{10,1... | collective-permute-start | bytes 258056 | tf_op jit(solution)/shard_map/ppermute | solution.py:520
  7.6 1.8 %copy-start = (bf16[256,5376]{1,0:T(8,128)(2,1)S(1)}, bf16[256,5376]{1,0:T(8,128)(2,1)}, u32[]{:S(2)}) copy-start(bf16[256,5376]{1,0:T(8,128)(2,1)} %refs_1_.3) | copy-start | bytes 8257540
  9.4 0.9 %copy-start.5 = (f32[4,5376]{1,0:T(4,128)S(1)}, f32[4,5376]{1,0:T(4,128)}, u32[]{:S(2)}) copy-start(f32[4,5376]{1,0:T(4,128)} %refs_4_.3) | copy-start | bytes 258052
  10.3 0.9 %copy-start.8 = (f32[80,256]{1,0:T(8,128)S(1)}, f32[80,256]{1,0:T(8,128)}, u32[]{:S(2)}) copy-start(f32[80,256]{1,0:T(8,128)} %refs_1_.2) | copy-start | bytes 245764
  11.2 0.9 %copy-start.9 = (f32[80,256]{1,0:T(8,128)S(1)}, f32[80,256]{1,0:T(8,128)}, u32[]{:S(2)}) copy-start(f32[80,256]{1,0:T(8,128)} %refs_2_.2) | copy-start | bytes 245764
  12.1 0.7 copy-start.12
  12.7 1.8 %copy-start.1 = (bf16[256,5376]{1,0:T(8,128)(2,1)S(1)}, bf16[256,5376]{1,0:T(8,128)(2,1)}, u32[]{:S(2)}) copy-start(bf16[256,5376]{1,0:T(8,128)(2,1)} %refs_1_.3) | copy-start | bytes 8257540
  14.5 15.3 %copy-start.2 = (bf16[256,5120]{1,0:T(8,128)(2,1)S(1)}, bf16[256,5120]{1,0:T(8,128)(2,1)}, u32[]{:S(2)}) copy-start(bf16[256,5120]{1,0:T(8,128)(2,1)} %refs_2_.3) | copy-start | bytes 7864324
  22.0 2.3 %collective-permute-start.1 = (bf16[4,144,640]{2,1,0:T(8,128)(2,1)S(1)}, bf16[4,144,640]{2,1,0:T(8,128)(2,1)S(1)}, u32[]{:S(2)}, u32[]{:S(2)}) collective-permute-start(bf16[4,144,640]{2,1,0:T(8,128)(2,1)S(1)} %get-tuple-element.36), channel_id=1, source_target_pairs={{0,1},{1,0},{2,3},{3,2},{4,5},{5,4},{6,7},{7,6},{8,9},{9,8},{10,11... | collective-permute-start | bytes 2211848 | tf_op jit(solution)/shard_map/ppermute | solution.py:445
  25.2 9.8 %collective-permute-start.2 = (bf16[144,640]{1,0:T(8,128)(2,1)S(1)}, bf16[144,640]{1,0:T(8,128)(2,1)S(1)}, u32[]{:S(2)}, u32[]{:S(2)}) collective-permute-start(bf16[144,640]{1,0:T(8,128)(2,1)S(1)} %get-tuple-element.37.refs_8_), channel_id=1, source_target_pairs={{0,2},{1,3},{2,4},{3,5},{4,6},{5,7},{6,0},{7,1},{8,10},{9,11},{10,... | collective-permute-start | bytes 552968 | tf_op jit(solution)/shard_map/ppermute | solution.py:445
  26.5 11.0 %collective-permute-start.3 = (bf16[144,640]{1,0:T(8,128)(2,1)S(1)}, bf16[144,640]{1,0:T(8,128)(2,1)S(1)}, u32[]{:S(2)}, u32[]{:S(2)}) collective-permute-start(bf16[144,640]{1,0:T(8,128)(2,1)S(1)} %get-tuple-element.38.refs_9_), channel_id=1, source_target_pairs={{0,4},{1,5},{2,6},{3,7},{4,0},{5,1},{6,2},{7,3},{8,12},{9,13},{10,... | collective-permute-start | bytes 552968 | tf_op jit(solution)/shard_map/ppermute | solution.py:445
  29.0 8.6 %collective-permute-start.4 = (bf16[144,640]{1,0:T(8,128)(2,1)S(1)}, bf16[144,640]{1,0:T(8,128)(2,1)S(1)}, u32[]{:S(2)}, u32[]{:S(2)}) collective-permute-start(bf16[144,640]{1,0:T(8,128)(2,1)S(1)} %get-tuple-element.39.refs_10_), channel_id=1, source_target_pairs={{0,6},{1,7},{2,0},{3,1},{4,2},{5,3},{6,4},{7,5},{8,14},{9,15},{10,... | collective-permute-start | bytes 552968 | tf_op jit(solution)/shard_map/ppermute | solution.py:445
  38.4 23.4 %copy-start.3 = (bf16[1,128,5376]{2,1,0:T(8,128)(2,1)S(1)}, bf16[1,128,5376]{2,1,0:T(8,128)(2,1)}, u32[]{:S(2)}) copy-start(bf16[1,128,5376]{2,1,0:T(8,128)(2,1)} %param.17) | copy-start | bytes 4128772
  38.4 23.4 %copy-start.4 = (bf16[1,128,5120]{2,1,0:T(8,128)(2,1)S(1)}, bf16[1,128,5120]{2,1,0:T(8,128)(2,1)}, u32[]{:S(2)}) copy-start(bf16[1,128,5120]{2,1,0:T(8,128)(2,1)} %param.18) | copy-start | bytes 3932164
  38.4 23.3 %copy-start.10 = (f32[80,1,128]{2,1,0:T(1,128)S(1)}, f32[80,1,128]{2,1,0:T(1,128)}, u32[]{:S(2)}) copy-start(f32[80,1,128]{2,1,0:T(1,128)} %param.20) | copy-start | bytes 122884
  38.4 23.3 %copy-start.11 = (f32[80,1,128]{2,1,0:T(1,128)S(1)}, f32[80,1,128]{2,1,0:T(1,128)}, u32[]{:S(2)}) copy-start(f32[80,1,128]{2,1,0:T(1,128)} %param.19) | copy-start | bytes 122884
  38.4 5.3 %collective-permute-start.7 = (bf16[144,640]{1,0:T(8,128)(2,1)S(1)}, bf16[144,640]{1,0:T(8,128)(2,1)S(1)}, u32[]{:S(2)}, u32[]{:S(2)}) collective-permute-start(bf16[144,640]{1,0:T(8,128)(2,1)S(1)} %row.1.refs_5_), channel_id=1, source_target_pairs={{0,24},{1,25},{2,26},{3,27},{4,28},{5,29},{6,30},{7,31},{8,0},{9,1... | collective-permute-start | bytes 552968 | tf_op jit(solution)/shard_map/ppermute | solution.py:445
  40.5 6.0 %collective-permute-start.6 = (bf16[144,640]{1,0:T(8,128)(2,1)S(1)}, bf16[144,640]{1,0:T(8,128)(2,1)S(1)}, u32[]{:S(2)}, u32[]{:S(2)}) collective-permute-start(bf16[144,640]{1,0:T(8,128)(2,1)S(1)} %row.1.refs_5_), channel_id=1, source_target_pairs={{0,16},{1,17},{2,18},{3,19},{4,20},{5,21},{6,22},{7,23},{8,24},{9,... | collective-permute-start | bytes 552968 | tf_op jit(solution)/shard_map/ppermute | solution.py:445
  41.6 10.5 %collective-permute-start.5 = (bf16[144,640]{1,0:T(8,128)(2,1)S(1)}, bf16[144,640]{1,0:T(8,128)(2,1)S(1)}, u32[]{:S(2)}, u32[]{:S(2)}) collective-permute-start(bf16[144,640]{1,0:T(8,128)(2,1)S(1)} %row.1.refs_5_), channel_id=1, source_target_pairs={{0,8},{1,9},{2,10},{3,11},{4,12},{5,13},{6,14},{7,15},{8,16},{9,17... | collective-permute-start | bytes 552968 | tf_op jit(solution)/shard_map/ppermute | solution.py:445
  54.5 12.1 %collective-permute-start.8 = (bf16[256,640]{1,0:T(8,128)(2,1)S(1)}, bf16[256,640]{1,0:T(8,128)(2,1)S(1)}, u32[]{:S(2)}, u32[]{:S(2)}) collective-permute-start(bf16[256,640]{1,0:T(8,128)(2,1)S(1)} %get-tuple-element.44.refs_10_), channel_id=1, source_target_pairs={{0,2},{1,3},{2,4},{3,5},{4,6},{5,7},{6,0},{7,1},{8,10},{9,11},{10,... | collective-permute-start | bytes 983048 | tf_op jit(solution)/shard_map/ppermute | solution.py:445
  56.8 16.9 %collective-permute-start.9 = (bf16[256,640]{1,0:T(8,128)(2,1)S(1)}, bf16[256,640]{1,0:T(8,128)(2,1)S(1)}, u32[]{:S(2)}, u32[]{:S(2)}) collective-permute-start(bf16[256,640]{1,0:T(8,128)(2,1)S(1)} %get-tuple-element.45.refs_11_), channel_id=1, source_target_pairs={{0,4},{1,5},{2,6},{3,7},{4,0},{5,1},{6,2},{7,3},{8,12},{9,13},{10,... | collective-permute-start | bytes 983048 | tf_op jit(solution)/shard_map/ppermute | solution.py:445
  59.4 14.3 %collective-permute-start.10 = (bf16[256,640]{1,0:T(8,128)(2,1)S(1)}, bf16[256,640]{1,0:T(8,128)(2,1)S(1)}, u32[]{:S(2)}, u32[]{:S(2)}) collective-permute-start(bf16[256,640]{1,0:T(8,128)(2,1)S(1)} %get-tuple-element.46.refs_12_), channel_id=1, source_target_pairs={{0,6},{1,7},{2,0},{3,1},{4,2},{5,3},{6,4},{7,5},{8,14},{9,15},{10,... | collective-permute-start | bytes 983048 | tf_op jit(solution)/shard_map/ppermute | solution.py:445
  59.4 2.3 %collective-permute-start.11 = (bf16[16,640]{1,0:T(8,128)(2,1)S(1)}, bf16[16,640]{1,0:T(8,128)(2,1)S(1)}, u32[]{:S(2)}, u32[]{:S(2)}) collective-permute-start(bf16[16,640]{1,0:T(8,128)(2,1)S(1)} %get-tuple-element.47.refs_2_), channel_id=1, source_target_pairs={{0,1},{1,0},{2,3},{3,2},{4,5},{5,4},{6,7},{7,6},{8,9},{9,8},{10,11... | collective-permute-start | bytes 61448 | tf_op jit(solution)/shard_map/ppermute | solution.py:445
  73.7 4.8 %copy-start.7 = (f32[5120]{0:T(1024)S(1)}, f32[5120]{0:T(1024)}, u32[]{:S(2)}) copy-start(f32[5120]{0:T(1024)} %param.25) | copy-start | bytes 61444
  75.4 3.1 %collective-permute-start.12 = (bf16[4,128,640]{2,1,0:T(8,128)(2,1)S(1)}, bf16[4,128,640]{2,1,0:T(8,128)(2,1)S(1)}, u32[]{:S(2)}, u32[]{:S(2)}) collective-permute-start(bf16[4,128,640]{2,1,0:T(8,128)(2,1)S(1)} %get-tuple-element.51), channel_id=1, source_target_pairs={{0,1},{1,0},{2,3},{3,2},{4,5},{5,4},{6,7},{7,6},{8,9},{9,8},{10,11... | collective-permute-start | bytes 1966088 | tf_op jit(solution)/shard_map/ppermute | solution.py:445
  76.8 5.7 %collective-permute-start.13 = (bf16[4,128,640]{2,1,0:T(8,128)(2,1)S(1)}, bf16[4,128,640]{2,1,0:T(8,128)(2,1)S(1)}, u32[]{:S(2)}, u32[]{:S(2)}) collective-permute-start(bf16[4,128,640]{2,1,0:T(8,128)(2,1)S(1)} %get-tuple-element.53.mine_ref), channel_id=1, source_target_pairs={{0,1},{1,0},{2,3},{3,2},{4,5},{5,4},{6,7},{7,6},{8,9},{9,8},{10,11... | collective-permute-start | bytes 1966088 | tf_op jit(solution)/shard_map/ppermute | solution.py:445

commit v2 on v1

v2 whole, which is shorter than its diff:
```python
import functools

import jax
import jax.numpy as jnp
from jax import lax
from jax.experimental import pallas as pl
from jax.experimental.pallas import tpu as pltpu
from jax.sharding import PartitionSpec as P

HEADS = 80
HEAD_DIM = 64
STATE = 128
KERNEL = 4
BLOCK = 128
D_INNER = 5120
SLABS = 8
SLAB = D_INNER // SLABS
SLAB_HEADS = HEADS // SLABS
PAIRS = SLAB // 128
EXTRA = 16
HIST = 8
HALF_TAIL = (D_INNER + 2 * STATE) // 2
PIECES = -(-HALF_TAIL // SLAB)
EPS = 1e-05
GROUP = ("seq", "resp")
SIDE = 4

F32 = jnp.float32
BF16 = jnp.bfloat16


SMEM = pl.BlockSpec(memory_space=pltpu.SMEM)
VMEM = pl.BlockSpec(memory_space=pltpu.VMEM)
HBM = pl.BlockSpec(memory_space=pltpu.HBM)


def ordered(kernel, inputs, extra):
    def body(*refs):
        kernel(*refs[:inputs], *refs[inputs + extra :])

    return body


def params(mib=12):
    return pltpu.CompilerParams(vmem_limit_bytes=mib * 2**20)


def whole(kernel, where, arrays, shapes, name, after=(), scratch=(), outside=0):
    return pl.pallas_call(
        ordered(kernel, 1 + len(arrays), len(after)),
        in_specs=[SMEM] + [HBM] * outside + [VMEM] * (len(arrays) - outside + len(after)),
        out_specs=[VMEM] * len(shapes),
        out_shape=[jax.ShapeDtypeStruct(shape, dtype) for shape, dtype in shapes],
        scratch_shapes=list(scratch),
        compiler_params=params(),
        name=name,
    )(where, *(pltpu.with_memory_space_constraint(a, pltpu.HBM) for a in arrays[:outside]), *arrays[outside:], *after)


def silu(value):
    return 0.5 * value * (1.0 + jnp.tanh(0.5 * value))


def spread(table, pair):
    lane = lax.broadcasted_iota(jnp.int32, table.shape, 1)
    return jnp.take_along_axis(table, 2 * pair + lane // HEAD_DIM, axis=1, mode="promise_in_bounds")


def lanes(slab, count=SLAB):
    return pl.ds(pl.multiple_of(slab * SLAB, 128), count)


def first_part(shape):
    return lax.broadcasted_iota(jnp.int32, shape, 1) % HEAD_DIM < HEAD_DIM // 2


def extra_rows(decay, tail):
    wide = jnp.broadcast_to(decay, tail.shape)
    high = wide.astype(BF16).astype(F32)
    coded = jnp.where(first_part(tail.shape), high, wide - high)
    return jnp.where(lax.broadcasted_iota(jnp.int32, tail.shape, 0) == 0, coded, tail).astype(BF16)


def decay_of(rows):
    wide = rows.astype(F32)
    half = HEAD_DIM // 2
    other = jnp.where(first_part(wide.shape), pltpu.roll(wide, SLAB - half, 1), pltpu.roll(wide, half, 1))
    return (wide + other)[0:1]


def tail_rows(rows_ref, half):
    block = jnp.zeros((EXTRA, SLAB), F32)
    place = lax.broadcasted_iota(jnp.int32, block.shape, 0)
    for piece in range(PIECES):
        width = min(SLAB, HALF_TAIL - piece * SLAB)
        start = pl.multiple_of(half * HALF_TAIL + piece * SLAB, 128)
        wide = rows_ref[:, pl.ds(start, width)].astype(F32)
        if width < SLAB:
            wide = jnp.concatenate([wide, jnp.zeros((HIST, SLAB - width), F32)], axis=1)
        for row in range(KERNEL - 1):
            line = wide[HIST - (KERNEL - 1) + row : HIST - (KERNEL - 1) + row + 1]
            block = jnp.where(place == 1 + PIECES * row + piece, line, block)
    return block


def block_table(keep, step):
    lane = lax.broadcasted_iota(jnp.int32, (HEADS, BLOCK), 1)
    cum = keep
    for by in (1, 2, 4, 8, 16, 32, 64):
        cum = cum + jnp.where(lane >= by, pltpu.roll(cum, by, 1), 0.0)
    gap = cum - 0.5 * cum[:, BLOCK - 1 : BLOCK]
    col = jnp.exp(-gap) * step
    blank = jnp.zeros((128 - HEADS, BLOCK), F32)
    return col, jnp.concatenate([jnp.exp(gap), blank], axis=0).T, jnp.concatenate([col, blank], axis=0).T


def tables_kernel(
    where_ref, keep_from, step_from, skip_ref, col_ref, rowt_ref, colt_ref, hcol_ref, keep_ref, step_ref, sems
):
    copies = [
        pltpu.make_async_copy(keep_from, keep_ref, sems.at[0]),
        pltpu.make_async_copy(step_from, step_ref, sems.at[1]),
    ]
    for copy in copies:
        copy.start()
    for copy in copies:
        copy.wait()
    place = lax.broadcasted_iota(jnp.int32, (8, 128), 0)
    stack = jnp.zeros((8, 128), F32)
    for block in range(2):
        here = slice(block * BLOCK, (block + 1) * BLOCK)
        col_ref[block], rowt, colt_ref[block] = block_table(keep_ref[:, here], step_ref[:, here])
        rowt_ref[block] = rowt
        stack = jnp.where(place == block, rowt[BLOCK - 1 : BLOCK], stack)
    stack = jnp.where(place == 3, jnp.concatenate([skip_ref[...], jnp.zeros((1, 128 - HEADS), F32)], axis=1), stack)
    for pair in range(HEADS // 2):
        at = (pair % PAIRS) * 128
        hcol_ref[pair // PAIRS, :, at : at + 128] = spread(stack, pair)


def conv_columns(rows, hist, weight, bias):
    wide = jnp.concatenate([hist, rows.astype(F32)], axis=0)
    total = bias + weight[KERNEL - 1 : KERNEL] * wide
    for back in range(1, KERNEL):
        total = total + weight[KERNEL - 1 - back : KERNEL - back] * pltpu.roll(wide, back, 0)
    return silu(total[HIST:]).astype(BF16)


def add_states(slab, at, conv, colt_ref, hcol_ref, keyt_ref, acts_ref, high_ref, weighted_ref, put):
    shift = lax.rem(128 - SLAB_HEADS * slab, 128)
    colts = [pltpu.roll(colt_ref[block], shift, 1) for block in range(2)]
    for pair in range(PAIRS):
        cols = slice(pair * 128, pair * 128 + 128)
        acts = conv(pl.ds(pl.multiple_of(slab * SLAB + pair * 128, 128), 128))
        acts_ref[at, :, cols] = acts
        for block in range(2):
            here = slice(block * BLOCK, (block + 1) * BLOCK)
            weight = spread(colts[block], pair) * hcol_ref[slab, block : block + 1, cols]
            weighted_ref[here, cols] = (acts[here].astype(F32) * weight).astype(BF16)
    first = jnp.dot(keyt_ref[:, 0:BLOCK], weighted_ref[0:BLOCK], preferred_element_type=F32)
    second = jnp.dot(keyt_ref[:, BLOCK:], weighted_ref[BLOCK:], preferred_element_type=F32)
    high_ref[at] = first.astype(BF16)
    put(hcol_ref[slab, 1:2] ** 2 * first + second)


def convolver(where_ref, x_ref, hist_ref, w_ref, b_ref):
    keep_history = where_ref[3].astype(F32)

    def conv(cols):
        hist = hist_ref[:, cols].astype(F32) * keep_history
        return conv_columns(x_ref[:, cols], hist, w_ref[:, cols], b_ref[:, cols])

    return conv


def sent_states_kernel(
    where_ref, x_from, w_from, hist_ref, b_ref, rows_ref, colt_ref, hcol_ref,
    acts_ref, kq_ref, keyt_ref, high_ref, msg_ref, x_ref, w_ref, weighted_ref, sems,
):
    half = 1 - where_ref[2]
    kq_cols = pl.ds(D_INNER, 2 * STATE)
    copies = [
        pltpu.make_async_copy(w_from, w_ref, sems.at[0]),
        pltpu.make_async_copy(x_from.at[:, kq_cols], x_ref.at[:, kq_cols], sems.at[1]),
    ]
    for at in range(4):
        cols = pl.ds(pl.multiple_of((half * 4 + at) * SLAB, 128), SLAB)
        copies.append(pltpu.make_async_copy(x_from.at[:, cols], x_ref.at[:, cols], sems.at[2 + at]))
    for copy in copies:
        copy.start()
    conv = convolver(where_ref, x_ref, hist_ref, w_ref, b_ref)
    for copy in copies[:2]:
        copy.wait()
    key = conv(slice(D_INNER, D_INNER + STATE))
    kq_ref[:, 0:STATE] = key
    kq_ref[:, STATE : 2 * STATE] = conv(slice(D_INNER + STATE, D_INNER + 2 * STATE))
    keyt_ref[...] = key.astype(F32).T.astype(BF16)
    for copy in copies[2:]:
        copy.wait()

    def body(at, carry):
        slab = half * 4 + at

        def put(state):
            msg_ref[at, 0:STATE] = state.astype(BF16)

        add_states(slab, at, conv, colt_ref, hcol_ref, keyt_ref, acts_ref, high_ref, weighted_ref, put)
        decay = (hcol_ref[slab, 0:1] * hcol_ref[slab, 1:2]) ** 2
        msg_ref[at, STATE:] = extra_rows(decay, jnp.zeros((EXTRA, SLAB), F32))
        return carry

    lax.fori_loop(0, 4, body, 0)
    slab = half * 4
    decay = (hcol_ref[slab, 0:1] * hcol_ref[slab, 1:2]) ** 2
    msg_ref[0, STATE:] = extra_rows(decay, tail_rows(rows_ref, half))


def kept_states_kernel(
    where_ref, x_ref, w_ref, hist_ref, b_ref, keyt_ref, colt_ref, hcol_ref, acts_ref, high_ref, own_ref, weighted_ref
):
    half = where_ref[2]
    conv = convolver(where_ref, x_ref, hist_ref, w_ref, b_ref)

    def body(at, carry):
        def put(state):
            own_ref[at] = state

        add_states(half * 4 + at, at, conv, colt_ref, hcol_ref, keyt_ref, acts_ref, high_ref, weighted_ref, put)
        return carry

    lax.fori_loop(0, 4, body, 0)


def masked_scores(key_query):
    scores = lax.dot_general(
        key_query[:, STATE:], key_query[:, :STATE], (((1,), (1,)), ((), ())), preferred_element_type=F32
    )
    row = lax.broadcasted_iota(jnp.int32, (BLOCK, BLOCK), 0)
    col = lax.broadcasted_iota(jnp.int32, (BLOCK, BLOCK), 1)
    return jnp.where(row >= col, scores, 0.0)


def within_pair(scores, col_rows, values):
    mixes = [(scores * row).astype(BF16) for row in col_rows]
    first = lax.broadcasted_iota(jnp.int32, (BLOCK, 128), 1) < HEAD_DIM
    wide = values.astype(F32)
    stacked = jnp.concatenate(
        [jnp.where(first, wide, 0.0).astype(BF16), jnp.where(first, 0.0, wide).astype(BF16)], axis=0
    )
    return jnp.dot(jnp.concatenate(mixes, axis=1), stacked, preferred_element_type=F32)


def prompt_within_kernel(
    where_ref, sent_acts, kept_acts, z_ref, kq_ref, sent_high, kept_high, col_ref, rowt_ref, hcol_ref,
    part_ref, gate_ref, scores_ref,
):
    for block in range(2):
        scores_ref[block] = masked_scores(kq_ref[block * BLOCK : (block + 1) * BLOCK, :])

    def step(half, acts_ref, high_ref, at, carry):
        slab = half * 4 + at
        shift = lax.rem(128 - SLAB_HEADS * slab, 128)
        rowts = [pltpu.roll(rowt_ref[block], shift, 1) for block in range(2)]
        earlier = jnp.dot(kq_ref[BLOCK : 2 * BLOCK, STATE:], high_ref[at], preferred_element_type=F32)
        for pair in range(PAIRS):
            cols = slice(pair * 128, pair * 128 + 128)
            gate_cols = pl.ds(pl.multiple_of(slab * SLAB + pair * 128, 128), 128)
            first_half = hcol_ref[slab, 0:1, cols]
            second_half = hcol_ref[slab, 1:2, cols]
            skip = hcol_ref[slab, 3:4, cols]
            head = slab * SLAB_HEADS + 2 * pair
            for block in range(2):
                here = slice(block * BLOCK, (block + 1) * BLOCK)
                values = acts_ref[at, here, cols]
                col_rows = [col_ref[block, pl.ds(head + which, 1), :] for which in range(2)]
                mixed = within_pair(scores_ref[block], col_rows, values)
                scale = first_half
                if block == 1:
                    mixed += second_half * earlier[:, cols]
                    scale = second_half * first_half * first_half
                gate = silu(z_ref[here, gate_cols].astype(F32))
                row = spread(rowts[block], pair)
                part_ref[slab, here, cols] = (row * mixed + skip * values.astype(F32)) * gate
                gate_ref[slab, here, cols] = row * scale * gate
        return carry

    core = where_ref[2]
    lax.fori_loop(0, 4, functools.partial(step, 1 - core, sent_acts, sent_high), 0)
    lax.fori_loop(0, 4, functools.partial(step, core, kept_acts, kept_high), 0)


def resp_within_kernel(
    where_ref, x_ref, mine_ref, other_ref, w_ref, b_ref, z_ref, keep_ref, step_ref, hcol_ref, final_ref,
    part_ref, gate_ref, kq_ref, passed_ref, hist_ref, scores_ref, col_ref, rowt_ref,
):
    core = where_ref[2]
    passed_ref[...] = final_ref[...]
    for half in range(2):
        flag = (core == half).astype(F32)
        tail = mine_ref[...].astype(F32) * flag + other_ref[...].astype(F32) * (1.0 - flag)
        for piece in range(PIECES):
            width = min(SLAB, HALF_TAIL - piece * SLAB)
            start = half * HALF_TAIL + piece * SLAB
            block = jnp.zeros((HIST, SLAB), F32)
            place = lax.broadcasted_iota(jnp.int32, block.shape, 0)
            for row in range(KERNEL - 1):
                at = 1 + PIECES * row + piece
                block = jnp.where(place == HIST - (KERNEL - 1) + row, tail[at : at + 1], block)
            hist_ref[:, start : start + width] = block[:, 0:width]
    col_ref[...], rowt_ref[...], _ = block_table(keep_ref[...], step_ref[...])

    def conv(cols):
        return conv_columns(x_ref[:, cols], hist_ref[:, cols], w_ref[:, cols], b_ref[:, cols])

    for at in (0, STATE):
        kq_ref[:, at : at + STATE] = conv(slice(D_INNER + at, D_INNER + at + STATE))
    scores_ref[...] = masked_scores(kq_ref[...])

    def step(slab, carry):
        rowt = pltpu.roll(rowt_ref[...], lax.rem(128 - SLAB_HEADS * slab, 128), 1)
        for pair in range(PAIRS):
            cols = slice(pair * 128, pair * 128 + 128)
            wide_cols = pl.ds(pl.multiple_of(slab * SLAB + pair * 128, 128), 128)
            values = conv(wide_cols)
            head = slab * SLAB_HEADS + 2 * pair
            col_rows = [col_ref[pl.ds(head + which, 1), :] for which in range(2)]
            mixed = within_pair(scores_ref[...], col_rows, values)
            gate = silu(z_ref[:, wide_cols].astype(F32))
            row = spread(rowt, pair)
            half = row[BLOCK - 1 : BLOCK]
            part_ref[slab, :, cols] = (row * mixed + hcol_ref[slab, 3:4, cols] * values.astype(F32)) * gate
            gate_ref[slab, :, cols] = row * half * gate
        return carry

    lax.fori_loop(0, SLABS, step, 0)


def at_shift(place, by):
    return lax.rem(place + by + SIDE, SIDE)


def pick(condition, value):
    flag = condition.astype(F32)
    return value * flag + (1.0 - flag)


CHUNKS = [slice(at, at + 128) for at in range(0, SLAB, 128)]


def chip_kernel(where_ref, own_ref, recv_ref, hcol_ref, rows_ref, *out_refs):
    x, core = where_ref[0], where_ref[2]
    first = (core == 0).astype(F32)
    tail = tail_rows(rows_ref, core) * (1.0 - first) + recv_ref[0, STATE:, :].astype(F32) * first
    for shift in range(SIDE):
        slab = at_shift(x, shift)
        half = hcol_ref[core * 4 + slab]
        mine = (half[0:1] * half[1:2]) ** 2
        theirs = decay_of(recv_ref[slab, STATE:, :])
        own_scale = theirs * first + (1.0 - first)
        recv_scale = mine * (1.0 - first) + first
        for cols in CHUNKS:
            received = recv_ref[slab, 0:STATE, cols].astype(F32)
            state = own_scale[:, cols] * own_ref[slab, :, cols] + recv_scale[:, cols] * received
            out_refs[shift][0:STATE, cols] = state.astype(BF16)
        out_refs[shift][STATE:] = extra_rows(mine * theirs, tail)


def weights_to(places, decays, target):
    ones = jnp.ones((1, SLAB), F32)
    weights = []
    for i in range(SIDE):
        scale = (places[i] < target).astype(F32) * ones
        for k in range(SIDE):
            if k != i:
                between = jnp.logical_and(places[k] > places[i], places[k] < target)
                scale = scale * pick(between, decays[k])
        weights.append(scale)
    through = ones
    for k in range(SIDE):
        through = through * pick(places[k] < target, decays[k])
    return weights, through


def weighted_sum(weights, refs, cols):
    return sum(w[:, cols] * ref[0:STATE, cols].astype(F32) for w, ref in zip(weights, refs))


def last_tail(places, refs):
    return sum(ref[STATE:].astype(F32) * (place == SIDE - 1).astype(F32) for place, ref in zip(places, refs))


def row_kernel(where_ref, r0, r1, r2, r3, out_ref):
    refs = (r0, r1, r2, r3)
    places = [at_shift(where_ref[0], -i) for i in range(SIDE)]
    weights, through = weights_to(places, [decay_of(ref[STATE:]) for ref in refs], SIDE)
    for cols in CHUNKS:
        out_ref[0:STATE, cols] = weighted_sum(weights, refs, cols).astype(BF16)
    out_ref[STATE:] = extra_rows(through, last_tail(places, refs))


def entering_kernel(where_ref, r0, r1, r2, r3, t0, t1, t2, t3, e0, e1, e2, e3, final_ref, tail_ref):
    x, y = where_ref[0], where_ref[1]
    refs, totals, outs = (r0, r1, r2, r3), (t0, t1, t2, t3), (e0, e1, e2, e3)
    rows = [at_shift(y, -i) for i in range(SIDE)]
    row_decays = [decay_of(ref[STATE:]) for ref in totals]
    to_end, _ = weights_to(rows, row_decays, SIDE)
    to_row, _ = weights_to(rows, row_decays, y)
    places = [at_shift(x, -i) for i in range(SIDE)]
    decays = [decay_of(ref[STATE:]) for ref in refs]
    to_chips = [weights_to(places, decays, at_shift(x, shift)) for shift in range(SIDE)]
    for cols in CHUNKS:
        final_ref[:, cols] = weighted_sum(to_end, totals, cols).astype(BF16)
        row_in = weighted_sum(to_row, totals, cols)
        for out, (weights, through) in zip(outs, to_chips):
            out[:, cols] = (through[:, cols] * row_in + weighted_sum(weights, refs, cols)).astype(BF16)
    tail_ref[...] = last_tail(rows, totals).astype(BF16)


def cores_kernel(where_ref, g0, g1, g2, g3, own_ref, recv_ref, hcol_ref, mine_ref, send_ref):
    x, core = where_ref[0], where_ref[2]
    first = (core == 0).astype(F32)
    last = 1.0 - first
    for i, ref in enumerate((g0, g1, g2, g3)):
        slab = at_shift(x, -i)
        half = hcol_ref[core * 4 + slab]
        mine = (half[0:1] * half[1:2]) ** 2
        decay = mine * first + decay_of(recv_ref[slab, STATE:, :]) * last
        for cols in CHUNKS:
            earlier = own_ref[slab, :, cols] * first + recv_ref[slab, 0:STATE, cols].astype(F32) * last
            start = ref[:, cols].astype(F32)
            later = decay[:, cols] * start + earlier
            mine_ref[slab, :, cols] = (start * first + later * last).astype(BF16)
            send_ref[slab, :, cols] = (later * first + start * last).astype(BF16)


def gather_kernel(where_ref, f0, f1, f2, f3, out_ref):
    for i, ref in enumerate((f0, f1, f2, f3)):
        out_ref[at_shift(where_ref[0], -i)] = ref[...]


TILE = 64


def half_gated(query, held_ref, half, here, part_ref, gate_ref, put):
    squares = jnp.zeros((TILE, 128), F32)
    for s in range(4):
        carried = jnp.dot(query, held_ref[s], preferred_element_type=F32)
        for cols in CHUNKS:
            gated = part_ref[half * 4 + s, here, cols] + gate_ref[half * 4 + s, here, cols] * carried[:, cols]
            put(s, cols, gated)
            squares = squares + gated * gated
    return squares


def own_half_kernel(where_ref, part_ref, gate_ref, kq_ref, held_ref, gated_ref, squares_ref):
    def body(at, carry):
        here = pl.ds(pl.multiple_of(at * TILE, TILE), TILE)

        def put(s, cols, gated):
            gated_ref[s, here, cols] = gated

        query = kq_ref[here, STATE:]
        squares_ref[here, :] = half_gated(query, held_ref, where_ref[2], here, part_ref, gate_ref, put)
        return carry

    lax.fori_loop(0, part_ref.shape[1] // TILE, body, 0)


def own_half(where, part, gate, kq, held, name, after=()):
    rows = part.shape[1]
    shapes = [((4, rows, SLAB), F32), ((rows, 128), F32)]
    return whole(own_half_kernel, where, (part, gate, kq, held), shapes, name, after)


def finish_kernel(
    length_at, where_ref, part_ref, gate_ref, kq_ref, held_ref, own_ref, squares_ref, gain_ref,
    out_ref, token_ref, gated_ref,
):
    core = where_ref[2]
    start = pl.program_id(0) * TILE
    here = pl.ds(pl.multiple_of(start, TILE), TILE)

    def put(s, cols, gated):
        gated_ref[s, :, cols] = gated

    squares = half_gated(kq_ref[here, STATE:], held_ref, 1 - core, here, part_ref, gate_ref, put)
    squares = squares + squares_ref[here, :]
    mean = jnp.sum(squares, axis=1, keepdims=True) * (1.0 / D_INNER)
    row = lax.broadcasted_iota(jnp.int32, (TILE, 1), 0) + start
    inv = jnp.where(row < where_ref[length_at], lax.rsqrt(mean + EPS), 0.0)
    inv = jnp.broadcast_to(inv, (TILE, 128))
    for s in range(4):
        for half, value_of in (
            (core, lambda cols: own_ref[s, here, cols]),
            (1 - core, lambda cols: gated_ref[s, :, cols]),
        ):
            for cols in CHUNKS:
                wide = pl.ds(pl.multiple_of((half * 4 + s) * SLAB + cols.start, 128), 128)
                out_ref[:, wide] = (value_of(cols) * inv * gain_ref[:, wide]).astype(BF16)
    token_ref[...] = jnp.zeros_like(token_ref)


def finish(where, part, gate, kq, held, own, squares, gain, length_at, name):
    rows = part.shape[1]
    return pl.pallas_call(
        functools.partial(finish_kernel, length_at),
        grid=(rows // TILE,),
        in_specs=[SMEM] + [VMEM] * 7,
        out_specs=[pl.BlockSpec((TILE, D_INNER), lambda i: (i, 0)), pl.BlockSpec((8, 128), lambda i: (0, 0))],
        scratch_shapes=[pltpu.VMEM((4, TILE, SLAB), F32)],
        out_shape=[jax.ShapeDtypeStruct((rows, D_INNER), BF16), jax.ShapeDtypeStruct((8, 128), F32)],
        compiler_params=params(),
        name=name,
    )(where, part, gate, kq, held, own, squares, gain)


def number(y, x, core):
    return (y % SIDE) * 2 * SIDE + (x % SIDE) * 2 + core


def moved(value, move):
    pairs = [
        (number(y, x, core), number(*move(y, x, core)))
        for y in range(SIDE)
        for x in range(SIDE)
        for core in range(2)
    ]
    return lax.ppermute(value, GROUP, pairs)


def swap_cores(value):
    return moved(value, lambda y, x, core: (y, x, 1 - core))


def along_x(value, by):
    return moved(value, lambda y, x, core: (y, x + by, core))


def along_y(value, by):
    return moved(value, lambda y, x, core: (y + by, x, core))


def make_tables(where, keep, step, skip):
    shapes = [((2, HEADS, BLOCK), F32), ((2, BLOCK, 128), F32), ((2, BLOCK, 128), F32), ((SLABS, 8, SLAB), F32)]
    scratch = [pltpu.VMEM(keep.shape, F32), pltpu.VMEM(step.shape, F32), pltpu.SemaphoreType.DMA((2,))]
    return whole(tables_kernel, where, (keep, step, skip[None, :]), shapes, "tables", scratch=scratch, outside=2)


def sent_states(where, xbc, weight, hist, bias, own_rows, colt, hcol):
    rows = xbc.shape[0]
    shapes = [
        ((4, rows, SLAB), BF16),
        ((rows, 2 * STATE), BF16),
        ((STATE, rows), BF16),
        ((4, STATE, SLAB), BF16),
        ((4, STATE + EXTRA, SLAB), BF16),
    ]
    scratch = [
        pltpu.VMEM(xbc.shape, BF16),
        pltpu.VMEM(weight.shape, F32),
        pltpu.VMEM((rows, SLAB), BF16),
        pltpu.SemaphoreType.DMA((6,)),
    ]
    arrays = (xbc, weight, hist, bias, own_rows, colt, hcol)
    return whole(sent_states_kernel, where, arrays, shapes, "sent_states", scratch=scratch, outside=2)


def kept_states(where, xbc, weight, hist, bias, keyt, colt, hcol, after):
    rows = xbc.shape[0]
    shapes = [((4, rows, SLAB), BF16), ((4, STATE, SLAB), BF16), ((4, STATE, SLAB), F32)]
    arrays = (xbc, weight, hist, bias, keyt, colt, hcol)
    return whole(kept_states_kernel, where, arrays, shapes, "kept_states", after, [pltpu.VMEM((rows, SLAB), BF16)])


def prompt_within(where, acts, z, kq, high, col, rowt, hcol, after):
    shapes = [((SLABS, z.shape[0], SLAB), F32)] * 2
    scratch = [pltpu.VMEM((2, BLOCK, BLOCK), F32)]
    arrays = (*acts, z, kq, *high, col, rowt, hcol)
    return whole(prompt_within_kernel, where, arrays, shapes, "prompt_within", after, scratch)


def resp_within(where, xbc, mine, other, weight, bias, z, keep, step, hcol, final, after):
    rows = z.shape[0]
    shapes = [((SLABS, rows, SLAB), F32)] * 2 + [((rows, 2 * STATE), BF16), (final.shape, BF16)]
    scratch = [
        pltpu.VMEM((HIST, D_INNER + 2 * STATE), F32),
        pltpu.VMEM((BLOCK, BLOCK), F32),
        pltpu.VMEM((HEADS, BLOCK), F32),
        pltpu.VMEM((BLOCK, 128), F32),
    ]
    arrays = (xbc, mine, other, weight, bias, z, keep, step, hcol, final)
    return whole(resp_within_kernel, where, arrays, shapes, "resp_within", after, scratch)


def shards(
    prompt_xbc,
    prompt_z,
    prompt_step,
    prompt_keep,
    resp_xbc,
    resp_z,
    resp_step,
    resp_keep,
    resp_len,
    conv_weight,
    conv_bias,
    skip,
    gain,
):
    rows = prompt_xbc.shape[0]
    seq, core = lax.axis_index("seq"), lax.axis_index("resp")
    fixed = [seq % SIDE, seq // SIDE, core, jnp.where(lax.axis_index(GROUP) == 0, 0, 1)]
    where = jnp.stack([jnp.asarray(v, jnp.int32) for v in fixed + [rows, resp_len[0]]])
    bias_row, gain_row = conv_bias[None, :], gain[None, :]

    own_rows = prompt_xbc[rows - HIST :]
    count = 2 * SIDE * SIDE
    hist = lax.ppermute(own_rows, GROUP, [(i, i + 1) for i in range(count - 1)])
    col, rowt, colt, hcol = make_tables(where, prompt_keep, prompt_step, skip)
    sent_acts, kq, keyt, sent_high, msg = sent_states(
        where, prompt_xbc, conv_weight, hist, bias_row, own_rows, colt, hcol
    )
    recv = swap_cores(msg)
    kept_acts, kept_high, own = kept_states(
        where, prompt_xbc, conv_weight, hist, bias_row, keyt, colt, hcol, after=(msg,)
    )
    with_extra, plain = ((STATE + EXTRA, SLAB), BF16), ((STATE, SLAB), BF16)
    c0, c1, c2, c3 = whole(chip_kernel, where, (own, recv, hcol, own_rows), [with_extra] * 4, "chip")
    pieces = (c0, along_x(c1, 1), along_x(c2, 2), along_x(c3, 3))
    part, gate = prompt_within(
        where, (sent_acts, kept_acts), prompt_z, kq, (sent_high, kept_high), col, rowt, hcol, after=(c1, c2, c3)
    )
    (total,) = whole(row_kernel, where, pieces, [with_extra], "row", after=(part, gate))
    totals = (total, along_y(total, 1), along_y(total, 2), along_y(total, 3))
    e0, e1, e2, e3, final, tail = whole(
        entering_kernel, where, pieces + totals, [plain] * 5 + [((EXTRA, SLAB), BF16)], "entering", after=(part, gate)
    )
    tail_other = swap_cores(tail)
    back = (e0, along_x(e1, 1), along_x(e2, 2), along_x(e3, 3))
    resp_part, resp_gate, resp_kq, final = resp_within(
        where, resp_xbc[0], tail, tail_other, conv_weight, bias_row, resp_z[0],
        resp_keep.reshape(HEADS, BLOCK), resp_step.reshape(HEADS, BLOCK), hcol, final, after=(e1, e2, e3),
    )
    finals = (final, along_x(final, 1), along_x(final, 2), along_x(final, 3))
    four = ((4, STATE, SLAB), BF16)
    mine, send = whole(
        cores_kernel, where, back + (own, recv, hcol), [four] * 2, "cores", after=(resp_part, resp_gate, part, gate)
    )
    other = swap_cores(send)
    gated, squares = own_half(where, part, gate, kq, mine, "prompt_own_half", after=(send,))
    prompt_out, token = finish(where, part, gate, kq, other, gated, squares, gain_row, 4, "prompt_finish")
    (final_mine,) = whole(gather_kernel, where, finals, [four], "gather", after=(token, resp_part, resp_gate))
    final_other = swap_cores(final_mine)
    gated, squares = own_half(where, resp_part, resp_gate, resp_kq, final_mine, "resp_own_half")
    resp_out, _ = finish(
        where, resp_part, resp_gate, resp_kq, final_other, gated, squares, gain_row, 5, "resp_finish"
    )
    return (prompt_out, resp_out[None])


def solution(mesh):
    return jax.shard_map(
        shards,
        mesh=mesh,
        in_specs=(
            P(("grp", "seq", "resp"), None),
            P(("grp", "seq", "resp"), None),
            P(None, ("grp", "seq", "resp")),
            P(None, ("grp", "seq", "resp")),
            P(("grp", "seq", "resp"), None, None),
            P(("grp", "seq", "resp"), None, None),
            P(None, ("grp", "seq", "resp"), None),
            P(None, ("grp", "seq", "resp"), None),
            P(("grp", "seq", "resp")),
            P(),
            P(),
            P(),
            P(),
        ),
        out_specs=(P(("grp", "seq", "resp"), None), P(("grp", "seq", "resp"), None, None)),
        check_vma=False,
    )
```

time: 85.4 us -> 81.1 us (0.950)
  waiting for transfers between devices: 24.4 us -> 13.3 us
  starting transfers between devices: 20.7 us -> 27.2 us
  Pallas kernels: 31.3 us -> 36.2 us
  local copies, waits for them, and re-layouts: 7.26 us -> 2.6 us
    ppermute x13 -> x16, waiting for transfers between devices: 24.4 us -> 13.3 us  [moved(): return lax.ppermute(value, GROUP, pairs)]
    ppermute x13 -> x16, starting transfers between devices: 16.2 us -> 22.7 us  [moved(): return lax.ppermute(value, GROUP, pairs)]
    pallas_call x8 -> x12, Pallas kernels: 24.8 us -> 29.7 us  [whole(): pl.pallas_call(ordered(kernel, 1 + len(arrays), len(after)), in_specs=[SM...]
    unnamed x26 -> x18, local copies, waits for them, and re-layouts: 5.49 us -> 0.71 us
  transfers between devices with their start and end apart: 14 -> 17, of which waited for: 8 -> 8; matrix products, arithmetic and copies ran while one was open for 1% -> 1% of each run, Pallas kernels for 18% -> 28%
where the time goes in v2:
time: 81.1 us; the launch traced here: 80.8 us
  Pallas kernels  36.2 us (45%)
  starting transfers between devices  27.2 us (34%)
  waiting for transfers between devices  13.3 us (16%)
  local copies, waits for them, and re-layouts  2.6 us (3%)
  between operations  1.54 us (2%)
    pallas_call x12, Pallas kernels, whole(): pl.pallas_call(ordered(kernel, 1 + len(arrays), len(after)), in_specs=[SM...  29.7 us
    ppermute x16, starting transfers between devices, moved(): return lax.ppermute(value, GROUP, pairs)  22.7 us
    ppermute x16, waiting for transfers between devices, moved(): return lax.ppermute(value, GROUP, pairs)  13.3 us
    pallas_call x2, Pallas kernels, finish(): pl.pallas_call(functools.partial(finish_kernel, length_at), grid=(rows //...  6.5 us
    ppermute x1, starting transfers between devices, shards(): hist = lax.ppermute(own_rows, GROUP, [(i, i + 1) for i in range(count - 1)])  4.5 us
  transfers between devices with their start and end apart: 17, of which 8 were waited for; matrix products, arithmetic and copies ran while one was open for 1% of the time, Pallas kernels for 28%

profile of v2, /device:TPU:1, one launch (start us, length us, event | category | flops | bytes accessed | tf_op | source)
XLA Modules:
  0.0 80.8 jit_solution(14332507024461005624)
XLA Ops:
  0.6 0.0 copy-start
  0.6 0.0 copy-start.4
  0.7 1.0 %slice.3.refs_5_.refs_4_ = bf16[8,5376]{1,0:T(8,128)(2,1)S(1)} slice(bf16[256,5376]{1,0:T(8,128)(2,1)} %refs_1_.5), slice={[248:256], [0:5376]} | slice | bytes 172032 | tf_op jit(solution)/shard_map/slice | solution.py:616
  1.7 4.5 %collective-permute-start = (bf16[8,5376]{1,0:T(8,128)(2,1)S(1)}, bf16[8,5376]{1,0:T(8,128)(2,1)S(1)}, u32[]{:S(2)}, u32[]{:S(2)}) collective-permute-start(bf16[8,5376]{1,0:T(8,128)(2,1)S(1)} %slice.3.refs_5_.refs_4_), channel_id=1, source_target_pairs={{0,1},{1,2},{2,3},{3,4},{4,5},{5,6},{6,7},{7,8},{8,9},{9,10},{10,1... | collective-permute-start | bytes 258056 | tf_op jit(solution)/shard_map/ppermute | solution.py:618
  6.9 0.8 broadcast_in_dim.12.refs_4_.refs_5_
  7.7 0.1 stack.19.refs_0_.where_ref
  7.7 0.7 copy-done.8
  8.4 2.4 %tables.1 = (f32[2,80,128]{2,1,0:T(8,128)S(1)}, f32[2,128,128]{2,1,0:T(8,128)S(1)}, f32[2,128,128]{2,1,0:T(8,128)S(1)}, f32[8,8,640]{2,1,0:T(8,128)S(1)}) custom-call(s32[6]{0:T(128)S(1)} %stack.19.refs_0_.where_ref, f32[80,256]{1,0:T(8,128)} %refs_1_.3, f32[80,256]{1,0:T(8,128)} %refs_2_.3, f32[1,80]{1,0:T(1,128)S(1)} %bitcast.17), custom_call_target="tpu_custom_call" | custom-call | tf_op jit(solution)/shard_map/tables/pallas_call | solution.py:49
  10.8 0.0 collective-permute-done.refs_3_
  10.8 5.4 %sent_states.1 = (bf16[4,256,640]{2,1,0:T(8,128)(2,1)S(1)}, bf16[256,256]{1,0:T(8,128)(2,1)S(1)}, bf16[128,256]{1,0:T(8,128)(2,1)S(1)}, bf16[4,128,640]{2,1,0:T(8,128)(2,1)S(1)}, bf16[4,144,640]{2,1,0:T(8,128)(2,1)S(1)}) custom-call(s32[6]{0:T(128)S(1)} %stack.19.refs_0_.where_ref, bf16[256,5376]{1,0:T(8,128)(2,1)} %refs_1_.5, f32[4,5376]{1,0:T(4,128)} %refs_4_.1, ...), custom_call_target="tpu_custom_call" | custom-call | tf_op jit(solution)/shard_map/sent_states/pallas_call | solution.py:49
  16.2 0.1 collective-permute-start.1
  16.3 0.0 copy-done
  16.3 0.0 copy-done.4
  16.3 0.0 copy-start.1
  16.3 3.9 %kept_states.1 = (bf16[4,256,640]{2,1,0:T(8,128)(2,1)S(1)}, bf16[4,128,640]{2,1,0:T(8,128)(2,1)S(1)}, f32[4,128,640]{2,1,0:T(8,128)S(1)}) custom-call(s32[6]{0:T(128)S(1)} %stack.19.refs_0_.where_ref, bf16[256,5376]{1,0:T(8,128)(2,1)S(1)} %copy-done, f32[4,5376]{1,0:T(4,128)S(1)} %copy-done.4, bf16[8,5376]{1,0:T(8,128)(2,1)S(1)} %collective-permute-done.refs_3_, ...), custom_call_target="tpu_custom_call" | custom-call | tf_op jit(solution)/shard_map/kept_states/pallas_call | solution.py:49
  20.2 0.0 collective-permute-done.1.refs_2_.refs_6_
  20.2 0.9 %chip.1 = (bf16[144,640]{1,0:T(8,128)(2,1)S(1)}, bf16[144,640]{1,0:T(8,128)(2,1)S(1)}, bf16[144,640]{1,0:T(8,128)(2,1)S(1)}, bf16[144,640]{1,0:T(8,128)(2,1)S(1)}) custom-call(s32[6]{0:T(128)S(1)} %stack.19.refs_0_.where_ref, f32[4,128,640]{2,1,0:T(8,128)S(1)} %get-tuple-element.50.refs_1_.refs_5_, ...), custom_call_target="tpu_custom_call" | custom-call | tf_op jit(solution)/shard_map/chip/pallas_call | solution.py:49
  21.1 1.3 %collective-permute-start.2 = (bf16[144,640]{1,0:T(8,128)(2,1)S(1)}, bf16[144,640]{1,0:T(8,128)(2,1)S(1)}, u32[]{:S(2)}, u32[]{:S(2)}) collective-permute-start(bf16[144,640]{1,0:T(8,128)(2,1)S(1)} %get-tuple-element.51.refs_10_), channel_id=1, source_target_pairs={{0,2},{1,3},{2,4},{3,5},{4,6},{5,7},{6,0},{7,1},{8,10},{9,11},{10,... | collective-permute-start | bytes 552968 | tf_op jit(solution)/shard_map/ppermute | solution.py:528
  22.4 2.4 %collective-permute-start.3 = (bf16[144,640]{1,0:T(8,128)(2,1)S(1)}, bf16[144,640]{1,0:T(8,128)(2,1)S(1)}, u32[]{:S(2)}, u32[]{:S(2)}) collective-permute-start(bf16[144,640]{1,0:T(8,128)(2,1)S(1)} %get-tuple-element.52.refs_11_), channel_id=1, source_target_pairs={{0,4},{1,5},{2,6},{3,7},{4,0},{5,1},{6,2},{7,3},{8,12},{9,13},{10,... | collective-permute-start | bytes 552968 | tf_op jit(solution)/shard_map/ppermute | solution.py:528
  24.8 0.9 %collective-permute-start.4 = (bf16[144,640]{1,0:T(8,128)(2,1)S(1)}, bf16[144,640]{1,0:T(8,128)(2,1)S(1)}, u32[]{:S(2)}, u32[]{:S(2)}) collective-permute-start(bf16[144,640]{1,0:T(8,128)(2,1)S(1)} %get-tuple-element.53.refs_12_), channel_id=1, source_target_pairs={{0,6},{1,7},{2,0},{3,1},{4,2},{5,3},{6,4},{7,5},{8,14},{9,15},{10,... | collective-permute-start | bytes 552968 | tf_op jit(solution)/shard_map/ppermute | solution.py:528
  25.7 0.0 copy-done.1
  25.7 5.2 %prompt_within.1 = (f32[8,256,640]{2,1,0:T(8,128)S(1)}, f32[8,256,640]{2,1,0:T(8,128)S(1)}) custom-call(s32[6]{0:T(128)S(1)} %stack.19.refs_0_.where_ref, bf16[4,256,640]{2,1,0:T(8,128)(2,1)S(1)} %get-tuple-element.41.refs_1_, bf16[4,256,640]{2,1,0:T(8,128)(2,1)S(1)} %get-tuple-element.44.refs_2_, bf16[256,5120]{1,0:T(8,128)(2,1)S(1)} %copy-done.1, ...), custom_call_target="tpu_custom_call" | custom-call | tf_op jit(solution)/shard_map/prompt_within/pallas_call | solution.py:49
  30.9 0.0 collective-permute-done.2.refs_2_
  30.9 2.2 %collective-permute-done.3.refs_3_ = bf16[144,640]{1,0:T(8,128)(2,1)S(1)} collective-permute-done((bf16[144,640]{1,0:T(8,128)(2,1)S(1)}, bf16[144,640]{1,0:T(8,128)(2,1)S(1)}, u32[]{:S(2)}, u32[]{:S(2)}) %collective-permute-start.3) | collective-permute-done | bytes 184352 | tf_op jit(solution)/shard_map/ppermute | solution.py:528
  33.0 0.0 collective-permute-done.4.refs_4_
  33.1 0.8 %row.1.refs_5_ = bf16[144,640]{1,0:T(8,128)(2,1)S(1)} custom-call(s32[6]{0:T(128)S(1)} %stack.19.refs_0_.where_ref, bf16[144,640]{1,0:T(8,128)(2,1)S(1)} %get-tuple-element.56.refs_1_, bf16[144,640]{1,0:T(8,128)(2,1)S(1)} %collective-permute-done.2.refs_2_, bf16[144,640]{1,0:T(8,128)(2,1)S(1)} %collective-permute-done.3.refs_3_, ...), custom_call_target="tpu_custom_call" | custom-call | tf_op jit(solution)/shard_map/row/pallas_call | solution.py:49
  33.9 0.0 copy-start.2
  33.9 0.0 copy-start.3
  33.9 0.0 copy-start.6
  33.9 0.0 copy-start.7
  33.9 1.4 %collective-permute-start.5 = (bf16[144,640]{1,0:T(8,128)(2,1)S(1)}, bf16[144,640]{1,0:T(8,128)(2,1)S(1)}, u32[]{:S(2)}, u32[]{:S(2)}) collective-permute-start(bf16[144,640]{1,0:T(8,128)(2,1)S(1)} %row.1.refs_5_), channel_id=1, source_target_pairs={{0,8},{1,9},{2,10},{3,11},{4,12},{5,13},{6,14},{7,15},{8,16},{9,17... | collective-permute-start | bytes 552968 | tf_op jit(solution)/shard_map/ppermute | solution.py:528
  35.3 2.5 %collective-permute-start.6 = (bf16[144,640]{1,0:T(8,128)(2,1)S(1)}, bf16[144,640]{1,0:T(8,128)(2,1)S(1)}, u32[]{:S(2)}, u32[]{:S(2)}) collective-permute-start(bf16[144,640]{1,0:T(8,128)(2,1)S(1)} %row.1.refs_5_), channel_id=1, source_target_pairs={{0,16},{1,17},{2,18},{3,19},{4,20},{5,21},{6,22},{7,23},{8,24},{9,... | collective-permute-start | bytes 552968 | tf_op jit(solution)/shard_map/ppermute | solution.py:528
  37.8 1.1 %collective-permute-start.7 = (bf16[144,640]{1,0:T(8,128)(2,1)S(1)}, bf16[144,640]{1,0:T(8,128)(2,1)S(1)}, u32[]{:S(2)}, u32[]{:S(2)}) collective-permute-start(bf16[144,640]{1,0:T(8,128)(2,1)S(1)} %row.1.refs_5_), channel_id=1, source_target_pairs={{0,24},{1,25},{2,26},{3,27},{4,28},{5,29},{6,30},{7,31},{8,0},{9,1... | collective-permute-start | bytes 552968 | tf_op jit(solution)/shard_map/ppermute | solution.py:528
  38.9 1.1 %collective-permute-done.5.refs_6_ = bf16[144,640]{1,0:T(8,128)(2,1)S(1)} collective-permute-done((bf16[144,640]{1,0:T(8,128)(2,1)S(1)}, bf16[144,640]{1,0:T(8,128)(2,1)S(1)}, u32[]{:S(2)}, u32[]{:S(2)}) %collective-permute-start.5) | collective-permute-done | bytes 184352 | tf_op jit(solution)/shard_map/ppermute | solution.py:528
  40.0 5.1 %collective-permute-done.6.refs_7_ = bf16[144,640]{1,0:T(8,128)(2,1)S(1)} collective-permute-done((bf16[144,640]{1,0:T(8,128)(2,1)S(1)}, bf16[144,640]{1,0:T(8,128)(2,1)S(1)}, u32[]{:S(2)}, u32[]{:S(2)}) %collective-permute-start.6) | collective-permute-done | bytes 184352 | tf_op jit(solution)/shard_map/ppermute | solution.py:528
  45.1 0.0 collective-permute-done.7.refs_8_
  45.1 1.7 %entering.1 = (bf16[128,640]{1,0:T(8,128)(2,1)S(1)}, bf16[128,640]{1,0:T(8,128)(2,1)S(1)}, bf16[128,640]{1,0:T(8,128)(2,1)S(1)}, bf16[128,640]{1,0:T(8,128)(2,1)...) custom-call(s32[6]{0:T(128)S(1)} %stack.19.refs_0_.where_ref, ...), custom_call_target="tpu_custom_call" | custom-call | tf_op jit(solution)/shard_map/entering/pallas_call | solution.py:49
  46.8 4.2 %collective-permute-start.10 = (bf16[128,640]{1,0:T(8,128)(2,1)S(1)}, bf16[128,640]{1,0:T(8,128)(2,1)S(1)}, u32[]{:S(2)}, u32[]{:S(2)}) collective-permute-start(bf16[128,640]{1,0:T(8,128)(2,1)S(1)} %get-tuple-element.60.refs_13_), channel_id=1, source_target_pairs={{0,6},{1,7},{2,0},{3,1},{4,2},{5,3},{6,4},{7,5},{8,14},{9,15},{10,... | collective-permute-start | bytes 491528 | tf_op jit(solution)/shard_map/ppermute | solution.py:528
  51.0 0.0 collective-permute-start.8
  51.0 1.3 %collective-permute-start.9 = (bf16[128,640]{1,0:T(8,128)(2,1)S(1)}, bf16[128,640]{1,0:T(8,128)(2,1)S(1)}, u32[]{:S(2)}, u32[]{:S(2)}) collective-permute-start(bf16[128,640]{1,0:T(8,128)(2,1)S(1)} %get-tuple-element.59.refs_12_), channel_id=1, source_target_pairs={{0,4},{1,5},{2,6},{3,7},{4,0},{5,1},{6,2},{7,3},{8,12},{9,13},{10,... | collective-permute-start | bytes 491528 | tf_op jit(solution)/shard_map/ppermute | solution.py:528
  52.2 1.9 %collective-permute-start.11 = (bf16[16,640]{1,0:T(8,128)(2,1)S(1)}, bf16[16,640]{1,0:T(8,128)(2,1)S(1)}, u32[]{:S(2)}, u32[]{:S(2)}) collective-permute-start(bf16[16,640]{1,0:T(8,128)(2,1)S(1)} %get-tuple-element.61.refs_2_), channel_id=1, source_target_pairs={{0,1},{1,0},{2,3},{3,2},{4,5},{5,4},{6,7},{7,6},{8,9},{9,8},{10,11... | collective-permute-start | bytes 61448 | tf_op jit(solution)/shard_map/ppermute | solution.py:528
  54.1 0.8 %collective-permute-done.11.refs_3_ = bf16[16,640]{1,0:T(8,128)(2,1)S(1)} collective-permute-done((bf16[16,640]{1,0:T(8,128)(2,1)S(1)}, bf16[16,640]{1,0:T(8,128)(2,1)S(1)}, u32[]{:S(2)}, u32[]{:S(2)}) %collective-permute-start.11) | collective-permute-done | bytes 20512 | tf_op jit(solution)/shard_map/ppermute | solution.py:528
  55.0 0.0 copy-done.3
  55.0 0.0 copy-done.7
  55.0 4.9 %resp_within.1 = (f32[8,128,640]{2,1,0:T(8,128)S(1)}, f32[8,128,640]{2,1,0:T(8,128)S(1)}, bf16[128,256]{1,0:T(8,128)(2,1)S(1)}, bf16[128,640]{1,0:T(8,128)(2,1)S(1)}) custom-call(s32[6]{0:T(128)S(1)} %stack.19.refs_0_.where_ref, bf16[128,5376]{1,0:T(8,128)(2,1)S(1)} %bitcast.11, bf16[16,640]{1,0:T(8,128)(2,1)S(1)} %get-tuple-element.61.refs_2_, ...), custom_call_target="tpu_custom_call" | custom-call | tf_op jit(solution)/shard_map/resp_within/pallas_call | solution.py:49
  59.9 0.0 collective-permute-done.10.refs_4_
  59.9 0.8 collective-permute-done.8.refs_2_
  60.7 0.0 collective-permute-done.9.refs_3_
  60.7 1.5 %cores.1 = (bf16[4,128,640]{2,1,0:T(8,128)(2,1)S(1)}, bf16[4,128,640]{2,1,0:T(8,128)(2,1)S(1)}) custom-call(s32[6]{0:T(128)S(1)} %stack.19.refs_0_.where_ref, bf16[128,640]{1,0:T(8,128)(2,1)S(1)} %get-tuple-element.57.refs_1_, bf16[128,640]{1,0:T(8,128)(2,1)S(1)} %collective-permute-done.8.refs_2_, bf16[128,640]{1,0:T(8,128)(2,1)S(1)} %collective-permute-done.9.refs_3_, ...), custom_call_target="tpu_custom_call" | custom-call | tf_op jit(solution)/shard_map/cores/pallas_call | solution.py:49
  62.2 1.7 %collective-permute-start.12 = (bf16[4,128,640]{2,1,0:T(8,128)(2,1)S(1)}, bf16[4,128,640]{2,1,0:T(8,128)(2,1)S(1)}, u32[]{:S(2)}, u32[]{:S(2)}) collective-permute-start(bf16[4,128,640]{2,1,0:T(8,128)(2,1)S(1)} %get-tuple-element.65.refs_5_), channel_id=1, source_target_pairs={{0,1},{1,0},{2,3},{3,2},{4,5},{5,4},{6,7},{7,6},{8,9},{9,8},{10,11... | collective-permute-start | bytes 1966088 | tf_op jit(solution)/shard_map/ppermute | solution.py:528
  63.9 0.2 collective-permute-start.13
  64.1 1.1 %collective-permute-start.14 = (bf16[128,640]{1,0:T(8,128)(2,1)S(1)}, bf16[128,640]{1,0:T(8,128)(2,1)S(1)}, u32[]{:S(2)}, u32[]{:S(2)}) collective-permute-start(bf16[128,640]{1,0:T(8,128)(2,1)S(1)} %get-tuple-element.71.refs_1_), channel_id=1, source_target_pairs={{0,4},{1,5},{2,6},{3,7},{4,0},{5,1},{6,2},{7,3},{8,12},{9,13},{10,... | collective-permute-start | bytes 491528 | tf_op jit(solution)/shard_map/ppermute | solution.py:528
  65.1 1.4 %collective-permute-start.15 = (bf16[128,640]{1,0:T(8,128)(2,1)S(1)}, bf16[128,640]{1,0:T(8,128)(2,1)S(1)}, u32[]{:S(2)}, u32[]{:S(2)}) collective-permute-start(bf16[128,640]{1,0:T(8,128)(2,1)S(1)} %get-tuple-element.71.refs_1_), channel_id=1, source_target_pairs={{0,6},{1,7},{2,0},{3,1},{4,2},{5,3},{6,4},{7,5},{8,14},{9,15},{10,... | collective-permute-start | bytes 491528 | tf_op jit(solution)/shard_map/ppermute | solution.py:528
  66.6 1.6 %prompt_own_half.1 = (f32[4,256,640]{2,1,0:T(8,128)S(1)}, f32[256,128]{1,0:T(8,128)S(1)}) custom-call(s32[6]{0:T(128)S(1)} %stack.19.refs_0_.where_ref, f32[8,256,640]{2,1,0:T(8,128)S(1)} %get-tuple-element.54.refs_5_.refs_9_.refs_10_.refs_1_.part_ref, f32[8,256,640]{2,1,0:T(8,128)S(1)} %get-tuple-element.55.refs_6_.refs_10_.refs_11_.refs_2_.gate_ref, ...), custom_call_target="tpu_custom_call" | custom-call | tf_op jit(solution)/shard_map/prompt_own_half/pallas_call | solution.py:49
  68.1 0.0 collective-permute-done.12.held_ref
  68.1 4.0 %prompt_finish.1 = (bf16[256,5120]{1,0:T(8,128)(2,1)}, f32[8,128]{1,0:T(8,128)S(1)}) custom-call(s32[6]{0:T(128)S(1)} %stack.19.refs_0_.where_ref, f32[8,256,640]{2,1,0:T(8,128)S(1)} %get-tuple-element.54.refs_5_.refs_9_.refs_10_.refs_1_.part_ref, f32[8,256,640]{2,1,0:T(8,128)S(1)} %get-tuple-element.55.refs_6_.refs_10_.refs_11_.refs_2_.gate_ref, ...), custom_call_target="tpu_custom_call" | custom-call | tf_op jit(solution)/shard_map/prompt_finish/pallas_call | solution.py:505
  72.1 2.2 %collective-permute-done.13.refs_2_ = bf16[128,640]{1,0:T(8,128)(2,1)S(1)} collective-permute-done((bf16[128,640]{1,0:T(8,128)(2,1)S(1)}, bf16[128,640]{1,0:T(8,128)(2,1)S(1)}, u32[]{:S(2)}, u32[]{:S(2)}) %collective-permute-start.13) | collective-permute-done | bytes 163872 | tf_op jit(solution)/shard_map/ppermute | solution.py:528
  74.3 0.0 collective-permute-done.14.refs_3_
  74.4 0.3 collective-permute-done.15.refs_4_
  74.7 0.6 gather.1.refs_4_
  75.3 1.3 %collective-permute-start.16 = (bf16[4,128,640]{2,1,0:T(8,128)(2,1)S(1)}, bf16[4,128,640]{2,1,0:T(8,128)(2,1)S(1)}, u32[]{:S(2)}, u32[]{:S(2)}) collective-permute-start(bf16[4,128,640]{2,1,0:T(8,128)(2,1)S(1)} %gather.1.refs_4_), channel_id=1, source_target_pairs={{0,1},{1,0},{2,3},{3,2},{4,5},{5,4},{6,7},{7,6},{8,9},{9,8},{10,11... | collective-permute-start | bytes 1966088 | tf_op jit(solution)/shard_map/ppermute | solution.py:528
  76.5 1.0 %resp_own_half.1 = (f32[4,128,640]{2,1,0:T(8,128)S(1)}, f32[128,128]{1,0:T(8,128)S(1)}) custom-call(s32[6]{0:T(128)S(1)} %stack.19.refs_0_.where_ref, f32[8,128,640]{2,1,0:T(8,128)S(1)} %get-tuple-element.63.refs_8_.refs_6_.refs_1_.part_ref, f32[8,128,640]{2,1,0:T(8,128)S(1)} %get-tuple-element.64.refs_9_.refs_7_.refs_2_.gate_ref, ...), custom_call_target="tpu_custom_call" | custom-call | tf_op jit(solution)/shard_map/resp_own_half/pallas_call | solution.py:49
  77.6 0.7 collective-permute-done.16.held_ref
  78.3 2.5 %resp_finish.1 = (bf16[128,5120]{1,0:T(8,128)(2,1)}, f32[8,128]{1,0:T(8,128)}) custom-call(s32[6]{0:T(128)S(1)} %stack.19.refs_0_.where_ref, f32[8,128,640]{2,1,0:T(8,128)S(1)} %get-tuple-element.63.refs_8_.refs_6_.refs_1_.part_ref, f32[8,128,640]{2,1,0:T(8,128)S(1)} %get-tuple-element.64.refs_9_.refs_7_.refs_2_.gate_ref, ...), custom_call_target="tpu_custom_call" | custom-call | tf_op jit(solution)/shard_map/resp_finish/pallas_call | solution.py:505
  (5 shorter events, 0.0 us)
Async XLA Ops:
  0.6 15.6 %copy-start = (bf16[256,5376]{1,0:T(8,128)(2,1)S(1)}, bf16[256,5376]{1,0:T(8,128)(2,1)}, u32[]{:S(2)}) copy-start(bf16[256,5376]{1,0:T(8,128)(2,1)} %refs_1_.5) | copy-start | bytes 8257540
  0.6 15.6 %copy-start.4 = (f32[4,5376]{1,0:T(4,128)S(1)}, f32[4,5376]{1,0:T(4,128)}, u32[]{:S(2)}) copy-start(f32[4,5376]{1,0:T(4,128)} %refs_4_.1) | copy-start | bytes 258052
  1.7 9.1 %collective-permute-start = (bf16[8,5376]{1,0:T(8,128)(2,1)S(1)}, bf16[8,5376]{1,0:T(8,128)(2,1)S(1)}, u32[]{:S(2)}, u32[]{:S(2)}) collective-permute-start(bf16[8,5376]{1,0:T(8,128)(2,1)S(1)} %slice.3.refs_5_.refs_4_), channel_id=1, source_target_pairs={{0,1},{1,2},{2,3},{3,4},{4,5},{5,6},{6,7},{7,8},{8,9},{9,10},{10,1... | collective-permute-start | bytes 258056 | tf_op jit(solution)/shard_map/ppermute | solution.py:618
  7.7 0.7 copy-start.8
  16.2 4.0 %collective-permute-start.1 = (bf16[4,144,640]{2,1,0:T(8,128)(2,1)S(1)}, bf16[4,144,640]{2,1,0:T(8,128)(2,1)S(1)}, u32[]{:S(2)}, u32[]{:S(2)}) collective-permute-start(bf16[4,144,640]{2,1,0:T(8,128)(2,1)S(1)} %get-tuple-element.43.refs_8_), channel_id=1, source_target_pairs={{0,1},{1,0},{2,3},{3,2},{4,5},{5,4},{6,7},{7,6},{8,9},{9,8},{10,11... | collective-permute-start | bytes 2211848 | tf_op jit(solution)/shard_map/ppermute | solution.py:528
  16.3 9.4 %copy-start.1 = (bf16[256,5120]{1,0:T(8,128)(2,1)S(1)}, bf16[256,5120]{1,0:T(8,128)(2,1)}, u32[]{:S(2)}) copy-start(bf16[256,5120]{1,0:T(8,128)(2,1)} %refs_3_.1) | copy-start | bytes 7864324
  21.1 9.8 %collective-permute-start.2 = (bf16[144,640]{1,0:T(8,128)(2,1)S(1)}, bf16[144,640]{1,0:T(8,128)(2,1)S(1)}, u32[]{:S(2)}, u32[]{:S(2)}) collective-permute-start(bf16[144,640]{1,0:T(8,128)(2,1)S(1)} %get-tuple-element.51.refs_10_), channel_id=1, source_target_pairs={{0,2},{1,3},{2,4},{3,5},{4,6},{5,7},{6,0},{7,1},{8,10},{9,11},{10,... | collective-permute-start | bytes 552968 | tf_op jit(solution)/shard_map/ppermute | solution.py:528
  22.4 10.7 %collective-permute-start.3 = (bf16[144,640]{1,0:T(8,128)(2,1)S(1)}, bf16[144,640]{1,0:T(8,128)(2,1)S(1)}, u32[]{:S(2)}, u32[]{:S(2)}) collective-permute-start(bf16[144,640]{1,0:T(8,128)(2,1)S(1)} %get-tuple-element.52.refs_11_), channel_id=1, source_target_pairs={{0,4},{1,5},{2,6},{3,7},{4,0},{5,1},{6,2},{7,3},{8,12},{9,13},{10,... | collective-permute-start | bytes 552968 | tf_op jit(solution)/shard_map/ppermute | solution.py:528
  24.8 8.2 %collective-permute-start.4 = (bf16[144,640]{1,0:T(8,128)(2,1)S(1)}, bf16[144,640]{1,0:T(8,128)(2,1)S(1)}, u32[]{:S(2)}, u32[]{:S(2)}) collective-permute-start(bf16[144,640]{1,0:T(8,128)(2,1)S(1)} %get-tuple-element.53.refs_12_), channel_id=1, source_target_pairs={{0,6},{1,7},{2,0},{3,1},{4,2},{5,3},{6,4},{7,5},{8,14},{9,15},{10,... | collective-permute-start | bytes 552968 | tf_op jit(solution)/shard_map/ppermute | solution.py:528
  33.9 21.1 %copy-start.2 = (bf16[1,128,5376]{2,1,0:T(8,128)(2,1)S(1)}, bf16[1,128,5376]{2,1,0:T(8,128)(2,1)}, u32[]{:S(2)}) copy-start(bf16[1,128,5376]{2,1,0:T(8,128)(2,1)} %param.17) | copy-start | bytes 4128772
  33.9 21.1 %copy-start.3 = (bf16[1,128,5120]{2,1,0:T(8,128)(2,1)S(1)}, bf16[1,128,5120]{2,1,0:T(8,128)(2,1)}, u32[]{:S(2)}) copy-start(bf16[1,128,5120]{2,1,0:T(8,128)(2,1)} %param.18) | copy-start | bytes 3932164
  33.9 21.1 %copy-start.6 = (f32[80,1,128]{2,1,0:T(1,128)S(1)}, f32[80,1,128]{2,1,0:T(1,128)}, u32[]{:S(2)}) copy-start(f32[80,1,128]{2,1,0:T(1,128)} %param.20) | copy-start | bytes 122884
  33.9 21.1 %copy-start.7 = (f32[80,1,128]{2,1,0:T(1,128)S(1)}, f32[80,1,128]{2,1,0:T(1,128)}, u32[]{:S(2)}) copy-start(f32[80,1,128]{2,1,0:T(1,128)} %param.19) | copy-start | bytes 122884
  33.9 6.1 %collective-permute-start.5 = (bf16[144,640]{1,0:T(8,128)(2,1)S(1)}, bf16[144,640]{1,0:T(8,128)(2,1)S(1)}, u32[]{:S(2)}, u32[]{:S(2)}) collective-permute-start(bf16[144,640]{1,0:T(8,128)(2,1)S(1)} %row.1.refs_5_), channel_id=1, source_target_pairs={{0,8},{1,9},{2,10},{3,11},{4,12},{5,13},{6,14},{7,15},{8,16},{9,17... | collective-permute-start | bytes 552968 | tf_op jit(solution)/shard_map/ppermute | solution.py:528
  35.3 9.8 %collective-permute-start.6 = (bf16[144,640]{1,0:T(8,128)(2,1)S(1)}, bf16[144,640]{1,0:T(8,128)(2,1)S(1)}, u32[]{:S(2)}, u32[]{:S(2)}) collective-permute-start(bf16[144,640]{1,0:T(8,128)(2,1)S(1)} %row.1.refs_5_), channel_id=1, source_target_pairs={{0,16},{1,17},{2,18},{3,19},{4,20},{5,21},{6,22},{7,23},{8,24},{9,... | collective-permute-start | bytes 552968 | tf_op jit(solution)/shard_map/ppermute | solution.py:528
  37.8 7.3 %collective-permute-start.7 = (bf16[144,640]{1,0:T(8,128)(2,1)S(1)}, bf16[144,640]{1,0:T(8,128)(2,1)S(1)}, u32[]{:S(2)}, u32[]{:S(2)}) collective-permute-start(bf16[144,640]{1,0:T(8,128)(2,1)S(1)} %row.1.refs_5_), channel_id=1, source_target_pairs={{0,24},{1,25},{2,26},{3,27},{4,28},{5,29},{6,30},{7,31},{8,0},{9,1... | collective-permute-start | bytes 552968 | tf_op jit(solution)/shard_map/ppermute | solution.py:528
  46.8 13.1 %collective-permute-start.10 = (bf16[128,640]{1,0:T(8,128)(2,1)S(1)}, bf16[128,640]{1,0:T(8,128)(2,1)S(1)}, u32[]{:S(2)}, u32[]{:S(2)}) collective-permute-start(bf16[128,640]{1,0:T(8,128)(2,1)S(1)} %get-tuple-element.60.refs_13_), channel_id=1, source_target_pairs={{0,6},{1,7},{2,0},{3,1},{4,2},{5,3},{6,4},{7,5},{8,14},{9,15},{10,... | collective-permute-start | bytes 491528 | tf_op jit(solution)/shard_map/ppermute | solution.py:528
  51.0 9.7 %collective-permute-start.8 = (bf16[128,640]{1,0:T(8,128)(2,1)S(1)}, bf16[128,640]{1,0:T(8,128)(2,1)S(1)}, u32[]{:S(2)}, u32[]{:S(2)}) collective-permute-start(bf16[128,640]{1,0:T(8,128)(2,1)S(1)} %get-tuple-element.58.refs_11_), channel_id=1, source_target_pairs={{0,2},{1,3},{2,4},{3,5},{4,6},{5,7},{6,0},{7,1},{8,10},{9,11},{10,... | collective-permute-start | bytes 491528 | tf_op jit(solution)/shard_map/ppermute | solution.py:528
  51.0 9.7 %collective-permute-start.9 = (bf16[128,640]{1,0:T(8,128)(2,1)S(1)}, bf16[128,640]{1,0:T(8,128)(2,1)S(1)}, u32[]{:S(2)}, u32[]{:S(2)}) collective-permute-start(bf16[128,640]{1,0:T(8,128)(2,1)S(1)} %get-tuple-element.59.refs_12_), channel_id=1, source_target_pairs={{0,4},{1,5},{2,6},{3,7},{4,0},{5,1},{6,2},{7,3},{8,12},{9,13},{10,... | collective-permute-start | bytes 491528 | tf_op jit(solution)/shard_map/ppermute | solution.py:528
  52.2 2.7 %collective-permute-start.11 = (bf16[16,640]{1,0:T(8,128)(2,1)S(1)}, bf16[16,640]{1,0:T(8,128)(2,1)S(1)}, u32[]{:S(2)}, u32[]{:S(2)}) collective-permute-start(bf16[16,640]{1,0:T(8,128)(2,1)S(1)} %get-tuple-element.61.refs_2_), channel_id=1, source_target_pairs={{0,1},{1,0},{2,3},{3,2},{4,5},{5,4},{6,7},{7,6},{8,9},{9,8},{10,11... | collective-permute-start | bytes 61448 | tf_op jit(solution)/shard_map/ppermute | solution.py:528
  62.2 6.0 %collective-permute-start.12 = (bf16[4,128,640]{2,1,0:T(8,128)(2,1)S(1)}, bf16[4,128,640]{2,1,0:T(8,128)(2,1)S(1)}, u32[]{:S(2)}, u32[]{:S(2)}) collective-permute-start(bf16[4,128,640]{2,1,0:T(8,128)(2,1)S(1)} %get-tuple-element.65.refs_5_), channel_id=1, source_target_pairs={{0,1},{1,0},{2,3},{3,2},{4,5},{5,4},{6,7},{7,6},{8,9},{9,8},{10,11... | collective-permute-start | bytes 1966088 | tf_op jit(solution)/shard_map/ppermute | solution.py:528
  63.9 10.5 %collective-permute-start.13 = (bf16[128,640]{1,0:T(8,128)(2,1)S(1)}, bf16[128,640]{1,0:T(8,128)(2,1)S(1)}, u32[]{:S(2)}, u32[]{:S(2)}) collective-permute-start(bf16[128,640]{1,0:T(8,128)(2,1)S(1)} %get-tuple-element.71.refs_1_), channel_id=1, source_target_pairs={{0,2},{1,3},{2,4},{3,5},{4,6},{5,7},{6,0},{7,1},{8,10},{9,11},{10,... | collective-permute-start | bytes 491528 | tf_op jit(solution)/shard_map/ppermute | solution.py:528
  64.1 10.3 %collective-permute-start.14 = (bf16[128,640]{1,0:T(8,128)(2,1)S(1)}, bf16[128,640]{1,0:T(8,128)(2,1)S(1)}, u32[]{:S(2)}, u32[]{:S(2)}) collective-permute-start(bf16[128,640]{1,0:T(8,128)(2,1)S(1)} %get-tuple-element.71.refs_1_), channel_id=1, source_target_pairs={{0,4},{1,5},{2,6},{3,7},{4,0},{5,1},{6,2},{7,3},{8,12},{9,13},{10,... | collective-permute-start | bytes 491528 | tf_op jit(solution)/shard_map/ppermute | solution.py:528
  65.1 9.5 %collective-permute-start.15 = (bf16[128,640]{1,0:T(8,128)(2,1)S(1)}, bf16[128,640]{1,0:T(8,128)(2,1)S(1)}, u32[]{:S(2)}, u32[]{:S(2)}) collective-permute-start(bf16[128,640]{1,0:T(8,128)(2,1)S(1)} %get-tuple-element.71.refs_1_), channel_id=1, source_target_pairs={{0,6},{1,7},{2,0},{3,1},{4,2},{5,3},{6,4},{7,5},{8,14},{9,15},{10,... | collective-permute-start | bytes 491528 | tf_op jit(solution)/shard_map/ppermute | solution.py:528
  66.6 1.6 %copy-start.5 = (f32[5120]{0:T(1024)S(1)}, f32[5120]{0:T(1024)}, u32[]{:S(2)}) copy-start(f32[5120]{0:T(1024)} %param.25) | copy-start | bytes 61444
  75.3 3.0 %collective-permute-start.16 = (bf16[4,128,640]{2,1,0:T(8,128)(2,1)S(1)}, bf16[4,128,640]{2,1,0:T(8,128)(2,1)S(1)}, u32[]{:S(2)}, u32[]{:S(2)}) collective-permute-start(bf16[4,128,640]{2,1,0:T(8,128)(2,1)S(1)} %gather.1.refs_4_), channel_id=1, source_target_pairs={{0,1},{1,0},{2,3},{3,2},{4,5},{5,4},{6,7},{7,6},{8,9},{9,8},{10,11... | collective-permute-start | bytes 1966088 | tf_op jit(solution)/shard_map/ppermute | solution.py:528

commit v3 on v2

--- a/solution.py
+++ b/solution.py
@@ -53,6 +53,7 @@
         out_shape=[jax.ShapeDtypeStruct(shape, dtype) for shape, dtype in shapes],
         scratch_shapes=list(scratch),
         compiler_params=params(),
+        cost_estimate=pl.CostEstimate(flops=1, bytes_accessed=1, transcendentals=0),
         name=name,
     )(where, *(pltpu.with_memory_space_constraint(a, pltpu.HBM) for a in arrays[:outside]), *arrays[outside:], *after)
 
@@ -66,8 +67,9 @@
     return jnp.take_along_axis(table, 2 * pair + lane // HEAD_DIM, axis=1, mode="promise_in_bounds")
 
 
-def lanes(slab, count=SLAB):
-    return pl.ds(pl.multiple_of(slab * SLAB, 128), count)
+def row_of_heads(ref, shift):
+    row = jnp.concatenate([ref[...], jnp.zeros((1, 128 - HEADS), F32)], axis=1)
+    return pltpu.roll(jnp.broadcast_to(row, (8, 128)), shift, 1)
 
 
 def first_part(shape):
@@ -115,7 +117,7 @@
 
 
 def tables_kernel(
-    where_ref, keep_from, step_from, skip_ref, col_ref, rowt_ref, colt_ref, hcol_ref, keep_ref, step_ref, sems
+    where_ref, keep_from, step_from, col_ref, rowt_ref, colt_ref, hcol_ref, keep_ref, step_ref, sems
 ):
     copies = [
         pltpu.make_async_copy(keep_from, keep_ref, sems.at[0]),
@@ -132,7 +134,6 @@
         col_ref[block], rowt, colt_ref[block] = block_table(keep_ref[:, here], step_ref[:, here])
         rowt_ref[block] = rowt
         stack = jnp.where(place == block, rowt[BLOCK - 1 : BLOCK], stack)
-    stack = jnp.where(place == 3, jnp.concatenate([skip_ref[...], jnp.zeros((1, 128 - HEADS), F32)], axis=1), stack)
     for pair in range(HEADS // 2):
         at = (pair % PAIRS) * 128
         hcol_ref[pair // PAIRS, :, at : at + 128] = spread(stack, pair)
@@ -195,11 +196,11 @@
     kq_ref[:, 0:STATE] = key
     kq_ref[:, STATE : 2 * STATE] = conv(slice(D_INNER + STATE, D_INNER + 2 * STATE))
     keyt_ref[...] = key.astype(F32).T.astype(BF16)
-    for copy in copies[2:]:
-        copy.wait()
 
     def body(at, carry):
         slab = half * 4 + at
+        cols = pl.ds(pl.multiple_of(slab * SLAB, 128), SLAB)
+        pltpu.make_async_copy(x_from.at[:, cols], x_ref.at[:, cols], sems.at[2 + at]).wait()
 
         def put(state):
             msg_ref[at, 0:STATE] = state.astype(BF16)
@@ -251,7 +252,7 @@
 
 
 def prompt_within_kernel(
-    where_ref, sent_acts, kept_acts, z_ref, kq_ref, sent_high, kept_high, col_ref, rowt_ref, hcol_ref,
+    where_ref, sent_acts, kept_acts, z_ref, kq_ref, sent_high, kept_high, col_ref, rowt_ref, hcol_ref, skip_ref,
     part_ref, gate_ref, scores_ref,
 ):
     for block in range(2):
@@ -261,13 +262,14 @@
         slab = half * 4 + at
         shift = lax.rem(128 - SLAB_HEADS * slab, 128)
         rowts = [pltpu.roll(rowt_ref[block], shift, 1) for block in range(2)]
+        skips = row_of_heads(skip_ref, shift)
         earlier = jnp.dot(kq_ref[BLOCK : 2 * BLOCK, STATE:], high_ref[at], preferred_element_type=F32)
         for pair in range(PAIRS):
             cols = slice(pair * 128, pair * 128 + 128)
             gate_cols = pl.ds(pl.multiple_of(slab * SLAB + pair * 128, 128), 128)
             first_half = hcol_ref[slab, 0:1, cols]
             second_half = hcol_ref[slab, 1:2, cols]
-            skip = hcol_ref[slab, 3:4, cols]
+            skip = spread(skips, pair)[0:1]
             head = slab * SLAB_HEADS + 2 * pair
             for block in range(2):
                 here = slice(block * BLOCK, (block + 1) * BLOCK)
@@ -290,11 +292,10 @@
 
 
 def resp_within_kernel(
-    where_ref, x_ref, mine_ref, other_ref, w_ref, b_ref, z_ref, keep_ref, step_ref, hcol_ref, final_ref,
-    part_ref, gate_ref, kq_ref, passed_ref, hist_ref, scores_ref, col_ref, rowt_ref,
+    where_ref, x_ref, mine_ref, other_ref, w_ref, b_ref, z_ref, keep_ref, step_ref, skip_ref,
+    part_ref, gate_ref, kq_ref, hist_ref, scores_ref, col_ref, rowt_ref,
 ):
     core = where_ref[2]
-    passed_ref[...] = final_ref[...]
     for half in range(2):
         flag = (core == half).astype(F32)
         tail = mine_ref[...].astype(F32) * flag + other_ref[...].astype(F32) * (1.0 - flag)
@@ -317,7 +318,9 @@
     scores_ref[...] = masked_scores(kq_ref[...])
 
     def step(slab, carry):
-        rowt = pltpu.roll(rowt_ref[...], lax.rem(128 - SLAB_HEADS * slab, 128), 1)
+        shift = lax.rem(128 - SLAB_HEADS * slab, 128)
+        rowt = pltpu.roll(rowt_ref[...], shift, 1)
+        skips = row_of_heads(skip_ref, shift)
         for pair in range(PAIRS):
             cols = slice(pair * 128, pair * 128 + 128)
             wide_cols = pl.ds(pl.multiple_of(slab * SLAB + pair * 128, 128), 128)
@@ -328,7 +331,7 @@
             gate = silu(z_ref[:, wide_cols].astype(F32))
             row = spread(rowt, pair)
             half = row[BLOCK - 1 : BLOCK]
-            part_ref[slab, :, cols] = (row * mixed + hcol_ref[slab, 3:4, cols] * values.astype(F32)) * gate
+            part_ref[slab, :, cols] = (row * mixed + spread(skips, pair)[0:1] * values.astype(F32)) * gate
             gate_ref[slab, :, cols] = row * half * gate
         return carry
 
@@ -389,16 +392,60 @@
     return sum(ref[STATE:].astype(F32) * (place == SIDE - 1).astype(F32) for place, ref in zip(places, refs))
 
 
-def row_kernel(where_ref, r0, r1, r2, r3, out_ref):
+def direction(state_ref):
+    total = jnp.zeros((STATE, 128), F32)
+    for cols in CHUNKS:
+        state = state_ref[:, cols]
+        total = total + state * jnp.sum(state, axis=0, keepdims=True)
+    along = jnp.sum(total, axis=1, keepdims=True)
+    along = along * (1.0 / (jnp.max(jnp.abs(along)) + 1e-30))
+    along = jnp.broadcast_to(along.astype(BF16).astype(F32), (STATE, 128))
+    return along, jnp.sum(along * along, axis=0, keepdims=True) + 1e-30
+
+
+def split_off(state_ref, along, square, out_ref):
+    highs, lows = [], []
+    for cols in CHUNKS:
+        state = state_ref[:, cols]
+        factor = jnp.sum(state * along, axis=0, keepdims=True) / square
+        high = factor.astype(BF16).astype(F32)
+        low = (factor - high).astype(BF16).astype(F32)
+        out_ref[0:STATE, cols] = (state - along * (high + low)).astype(BF16)
+        highs.append(high)
+        lows.append(low)
+    return highs, lows
+
+
+def as_columns(row):
+    return jnp.broadcast_to(row, (STATE, 128)).T
+
+
+def joined(ref, along, factor, cols):
+    return ref[0:STATE, cols].astype(F32) + along * factor[:, cols]
+
+
+def row_kernel(where_ref, r2, r0, r1, r3, out_ref, state_ref):
     refs = (r0, r1, r2, r3)
     places = [at_shift(where_ref[0], -i) for i in range(SIDE)]
     weights, through = weights_to(places, [decay_of(ref[STATE:]) for ref in refs], SIDE)
     for cols in CHUNKS:
-        out_ref[0:STATE, cols] = weighted_sum(weights, refs, cols).astype(BF16)
-    out_ref[STATE:] = extra_rows(through, last_tail(places, refs))
-
-
-def entering_kernel(where_ref, r0, r1, r2, r3, t0, t1, t2, t3, e0, e1, e2, e3, final_ref, tail_ref):
+        state_ref[:, cols] = weighted_sum(weights, refs, cols)
+    along, square = direction(state_ref)
+    highs, lows = split_off(state_ref, along, square, out_ref)
+    tail = last_tail(places, refs)
+    blank = jnp.zeros((1, 128), F32)
+    lines = [
+        jnp.concatenate([blank] + highs[:4], axis=1),
+        jnp.concatenate([blank] + lows[:4], axis=1),
+        jnp.concatenate([blank, highs[4], lows[4], along.T[0:1], blank], axis=1),
+    ]
+    place = lax.broadcasted_iota(jnp.int32, tail.shape, 0)
+    for row, line in enumerate(lines):
+        tail = tail + jnp.where(place == PIECES * (row + 1), line, 0.0)
+    out_ref[STATE:] = extra_rows(through, tail)
+
+
+def entering_kernel(where_ref, t2, t0, t1, t3, r2, r0, r1, r3, e0, e1, e2, e3, final_ref, tail_ref, state_ref):
     x, y = where_ref[0], where_ref[1]
     refs, totals, outs = (r0, r1, r2, r3), (t0, t1, t2, t3), (e0, e1, e2, e3)
     rows = [at_shift(y, -i) for i in range(SIDE)]
@@ -408,34 +455,61 @@
     places = [at_shift(x, -i) for i in range(SIDE)]
     decays = [decay_of(ref[STATE:]) for ref in refs]
     to_chips = [weights_to(places, decays, at_shift(x, shift)) for shift in range(SIDE)]
+    coded = []
+    for ref in totals:
+        wide = ref[STATE:].astype(F32)
+        high = jnp.concatenate([wide[PIECES : PIECES + 1, 128:], wide[3 * PIECES : 3 * PIECES + 1, 128:256]], axis=1)
+        low = jnp.concatenate(
+            [wide[2 * PIECES : 2 * PIECES + 1, 128:], wide[3 * PIECES : 3 * PIECES + 1, 256:384]], axis=1
+        )
+        coded.append((as_columns(wide[3 * PIECES : 3 * PIECES + 1, 384:512]), high + low))
     for cols in CHUNKS:
-        final_ref[:, cols] = weighted_sum(to_end, totals, cols).astype(BF16)
-        row_in = weighted_sum(to_row, totals, cols)
-        for out, (weights, through) in zip(outs, to_chips):
-            out[:, cols] = (through[:, cols] * row_in + weighted_sum(weights, refs, cols)).astype(BF16)
+        states = [joined(ref, along, factor, cols) for ref, (along, factor) in zip(totals, coded)]
+        state_ref[SIDE, :, cols] = sum(w[:, cols] * state for w, state in zip(to_end, states))
+        row_in = sum(w[:, cols] * state for w, state in zip(to_row, states))
+        for shift, (weights, through) in enumerate(to_chips):
+            state_ref[shift, :, cols] = through[:, cols] * row_in + weighted_sum(weights, refs, cols)
+    along, square = direction(state_ref.at[SIDE])
+    line = jnp.concatenate([along.T[0:1], jnp.zeros((1, SLAB - 128), F32)], axis=1)
+    place = lax.broadcasted_iota(jnp.int32, (EXTRA, SLAB), 0)
+    for at, out in enumerate(outs + (final_ref,)):
+        highs, lows = split_off(state_ref.at[at], along, square, out)
+        block = jnp.where(place == 0, jnp.concatenate(highs, axis=1), jnp.where(place == 1, jnp.concatenate(lows, axis=1), 0.0))
+        out[STATE:] = jnp.where(place == 2, line, block).astype(BF16)
     tail_ref[...] = last_tail(rows, totals).astype(BF16)
 
 
-def cores_kernel(where_ref, g0, g1, g2, g3, own_ref, recv_ref, hcol_ref, mine_ref, send_ref):
+def put_pair(ref, slab, cols, state):
+    high = state.astype(BF16)
+    ref[slab, 0:STATE, cols] = high
+    ref[slab, STATE:, cols] = (state - high.astype(F32)).astype(BF16)
+
+
+def uncoded(ref):
+    wide = ref[STATE:].astype(F32)
+    return as_columns(wide[2:3, 0:128]), wide[0:1] + wide[1:2]
+
+
+def cores_kernel(
+    where_ref, g2, g0, g1, g3, f2, f0, f1, f3, own_ref, recv_ref, hcol_ref, mine_ref, send_ref, final_ref
+):
     x, core = where_ref[0], where_ref[2]
     first = (core == 0).astype(F32)
     last = 1.0 - first
-    for i, ref in enumerate((g0, g1, g2, g3)):
+    for i, (ref, passed_ref) in enumerate(zip((g0, g1, g2, g3), (f0, f1, f2, f3))):
         slab = at_shift(x, -i)
         half = hcol_ref[core * 4 + slab]
         mine = (half[0:1] * half[1:2]) ** 2
         decay = mine * first + decay_of(recv_ref[slab, STATE:, :]) * last
+        along, factor = uncoded(ref)
+        final_along, final_factor = uncoded(passed_ref)
         for cols in CHUNKS:
+            put_pair(final_ref, slab, cols, joined(passed_ref, final_along, final_factor, cols))
             earlier = own_ref[slab, :, cols] * first + recv_ref[slab, 0:STATE, cols].astype(F32) * last
-            start = ref[:, cols].astype(F32)
+            start = joined(ref, along, factor, cols)
             later = decay[:, cols] * start + earlier
-            mine_ref[slab, :, cols] = (start * first + later * last).astype(BF16)
-            send_ref[slab, :, cols] = (later * first + start * last).astype(BF16)
-
-
-def gather_kernel(where_ref, f0, f1, f2, f3, out_ref):
-    for i, ref in enumerate((f0, f1, f2, f3)):
-        out_ref[at_shift(where_ref[0], -i)] = ref[...]
+            put_pair(mine_ref, slab, cols, start * first + later * last)
+            put_pair(send_ref, slab, cols, later * first + start * last)
 
 
 TILE = 64
@@ -443,8 +517,9 @@
 
 def half_gated(query, held_ref, half, here, part_ref, gate_ref, put):
     squares = jnp.zeros((TILE, 128), F32)
+    twice = jnp.concatenate([query, query], axis=1)
     for s in range(4):
-        carried = jnp.dot(query, held_ref[s], preferred_element_type=F32)
+        carried = jnp.dot(twice, held_ref[s], preferred_element_type=F32)
         for cols in CHUNKS:
             gated = part_ref[half * 4 + s, here, cols] + gate_ref[half * 4 + s, here, cols] * carried[:, cols]
             put(s, cols, gated)
@@ -474,44 +549,61 @@
 
 def finish_kernel(
     length_at, where_ref, part_ref, gate_ref, kq_ref, held_ref, own_ref, squares_ref, gain_ref,
-    out_ref, token_ref, gated_ref,
+    out_ref, token_ref, gated_ref, rows_ref, sems,
 ):
     core = where_ref[2]
-    start = pl.program_id(0) * TILE
-    here = pl.ds(pl.multiple_of(start, TILE), TILE)
-
-    def put(s, cols, gated):
-        gated_ref[s, :, cols] = gated
-
-    squares = half_gated(kq_ref[here, STATE:], held_ref, 1 - core, here, part_ref, gate_ref, put)
-    squares = squares + squares_ref[here, :]
-    mean = jnp.sum(squares, axis=1, keepdims=True) * (1.0 / D_INNER)
-    row = lax.broadcasted_iota(jnp.int32, (TILE, 1), 0) + start
-    inv = jnp.where(row < where_ref[length_at], lax.rsqrt(mean + EPS), 0.0)
-    inv = jnp.broadcast_to(inv, (TILE, 128))
-    for s in range(4):
-        for half, value_of in (
-            (core, lambda cols: own_ref[s, here, cols]),
-            (1 - core, lambda cols: gated_ref[s, :, cols]),
-        ):
-            for cols in CHUNKS:
-                wide = pl.ds(pl.multiple_of((half * 4 + s) * SLAB + cols.start, 128), 128)
-                out_ref[:, wide] = (value_of(cols) * inv * gain_ref[:, wide]).astype(BF16)
+
+    def copy_out(at):
+        here = pl.ds(pl.multiple_of(at * TILE, TILE), TILE)
+        return pltpu.make_async_copy(rows_ref.at[here], out_ref.at[here], sems.at[at])
+
+    def body(at, carry):
+        start = at * TILE
+        here = pl.ds(pl.multiple_of(start, TILE), TILE)
+
+        def put(s, cols, gated):
+            gated_ref[s, :, cols] = gated
+
+        squares = half_gated(kq_ref[here, STATE:], held_ref, 1 - core, here, part_ref, gate_ref, put)
+        squares = squares + squares_ref[here, :]
+        mean = jnp.sum(squares, axis=1, keepdims=True) * (1.0 / D_INNER)
+        row = lax.broadcasted_iota(jnp.int32, (TILE, 1), 0) + start
+        inv = jnp.where(row < where_ref[length_at], lax.rsqrt(mean + EPS), 0.0)
+        inv = jnp.broadcast_to(inv, (TILE, 128))
+        for s in range(4):
+            for half, value_of in (
+                (core, lambda cols: own_ref[s, here, cols]),
+                (1 - core, lambda cols: gated_ref[s, :, cols]),
+            ):
+                for cols in CHUNKS:
+                    wide = pl.ds(pl.multiple_of((half * 4 + s) * SLAB + cols.start, 128), 128)
+                    rows_ref[here, wide] = (value_of(cols) * inv * gain_ref[:, wide]).astype(BF16)
+        copy_out(at).start()
+        return carry
+
+    tiles = part_ref.shape[1] // TILE
+    lax.fori_loop(0, tiles, body, 0)
     token_ref[...] = jnp.zeros_like(token_ref)
-
-
-def finish(where, part, gate, kq, held, own, squares, gain, length_at, name):
+    for at in range(tiles):
+        copy_out(at).wait()
+
+
+def finish(where, part, gate, kq, held, own, squares, gain, length_at, name, after):
     rows = part.shape[1]
     return pl.pallas_call(
-        functools.partial(finish_kernel, length_at),
-        grid=(rows // TILE,),
-        in_specs=[SMEM] + [VMEM] * 7,
-        out_specs=[pl.BlockSpec((TILE, D_INNER), lambda i: (i, 0)), pl.BlockSpec((8, 128), lambda i: (0, 0))],
-        scratch_shapes=[pltpu.VMEM((4, TILE, SLAB), F32)],
+        ordered(functools.partial(finish_kernel, length_at), 8, len(after)),
+        in_specs=[SMEM] + [VMEM] * (7 + len(after)),
+        out_specs=[HBM, VMEM],
+        scratch_shapes=[
+            pltpu.VMEM((4, TILE, SLAB), F32),
+            pltpu.VMEM((rows, D_INNER), BF16),
+            pltpu.SemaphoreType.DMA((rows // TILE,)),
+        ],
         out_shape=[jax.ShapeDtypeStruct((rows, D_INNER), BF16), jax.ShapeDtypeStruct((8, 128), F32)],
         compiler_params=params(),
+        cost_estimate=pl.CostEstimate(flops=1, bytes_accessed=1, transcendentals=0),
         name=name,
-    )(where, part, gate, kq, held, own, squares, gain)
+    )(where, part, gate, kq, held, own, squares, gain, *after)
 
 
 def number(y, x, core):
@@ -536,14 +628,19 @@
     return moved(value, lambda y, x, core: (y, x + by, core))
 
 
+def round_x(here, to_next, to_opposite, to_last):
+    opposite = along_x(to_opposite, 2)
+    return opposite, here, along_x(to_next, 1), along_x(to_last, 3)
+
+
 def along_y(value, by):
     return moved(value, lambda y, x, core: (y + by, x, core))
 
 
-def make_tables(where, keep, step, skip):
+def make_tables(where, keep, step):
     shapes = [((2, HEADS, BLOCK), F32), ((2, BLOCK, 128), F32), ((2, BLOCK, 128), F32), ((SLABS, 8, SLAB), F32)]
     scratch = [pltpu.VMEM(keep.shape, F32), pltpu.VMEM(step.shape, F32), pltpu.SemaphoreType.DMA((2,))]
-    return whole(tables_kernel, where, (keep, step, skip[None, :]), shapes, "tables", scratch=scratch, outside=2)
+    return whole(tables_kernel, where, (keep, step), shapes, "tables", scratch=scratch, outside=2)
 
 
 def sent_states(where, xbc, weight, hist, bias, own_rows, colt, hcol):
@@ -572,23 +669,23 @@
     return whole(kept_states_kernel, where, arrays, shapes, "kept_states", after, [pltpu.VMEM((rows, SLAB), BF16)])
 
 
-def prompt_within(where, acts, z, kq, high, col, rowt, hcol, after):
+def prompt_within(where, acts, z, kq, high, col, rowt, hcol, skip, after):
     shapes = [((SLABS, z.shape[0], SLAB), F32)] * 2
     scratch = [pltpu.VMEM((2, BLOCK, BLOCK), F32)]
-    arrays = (*acts, z, kq, *high, col, rowt, hcol)
+    arrays = (*acts, z, kq, *high, col, rowt, hcol, skip)
     return whole(prompt_within_kernel, where, arrays, shapes, "prompt_within", after, scratch)
 
 
-def resp_within(where, xbc, mine, other, weight, bias, z, keep, step, hcol, final, after):
+def resp_within(where, xbc, mine, other, weight, bias, z, keep, step, skip, after):
     rows = z.shape[0]
-    shapes = [((SLABS, rows, SLAB), F32)] * 2 + [((rows, 2 * STATE), BF16), (final.shape, BF16)]
+    shapes = [((SLABS, rows, SLAB), F32)] * 2 + [((rows, 2 * STATE), BF16)]
     scratch = [
         pltpu.VMEM((HIST, D_INNER + 2 * STATE), F32),
         pltpu.VMEM((BLOCK, BLOCK), F32),
         pltpu.VMEM((HEADS, BLOCK), F32),
         pltpu.VMEM((BLOCK, 128), F32),
     ]
-    arrays = (xbc, mine, other, weight, bias, z, keep, step, hcol, final)
+    arrays = (xbc, mine, other, weight, bias, z, keep, step, skip)
     return whole(resp_within_kernel, where, arrays, shapes, "resp_within", after, scratch)
 
 
@@ -611,12 +708,12 @@
     seq, core = lax.axis_index("seq"), lax.axis_index("resp")
     fixed = [seq % SIDE, seq // SIDE, core, jnp.where(lax.axis_index(GROUP) == 0, 0, 1)]
     where = jnp.stack([jnp.asarray(v, jnp.int32) for v in fixed + [rows, resp_len[0]]])
-    bias_row, gain_row = conv_bias[None, :], gain[None, :]
+    bias_row, gain_row, skip_row = conv_bias[None, :], gain[None, :], skip[None, :]
 
     own_rows = prompt_xbc[rows - HIST :]
     count = 2 * SIDE * SIDE
     hist = lax.ppermute(own_rows, GROUP, [(i, i + 1) for i in range(count - 1)])
-    col, rowt, colt, hcol = make_tables(where, prompt_keep, prompt_step, skip)
+    col, rowt, colt, hcol = make_tables(where, prompt_keep, prompt_step)
     sent_acts, kq, keyt, sent_high, msg = sent_states(
         where, prompt_xbc, conv_weight, hist, bias_row, own_rows, colt, hcol
     )
@@ -624,36 +721,47 @@
     kept_acts, kept_high, own = kept_states(
         where, prompt_xbc, conv_weight, hist, bias_row, keyt, colt, hcol, after=(msg,)
     )
-    with_extra, plain = ((STATE + EXTRA, SLAB), BF16), ((STATE, SLAB), BF16)
+    with_extra = ((STATE + EXTRA, SLAB), BF16)
     c0, c1, c2, c3 = whole(chip_kernel, where, (own, recv, hcol, own_rows), [with_extra] * 4, "chip")
-    pieces = (c0, along_x(c1, 1), along_x(c2, 2), along_x(c3, 3))
+    pieces = round_x(c0, c1, c2, c3)
     part, gate = prompt_within(
-        where, (sent_acts, kept_acts), prompt_z, kq, (sent_high, kept_high), col, rowt, hcol, after=(c1, c2, c3)
-    )
-    (total,) = whole(row_kernel, where, pieces, [with_extra], "row", after=(part, gate))
-    totals = (total, along_y(total, 1), along_y(total, 2), along_y(total, 3))
+        where, (sent_acts, kept_acts), prompt_z, kq, (sent_high, kept_high), col, rowt, hcol, skip_row,
+        after=(c1, c2, c3),
+    )
+    (total,) = whole(row_kernel, where, pieces, [with_extra], "row", after=(part, gate), scratch=[pltpu.VMEM((STATE, SLAB), F32)])
+    opposite = along_y(total, 2)
+    totals = (opposite, total, along_y(total, 1), along_y(total, 3))
     e0, e1, e2, e3, final, tail = whole(
-        entering_kernel, where, pieces + totals, [plain] * 5 + [((EXTRA, SLAB), BF16)], "entering", after=(part, gate)
+        entering_kernel, where, totals + pieces, [with_extra] * 5 + [((EXTRA, SLAB), BF16)], "entering", after=(part, gate),
+        scratch=[pltpu.VMEM((SIDE + 1, STATE, SLAB), F32)],
     )
     tail_other = swap_cores(tail)
-    back = (e0, along_x(e1, 1), along_x(e2, 2), along_x(e3, 3))
-    resp_part, resp_gate, resp_kq, final = resp_within(
+    back = round_x(e0, e1, e2, e3)
+    finals = round_x(final, final, final, final)
+    resp_part, resp_gate, resp_kq = resp_within(
         where, resp_xbc[0], tail, tail_other, conv_weight, bias_row, resp_z[0],
-        resp_keep.reshape(HEADS, BLOCK), resp_step.reshape(HEADS, BLOCK), hcol, final, after=(e1, e2, e3),
-    )
-    finals = (final, along_x(final, 1), along_x(final, 2), along_x(final, 3))
-    four = ((4, STATE, SLAB), BF16)
-    mine, send = whole(
-        cores_kernel, where, back + (own, recv, hcol), [four] * 2, "cores", after=(resp_part, resp_gate, part, gate)
-    )
-    other = swap_cores(send)
+        resp_keep.reshape(HEADS, BLOCK), resp_step.reshape(HEADS, BLOCK), skip_row, after=(e1, e2, e3),
+    )
+    four = ((4, 2 * STATE, SLAB), BF16)
+    mine, send, final_mine = whole(
+        cores_kernel,
+        where,
+        back + finals + (own, recv, hcol),
+        [four] * 3,
+        "cores",
+        after=(resp_part, resp_gate, part, gate),
+    )
+    other, final_other = swap_cores(send), swap_cores(final_mine)
     gated, squares = own_half(where, part, gate, kq, mine, "prompt_own_half", after=(send,))
-    prompt_out, token = finish(where, part, gate, kq, other, gated, squares, gain_row, 4, "prompt_finish")
-    (final_mine,) = whole(gather_kernel, where, finals, [four], "gather", after=(token, resp_part, resp_gate))
-    final_other = swap_cores(final_mine)
-    gated, squares = own_half(where, resp_part, resp_gate, resp_kq, final_mine, "resp_own_half")
+    resp_gated, resp_squares = own_half(
+        where, resp_part, resp_gate, resp_kq, final_mine, "resp_own_half", after=(squares,)
+    )
+    prompt_out, token = finish(
+        where, part, gate, kq, other, gated, squares, gain_row, 4, "prompt_finish", after=(resp_squares,)
+    )
     resp_out, _ = finish(
-        where, resp_part, resp_gate, resp_kq, final_other, gated, squares, gain_row, 5, "resp_finish"
+        where, resp_part, resp_gate, resp_kq, final_other, resp_gated, resp_squares, gain_row, 5, "resp_finish",
+        after=(token,),
     )
     return (prompt_out, resp_out[None])
 

time: 81.1 us -> 83.2 us (1.026)
  waiting for transfers between devices: 13.3 us -> 15.3 us
  Pallas kernels: 36.2 us -> 38.1 us
  starting transfers between devices: 27.2 us -> 26 us
    ppermute x16, waiting for transfers between devices: 13.3 us -> 15.2 us  [moved(): return lax.ppermute(value, GROUP, pairs)]
    pallas_call x12 -> x11, Pallas kernels: 29.7 us -> 31.2 us  [whole(): pl.pallas_call(ordered(kernel, 1 + len(arrays), len(after)), in_specs=[SM...]
    ppermute x16, starting transfers between devices: 22.7 us -> 21.5 us  [moved(): return lax.ppermute(value, GROUP, pairs)]
  transfers between devices with their start and end apart: 17 -> 17, of which waited for: 8 -> 6; matrix products, arithmetic and copies ran while one was open for 1% -> 1% of each run, Pallas kernels for 28% -> 28%
where the time goes in v3:
time: 83.2 us; the launch traced here: 82.9 us
  Pallas kernels  38.1 us (46%)
  starting transfers between devices  26 us (31%)
  waiting for transfers between devices  15.3 us (18%)
  local copies, waits for them, and re-layouts  1.79 us (2%)
  between operations  1.71 us (2%)
    pallas_call x11, Pallas kernels, whole(): pl.pallas_call(ordered(kernel, 1 + len(arrays), len(after)), in_specs=[SM...  31.2 us
    ppermute x16, starting transfers between devices, moved(): return lax.ppermute(value, GROUP, pairs)  21.5 us
    ppermute x16, waiting for transfers between devices, moved(): return lax.ppermute(value, GROUP, pairs)  15.2 us
    pallas_call x2, Pallas kernels, finish(): pl.pallas_call(ordered(functools.partial(finish_kernel, length_at), 8, le...  6.97 us
    ppermute x1, starting transfers between devices, shards(): hist = lax.ppermute(own_rows, GROUP, [(i, i + 1) for i in range(count - 1)])  4.5 us
  transfers between devices with their start and end apart: 17, of which 6 were waited for; matrix products, arithmetic and copies ran while one was open for 1% of the time, Pallas kernels for 28%

profile of v3, /device:TPU:1, one launch (start us, length us, event | category | flops | bytes accessed | tf_op | source)
XLA Modules:
  0.0 82.9 jit_solution(11153903526207035663)
XLA Ops:
  0.6 0.9 %slice.3.refs_5_.refs_4_ = bf16[8,5376]{1,0:T(8,128)(2,1)S(1)} slice(bf16[256,5376]{1,0:T(8,128)(2,1)} %refs_1_.5), slice={[248:256], [0:5376]} | slice | bytes 172032 | tf_op jit(solution)/shard_map/slice | solution.py:713
  1.5 4.5 %collective-permute-start = (bf16[8,5376]{1,0:T(8,128)(2,1)S(1)}, bf16[8,5376]{1,0:T(8,128)(2,1)S(1)}, u32[]{:S(2)}, u32[]{:S(2)}) collective-permute-start(bf16[8,5376]{1,0:T(8,128)(2,1)S(1)} %slice.3.refs_5_.refs_4_), channel_id=1, source_target_pairs={{0,1},{1,2},{2,3},{3,4},{4,5},{5,6},{6,7},{7,8},{8,9},{9,10},{10,1... | collective-permute-start | bytes 258056 | tf_op jit(solution)/shard_map/ppermute | solution.py:715
  6.7 0.1 stack.19.refs_0_
  6.8 2.4 %tables.1 = (f32[2,80,128]{2,1,0:T(8,128)S(1)}, f32[2,128,128]{2,1,0:T(8,128)S(1)}, f32[2,128,128]{2,1,0:T(8,128)S(1)}, f32[8,8,640]{2,1,0:T(8,128)S(1)}) custom-call(s32[6]{0:T(128)S(1)} %stack.19.refs_0_, f32[80,256]{1,0:T(8,128)} %refs_1_.3, f32[80,256]{1,0:T(8,128)} %refs_2_.3), custom_call_target="tpu_custom_call" | custom-call | flops 1 | bytes 1 | tf_op jit(solution)/shard_map/tables/pallas_call | solution.py:49
  9.2 0.8 broadcast_in_dim.12.refs_4_.refs_5_
  9.9 0.0 collective-permute-done.refs_3_
  9.9 0.0 copy-start
  9.9 0.0 copy-start.4
  10.0 5.5 %sent_states.1 = (bf16[4,256,640]{2,1,0:T(8,128)(2,1)S(1)}, bf16[256,256]{1,0:T(8,128)(2,1)S(1)}, bf16[128,256]{1,0:T(8,128)(2,1)S(1)}, bf16[4,128,640]{2,1,0:T(8,128)(2,1)S(1)}, bf16[4,144,640]{2,1,0:T(8,128)(2,1)S(1)}) custom-call(s32[6]{0:T(128)S(1)} %stack.19.refs_0_, bf16[256,5376]{1,0:T(8,128)(2,1)} %refs_1_.5, f32[4,5376]{1,0:T(4,128)} %refs_4_.1, ...), custom_call_target="tpu_custom_call" | custom-call | flops 1 | bytes 1 | tf_op jit(solution)/shard_map/sent_states/pallas_call | solution.py:49
  15.4 0.1 collective-permute-start.1
  15.5 0.0 copy-done
  15.5 0.0 copy-done.4
  15.6 3.9 %kept_states.1 = (bf16[4,256,640]{2,1,0:T(8,128)(2,1)S(1)}, bf16[4,128,640]{2,1,0:T(8,128)(2,1)S(1)}, f32[4,128,640]{2,1,0:T(8,128)S(1)}) custom-call(s32[6]{0:T(128)S(1)} %stack.19.refs_0_, bf16[256,5376]{1,0:T(8,128)(2,1)S(1)} %copy-done, f32[4,5376]{1,0:T(4,128)S(1)} %copy-done.4, bf16[8,5376]{1,0:T(8,128)(2,1)S(1)} %collective-permute-done.refs_3_, ...), custom_call_target="tpu_custom_call" | custom-call | flops 1 | bytes 1 | tf_op jit(solution)/shard_map/kept_states/pallas_call | solution.py:49
  19.4 0.0 copy-start.8
  19.5 0.0 collective-permute-done.1.refs_2_.refs_10_
  19.5 0.9 %chip.1 = (bf16[144,640]{1,0:T(8,128)(2,1)S(1)}, bf16[144,640]{1,0:T(8,128)(2,1)S(1)}, bf16[144,640]{1,0:T(8,128)(2,1)S(1)}, bf16[144,640]{1,0:T(8,128)(2,1)S(1)}) custom-call(s32[6]{0:T(128)S(1)} %stack.19.refs_0_, f32[4,128,640]{2,1,0:T(8,128)S(1)} %get-tuple-element.50.refs_1_.refs_9_, bf16[4,144,640]{2,1,0:T(8,128)(2,1)S(1)} %collective-permute-done.1.refs_2_.refs_10_, ...), custom_call_target="tpu_custom_call" | custom-call | flops 1 | bytes 1 | tf_op jit(solution)/shard_map/chip/pallas_call | solution.py:49
  20.4 1.3 %collective-permute-start.3 = (bf16[144,640]{1,0:T(8,128)(2,1)S(1)}, bf16[144,640]{1,0:T(8,128)(2,1)S(1)}, u32[]{:S(2)}, u32[]{:S(2)}) collective-permute-start(bf16[144,640]{1,0:T(8,128)(2,1)S(1)} %get-tuple-element.51.refs_11_), channel_id=1, source_target_pairs={{0,2},{1,3},{2,4},{3,5},{4,6},{5,7},{6,0},{7,1},{8,10},{9,11},{10,... | collective-permute-start | bytes 552968 | tf_op jit(solution)/shard_map/ppermute | solution.py:620
  21.7 2.4 %collective-permute-start.2 = (bf16[144,640]{1,0:T(8,128)(2,1)S(1)}, bf16[144,640]{1,0:T(8,128)(2,1)S(1)}, u32[]{:S(2)}, u32[]{:S(2)}) collective-permute-start(bf16[144,640]{1,0:T(8,128)(2,1)S(1)} %get-tuple-element.52.refs_12_), channel_id=1, source_target_pairs={{0,4},{1,5},{2,6},{3,7},{4,0},{5,1},{6,2},{7,3},{8,12},{9,13},{10,... | collective-permute-start | bytes 552968 | tf_op jit(solution)/shard_map/ppermute | solution.py:620
  24.1 0.9 %collective-permute-start.4 = (bf16[144,640]{1,0:T(8,128)(2,1)S(1)}, bf16[144,640]{1,0:T(8,128)(2,1)S(1)}, u32[]{:S(2)}, u32[]{:S(2)}) collective-permute-start(bf16[144,640]{1,0:T(8,128)(2,1)S(1)} %get-tuple-element.53.refs_13_), channel_id=1, source_target_pairs={{0,6},{1,7},{2,0},{3,1},{4,2},{5,3},{6,4},{7,5},{8,14},{9,15},{10,... | collective-permute-start | bytes 552968 | tf_op jit(solution)/shard_map/ppermute | solution.py:620
  25.0 0.0 copy-done.1
  25.0 0.0 copy-done.8
  25.0 5.2 %prompt_within.1 = (f32[8,256,640]{2,1,0:T(8,128)S(1)}, f32[8,256,640]{2,1,0:T(8,128)S(1)}) custom-call(s32[6]{0:T(128)S(1)} %stack.19.refs_0_, bf16[4,256,640]{2,1,0:T(8,128)(2,1)S(1)} %get-tuple-element.41.refs_1_, bf16[4,256,640]{2,1,0:T(8,128)(2,1)S(1)} %get-tuple-element.44.refs_2_, bf16[256,5120]{1,0:T(8,128)(2,1)S(1)} %copy-done.1, ...), custom_call_target="tpu_custom_call" | custom-call | flops 1 | bytes 1 | tf_op jit(solution)/shard_map/prompt_within/pallas_call | solution.py:49
  30.2 0.0 collective-permute-done.3.refs_3_.refs_7_
  30.2 2.1 %collective-permute-done.2.refs_1_.refs_5_ = bf16[144,640]{1,0:T(8,128)(2,1)S(1)} collective-permute-done((bf16[144,640]{1,0:T(8,128)(2,1)S(1)}, bf16[144,640]{1,0:T(8,128)(2,1)S(1)}, u32[]{:S(2)}, u32[]{:S(2)}) %collective-permute-start.2) | collective-permute-done | bytes 184352 | tf_op jit(solution)/shard_map/ppermute | solution.py:620
  32.3 0.0 collective-permute-done.4.refs_4_.refs_8_
  32.3 1.1 %row.1.refs_2_ = bf16[144,640]{1,0:T(8,128)(2,1)S(1)} custom-call(s32[6]{0:T(128)S(1)} %stack.19.refs_0_, bf16[144,640]{1,0:T(8,128)(2,1)S(1)} %collective-permute-done.2.refs_1_.refs_5_, bf16[144,640]{1,0:T(8,128)(2,1)S(1)} %get-tuple-element.56.refs_2_.refs_6_, bf16[144,640]{1,0:T(8,128)(2,1)S(1)} %collective-permute-done.3.refs_3_.refs_7_, ...), custom_call_target="tpu_custom_call" | custom-call | flops 1 | bytes 1 | tf_op jit(solution)/shard_map/row/pallas_call | solution.py:49
  33.4 0.0 copy-start.2
  33.4 0.0 copy-start.3
  33.4 0.0 copy-start.6
  33.5 0.0 copy-start.7
  33.5 3.5 %collective-permute-start.7 = (bf16[144,640]{1,0:T(8,128)(2,1)S(1)}, bf16[144,640]{1,0:T(8,128)(2,1)S(1)}, u32[]{:S(2)}, u32[]{:S(2)}) collective-permute-start(bf16[144,640]{1,0:T(8,128)(2,1)S(1)} %row.1.refs_2_), channel_id=1, source_target_pairs={{0,24},{1,25},{2,26},{3,27},{4,28},{5,29},{6,30},{7,31},{8,0},{9,1... | collective-permute-start | bytes 552968 | tf_op jit(solution)/shard_map/ppermute | solution.py:620
  37.0 0.0 collective-permute-start.6
  37.0 1.6 %collective-permute-start.5 = (bf16[144,640]{1,0:T(8,128)(2,1)S(1)}, bf16[144,640]{1,0:T(8,128)(2,1)S(1)}, u32[]{:S(2)}, u32[]{:S(2)}) collective-permute-start(bf16[144,640]{1,0:T(8,128)(2,1)S(1)} %row.1.refs_2_), channel_id=1, source_target_pairs={{0,16},{1,17},{2,18},{3,19},{4,20},{5,21},{6,22},{7,23},{8,24},{9,... | collective-permute-start | bytes 552968 | tf_op jit(solution)/shard_map/ppermute | solution.py:620
  38.7 1.1 %collective-permute-done.7.refs_4_ = bf16[144,640]{1,0:T(8,128)(2,1)S(1)} collective-permute-done((bf16[144,640]{1,0:T(8,128)(2,1)S(1)}, bf16[144,640]{1,0:T(8,128)(2,1)S(1)}, u32[]{:S(2)}, u32[]{:S(2)}) %collective-permute-start.7) | collective-permute-done | bytes 184352 | tf_op jit(solution)/shard_map/ppermute | solution.py:620
  39.8 5.1 %collective-permute-done.6.refs_3_ = bf16[144,640]{1,0:T(8,128)(2,1)S(1)} collective-permute-done((bf16[144,640]{1,0:T(8,128)(2,1)S(1)}, bf16[144,640]{1,0:T(8,128)(2,1)S(1)}, u32[]{:S(2)}, u32[]{:S(2)}) %collective-permute-start.6) | collective-permute-done | bytes 184352 | tf_op jit(solution)/shard_map/ppermute | solution.py:620
  44.9 1.0 %collective-permute-done.5.refs_1_ = bf16[144,640]{1,0:T(8,128)(2,1)S(1)} collective-permute-done((bf16[144,640]{1,0:T(8,128)(2,1)S(1)}, bf16[144,640]{1,0:T(8,128)(2,1)S(1)}, u32[]{:S(2)}, u32[]{:S(2)}) %collective-permute-start.5) | collective-permute-done | bytes 184352 | tf_op jit(solution)/shard_map/ppermute | solution.py:620
  45.9 2.2 %entering.1 = (bf16[144,640]{1,0:T(8,128)(2,1)S(1)}, bf16[144,640]{1,0:T(8,128)(2,1)S(1)}, bf16[144,640]{1,0:T(8,128)(2,1)S(1)}, bf16[144,640]{1,0:T(8,128)(2,1)...) custom-call(s32[6]{0:T(128)S(1)} %stack.19.refs_0_, ...), custom_call_target="tpu_custom_call" | custom-call | flops 1 | bytes 1 | tf_op jit(solution)/shard_map/entering/pallas_call | solution.py:49
  48.1 0.6 collective-permute-start.8
  48.7 4.2 %collective-permute-start.14 = (bf16[16,640]{1,0:T(8,128)(2,1)S(1)}, bf16[16,640]{1,0:T(8,128)(2,1)S(1)}, u32[]{:S(2)}, u32[]{:S(2)}) collective-permute-start(bf16[16,640]{1,0:T(8,128)(2,1)S(1)} %get-tuple-element.62.refs_2_), channel_id=1, source_target_pairs={{0,1},{1,0},{2,3},{3,2},{4,5},{5,4},{6,7},{7,6},{8,9},{9,8},{10,11... | collective-permute-start | bytes 61448 | tf_op jit(solution)/shard_map/ppermute | solution.py:620
  52.9 2.5 %collective-permute-start.9 = (bf16[144,640]{1,0:T(8,128)(2,1)S(1)}, bf16[144,640]{1,0:T(8,128)(2,1)S(1)}, u32[]{:S(2)}, u32[]{:S(2)}) collective-permute-start(bf16[144,640]{1,0:T(8,128)(2,1)S(1)} %get-tuple-element.59.refs_10_), channel_id=1, source_target_pairs={{0,2},{1,3},{2,4},{3,5},{4,6},{5,7},{6,0},{7,1},{8,10},{9,11},{10,... | collective-permute-start | bytes 552968 | tf_op jit(solution)/shard_map/ppermute | solution.py:620
  55.4 0.3 collective-permute-start.10
  55.8 1.5 %collective-permute-start.13 = (bf16[144,640]{1,0:T(8,128)(2,1)S(1)}, bf16[144,640]{1,0:T(8,128)(2,1)S(1)}, u32[]{:S(2)}, u32[]{:S(2)}) collective-permute-start(bf16[144,640]{1,0:T(8,128)(2,1)S(1)} %get-tuple-element.61.refs_6_), channel_id=1, source_target_pairs={{0,6},{1,7},{2,0},{3,1},{4,2},{5,3},{6,4},{7,5},{8,14},{9,15},{10,... | collective-permute-start | bytes 552968 | tf_op jit(solution)/shard_map/ppermute | solution.py:620
  57.2 0.0 collective-permute-done.14.refs_3_
  57.2 0.0 collective-permute-start.12
  57.2 0.0 collective-permute-done.8.refs_1_
  57.2 1.5 %collective-permute-start.11 = (bf16[144,640]{1,0:T(8,128)(2,1)S(1)}, bf16[144,640]{1,0:T(8,128)(2,1)S(1)}, u32[]{:S(2)}, u32[]{:S(2)}) collective-permute-start(bf16[144,640]{1,0:T(8,128)(2,1)S(1)} %get-tuple-element.61.refs_6_), channel_id=1, source_target_pairs={{0,4},{1,5},{2,6},{3,7},{4,0},{5,1},{6,2},{7,3},{8,12},{9,13},{10,... | collective-permute-start | bytes 552968 | tf_op jit(solution)/shard_map/ppermute | solution.py:620
  58.8 0.0 copy-done.2
  58.8 5.0 %resp_within.1 = (f32[8,128,640]{2,1,0:T(8,128)S(1)}, f32[8,128,640]{2,1,0:T(8,128)S(1)}, bf16[128,256]{1,0:T(8,128)(2,1)S(1)}) custom-call(s32[6]{0:T(128)S(1)} %stack.19.refs_0_, bf16[128,5376]{1,0:T(8,128)(2,1)S(1)} %bitcast.11, bf16[16,640]{1,0:T(8,128)(2,1)S(1)} %get-tuple-element.62.refs_2_, bf16[16,640]{1,0:T(8,128)(2,1)S(1)} %collective-permute-done.14.refs_3_, ...), custom_call_target="tpu_custom_call" | custom-call | flops 1 | bytes 1 | tf_op jit(solution)/shard_map/resp_within/pallas_call | solution.py:49
  63.8 0.0 collective-permute-done.9.refs_3_
  63.8 0.0 collective-permute-done.10.refs_4_
  63.8 2.3 %collective-permute-done.13.refs_8_ = bf16[144,640]{1,0:T(8,128)(2,1)S(1)} collective-permute-done((bf16[144,640]{1,0:T(8,128)(2,1)S(1)}, bf16[144,640]{1,0:T(8,128)(2,1)S(1)}, u32[]{:S(2)}, u32[]{:S(2)}) %collective-permute-start.13) | collective-permute-done | bytes 184352 | tf_op jit(solution)/shard_map/ppermute | solution.py:620
  66.0 0.0 collective-permute-done.12.refs_7_
  66.1 3.6 %collective-permute-done.11.refs_5_ = bf16[144,640]{1,0:T(8,128)(2,1)S(1)} collective-permute-done((bf16[144,640]{1,0:T(8,128)(2,1)S(1)}, bf16[144,640]{1,0:T(8,128)(2,1)S(1)}, u32[]{:S(2)}, u32[]{:S(2)}) %collective-permute-start.11) | collective-permute-done | bytes 184352 | tf_op jit(solution)/shard_map/ppermute | solution.py:620
  69.7 2.0 %cores.1 = (bf16[4,256,640]{2,1,0:T(8,128)(2,1)S(1)}, bf16[4,256,640]{2,1,0:T(8,128)(2,1)S(1)}, bf16[4,256,640]{2,1,0:T(8,128)(2,1)S(1)}) custom-call(s32[6]{0:T(128)S(1)} %stack.19.refs_0_, bf16[144,640]{1,0:T(8,128)(2,1)S(1)} %collective-permute-done.8.refs_1_, bf16[144,640]{1,0:T(8,128)(2,1)S(1)} %get-tuple-element.58.refs_2_, ...), custom_call_target="tpu_custom_call" | custom-call | flops 1 | bytes 1 | tf_op jit(solution)/shard_map/cores/pallas_call | solution.py:49
  71.7 0.9 %collective-permute-start.15 = (bf16[4,256,640]{2,1,0:T(8,128)(2,1)S(1)}, bf16[4,256,640]{2,1,0:T(8,128)(2,1)S(1)}, u32[]{:S(2)}, u32[]{:S(2)}) collective-permute-start(bf16[4,256,640]{2,1,0:T(8,128)(2,1)S(1)} %get-tuple-element.65.refs_5_), channel_id=1, source_target_pairs={{0,1},{1,0},{2,3},{3,2},{4,5},{5,4},{6,7},{7,6},{8,9},{9,8},{10,11... | collective-permute-start | bytes 3932168 | tf_op jit(solution)/shard_map/ppermute | solution.py:620
  72.6 0.1 collective-permute-start.16
  72.7 1.9 %prompt_own_half.1 = (f32[4,256,640]{2,1,0:T(8,128)S(1)}, f32[256,128]{1,0:T(8,128)S(1)}) custom-call(s32[6]{0:T(128)S(1)} %stack.19.refs_0_, f32[8,256,640]{2,1,0:T(8,128)S(1)} %get-tuple-element.54.refs_5_.refs_9_.refs_14_.refs_1_, f32[8,256,640]{2,1,0:T(8,128)S(1)} %get-tuple-element.55.refs_6_.refs_10_.refs_15_.refs_2_, ...), custom_call_target="tpu_custom_call" | custom-call | flops 1 | bytes 1 | tf_op jit(solution)/shard_map/prompt_own_half/pallas_call | solution.py:49
  74.5 0.0 copy-start.5
  74.5 1.2 %resp_own_half.1 = (f32[4,128,640]{2,1,0:T(8,128)S(1)}, f32[128,128]{1,0:T(8,128)S(1)}) custom-call(s32[6]{0:T(128)S(1)} %stack.19.refs_0_, f32[8,128,640]{2,1,0:T(8,128)S(1)} %get-tuple-element.63.refs_12_.refs_1_, f32[8,128,640]{2,1,0:T(8,128)S(1)} %get-tuple-element.64.refs_13_.refs_2_, bf16[128,256]{1,0:T(8,128)(2,1)S(1)} %get-tuple-element.69.refs_3_, ...), custom_call_target="tpu_custom_call" | custom-call | flops 1 | bytes 1 | tf_op jit(solution)/shard_map/resp_own_half/pallas_call | solution.py:49
  75.8 0.0 collective-permute-done.15.refs_4_
  75.8 0.0 copy-done.5
  75.8 3.8 %prompt_finish.1 = (bf16[256,5120]{1,0:T(8,128)(2,1)}, f32[8,128]{1,0:T(8,128)S(1)}) custom-call(s32[6]{0:T(128)S(1)} %stack.19.refs_0_, f32[8,256,640]{2,1,0:T(8,128)S(1)} %get-tuple-element.54.refs_5_.refs_9_.refs_14_.refs_1_, f32[8,256,640]{2,1,0:T(8,128)S(1)} %get-tuple-element.55.refs_6_.refs_10_.refs_15_.refs_2_, ...), custom_call_target="tpu_custom_call" | custom-call | flops 1 | bytes 1 | tf_op jit(solution)/shard_map/prompt_finish/pallas_call | solution.py:593
  79.6 0.0 collective-permute-done.16.refs_4_
  79.6 3.2 %resp_finish.1 = (bf16[128,5120]{1,0:T(8,128)(2,1)}, f32[8,128]{1,0:T(8,128)}) custom-call(s32[6]{0:T(128)S(1)} %stack.19.refs_0_, f32[8,128,640]{2,1,0:T(8,128)S(1)} %get-tuple-element.63.refs_12_.refs_1_, f32[8,128,640]{2,1,0:T(8,128)S(1)} %get-tuple-element.64.refs_13_.refs_2_, bf16[128,256]{1,0:T(8,128)(2,1)S(1)} %get-tuple-element.69.refs_3_, ...), custom_call_target="tpu_custom_call" | custom-call | flops 1 | bytes 1 | tf_op jit(solution)/shard_map/resp_finish/pallas_call | solution.py:593
  (4 shorter events, 0.0 us)
Async XLA Ops:
  1.5 8.4 %collective-permute-start = (bf16[8,5376]{1,0:T(8,128)(2,1)S(1)}, bf16[8,5376]{1,0:T(8,128)(2,1)S(1)}, u32[]{:S(2)}, u32[]{:S(2)}) collective-permute-start(bf16[8,5376]{1,0:T(8,128)(2,1)S(1)} %slice.3.refs_5_.refs_4_), channel_id=1, source_target_pairs={{0,1},{1,2},{2,3},{3,4},{4,5},{5,6},{6,7},{7,8},{8,9},{9,10},{10,1... | collective-permute-start | bytes 258056 | tf_op jit(solution)/shard_map/ppermute | solution.py:715
  9.9 5.6 %copy-start = (bf16[256,5376]{1,0:T(8,128)(2,1)S(1)}, bf16[256,5376]{1,0:T(8,128)(2,1)}, u32[]{:S(2)}) copy-start(bf16[256,5376]{1,0:T(8,128)(2,1)} %refs_1_.5) | copy-start | bytes 8257540
  9.9 5.6 %copy-start.4 = (f32[4,5376]{1,0:T(4,128)S(1)}, f32[4,5376]{1,0:T(4,128)}, u32[]{:S(2)}) copy-start(f32[4,5376]{1,0:T(4,128)} %refs_4_.1) | copy-start | bytes 258052
  15.4 4.0 %collective-permute-start.1 = (bf16[4,144,640]{2,1,0:T(8,128)(2,1)S(1)}, bf16[4,144,640]{2,1,0:T(8,128)(2,1)S(1)}, u32[]{:S(2)}, u32[]{:S(2)}) collective-permute-start(bf16[4,144,640]{2,1,0:T(8,128)(2,1)S(1)} %get-tuple-element.43.refs_8_), channel_id=1, source_target_pairs={{0,1},{1,0},{2,3},{3,2},{4,5},{5,4},{6,7},{7,6},{8,9},{9,8},{10,11... | collective-permute-start | bytes 2211848 | tf_op jit(solution)/shard_map/ppermute | solution.py:620
  15.6 9.4 %copy-start.1 = (bf16[256,5120]{1,0:T(8,128)(2,1)S(1)}, bf16[256,5120]{1,0:T(8,128)(2,1)}, u32[]{:S(2)}) copy-start(bf16[256,5120]{1,0:T(8,128)(2,1)} %refs_3_.1) | copy-start | bytes 7864324
  19.4 5.5 %copy-start.8 = (f32[80]{0:T(128)S(1)}, f32[80]{0:T(128)}, u32[]{:S(2)}) copy-start(f32[80]{0:T(128)} %param.24) | copy-start | bytes 964
  20.4 9.8 %collective-permute-start.3 = (bf16[144,640]{1,0:T(8,128)(2,1)S(1)}, bf16[144,640]{1,0:T(8,128)(2,1)S(1)}, u32[]{:S(2)}, u32[]{:S(2)}) collective-permute-start(bf16[144,640]{1,0:T(8,128)(2,1)S(1)} %get-tuple-element.51.refs_11_), channel_id=1, source_target_pairs={{0,2},{1,3},{2,4},{3,5},{4,6},{5,7},{6,0},{7,1},{8,10},{9,11},{10,... | collective-permute-start | bytes 552968 | tf_op jit(solution)/shard_map/ppermute | solution.py:620
  21.7 10.7 %collective-permute-start.2 = (bf16[144,640]{1,0:T(8,128)(2,1)S(1)}, bf16[144,640]{1,0:T(8,128)(2,1)S(1)}, u32[]{:S(2)}, u32[]{:S(2)}) collective-permute-start(bf16[144,640]{1,0:T(8,128)(2,1)S(1)} %get-tuple-element.52.refs_12_), channel_id=1, source_target_pairs={{0,4},{1,5},{2,6},{3,7},{4,0},{5,1},{6,2},{7,3},{8,12},{9,13},{10,... | collective-permute-start | bytes 552968 | tf_op jit(solution)/shard_map/ppermute | solution.py:620
  24.1 8.2 %collective-permute-start.4 = (bf16[144,640]{1,0:T(8,128)(2,1)S(1)}, bf16[144,640]{1,0:T(8,128)(2,1)S(1)}, u32[]{:S(2)}, u32[]{:S(2)}) collective-permute-start(bf16[144,640]{1,0:T(8,128)(2,1)S(1)} %get-tuple-element.53.refs_13_), channel_id=1, source_target_pairs={{0,6},{1,7},{2,0},{3,1},{4,2},{5,3},{6,4},{7,5},{8,14},{9,15},{10,... | collective-permute-start | bytes 552968 | tf_op jit(solution)/shard_map/ppermute | solution.py:620
  33.4 25.3 %copy-start.2 = (bf16[1,128,5376]{2,1,0:T(8,128)(2,1)S(1)}, bf16[1,128,5376]{2,1,0:T(8,128)(2,1)}, u32[]{:S(2)}) copy-start(bf16[1,128,5376]{2,1,0:T(8,128)(2,1)} %param.17) | copy-start | bytes 4128772
  33.4 25.3 %copy-start.3 = (bf16[1,128,5120]{2,1,0:T(8,128)(2,1)S(1)}, bf16[1,128,5120]{2,1,0:T(8,128)(2,1)}, u32[]{:S(2)}) copy-start(bf16[1,128,5120]{2,1,0:T(8,128)(2,1)} %param.18) | copy-start | bytes 3932164
  33.4 25.3 %copy-start.6 = (f32[80,1,128]{2,1,0:T(1,128)S(1)}, f32[80,1,128]{2,1,0:T(1,128)}, u32[]{:S(2)}) copy-start(f32[80,1,128]{2,1,0:T(1,128)} %param.20) | copy-start | bytes 122884
  33.5 25.3 %copy-start.7 = (f32[80,1,128]{2,1,0:T(1,128)S(1)}, f32[80,1,128]{2,1,0:T(1,128)}, u32[]{:S(2)}) copy-start(f32[80,1,128]{2,1,0:T(1,128)} %param.19) | copy-start | bytes 122884
  33.5 6.3 %collective-permute-start.7 = (bf16[144,640]{1,0:T(8,128)(2,1)S(1)}, bf16[144,640]{1,0:T(8,128)(2,1)S(1)}, u32[]{:S(2)}, u32[]{:S(2)}) collective-permute-start(bf16[144,640]{1,0:T(8,128)(2,1)S(1)} %row.1.refs_2_), channel_id=1, source_target_pairs={{0,24},{1,25},{2,26},{3,27},{4,28},{5,29},{6,30},{7,31},{8,0},{9,1... | collective-permute-start | bytes 552968 | tf_op jit(solution)/shard_map/ppermute | solution.py:620
  37.0 7.8 %collective-permute-start.6 = (bf16[144,640]{1,0:T(8,128)(2,1)S(1)}, bf16[144,640]{1,0:T(8,128)(2,1)S(1)}, u32[]{:S(2)}, u32[]{:S(2)}) collective-permute-start(bf16[144,640]{1,0:T(8,128)(2,1)S(1)} %row.1.refs_2_), channel_id=1, source_target_pairs={{0,8},{1,9},{2,10},{3,11},{4,12},{5,13},{6,14},{7,15},{8,16},{9,17... | collective-permute-start | bytes 552968 | tf_op jit(solution)/shard_map/ppermute | solution.py:620
  37.0 8.8 %collective-permute-start.5 = (bf16[144,640]{1,0:T(8,128)(2,1)S(1)}, bf16[144,640]{1,0:T(8,128)(2,1)S(1)}, u32[]{:S(2)}, u32[]{:S(2)}) collective-permute-start(bf16[144,640]{1,0:T(8,128)(2,1)S(1)} %row.1.refs_2_), channel_id=1, source_target_pairs={{0,16},{1,17},{2,18},{3,19},{4,20},{5,21},{6,22},{7,23},{8,24},{9,... | collective-permute-start | bytes 552968 | tf_op jit(solution)/shard_map/ppermute | solution.py:620
  48.1 9.2 %collective-permute-start.8 = (bf16[144,640]{1,0:T(8,128)(2,1)S(1)}, bf16[144,640]{1,0:T(8,128)(2,1)S(1)}, u32[]{:S(2)}, u32[]{:S(2)}) collective-permute-start(bf16[144,640]{1,0:T(8,128)(2,1)S(1)} %get-tuple-element.57.refs_11_), channel_id=1, source_target_pairs={{0,4},{1,5},{2,6},{3,7},{4,0},{5,1},{6,2},{7,3},{8,12},{9,13},{10,... | collective-permute-start | bytes 552968 | tf_op jit(solution)/shard_map/ppermute | solution.py:620
  48.7 8.5 %collective-permute-start.14 = (bf16[16,640]{1,0:T(8,128)(2,1)S(1)}, bf16[16,640]{1,0:T(8,128)(2,1)S(1)}, u32[]{:S(2)}, u32[]{:S(2)}) collective-permute-start(bf16[16,640]{1,0:T(8,128)(2,1)S(1)} %get-tuple-element.62.refs_2_), channel_id=1, source_target_pairs={{0,1},{1,0},{2,3},{3,2},{4,5},{5,4},{6,7},{7,6},{8,9},{9,8},{10,11... | collective-permute-start | bytes 61448 | tf_op jit(solution)/shard_map/ppermute | solution.py:620
  52.9 10.8 %collective-permute-start.9 = (bf16[144,640]{1,0:T(8,128)(2,1)S(1)}, bf16[144,640]{1,0:T(8,128)(2,1)S(1)}, u32[]{:S(2)}, u32[]{:S(2)}) collective-permute-start(bf16[144,640]{1,0:T(8,128)(2,1)S(1)} %get-tuple-element.59.refs_10_), channel_id=1, source_target_pairs={{0,2},{1,3},{2,4},{3,5},{4,6},{5,7},{6,0},{7,1},{8,10},{9,11},{10,... | collective-permute-start | bytes 552968 | tf_op jit(solution)/shard_map/ppermute | solution.py:620
  55.4 8.4 %collective-permute-start.10 = (bf16[144,640]{1,0:T(8,128)(2,1)S(1)}, bf16[144,640]{1,0:T(8,128)(2,1)S(1)}, u32[]{:S(2)}, u32[]{:S(2)}) collective-permute-start(bf16[144,640]{1,0:T(8,128)(2,1)S(1)} %get-tuple-element.60.refs_12_), channel_id=1, source_target_pairs={{0,6},{1,7},{2,0},{3,1},{4,2},{5,3},{6,4},{7,5},{8,14},{9,15},{10,... | collective-permute-start | bytes 552968 | tf_op jit(solution)/shard_map/ppermute | solution.py:620
  55.8 10.3 %collective-permute-start.13 = (bf16[144,640]{1,0:T(8,128)(2,1)S(1)}, bf16[144,640]{1,0:T(8,128)(2,1)S(1)}, u32[]{:S(2)}, u32[]{:S(2)}) collective-permute-start(bf16[144,640]{1,0:T(8,128)(2,1)S(1)} %get-tuple-element.61.refs_6_), channel_id=1, source_target_pairs={{0,6},{1,7},{2,0},{3,1},{4,2},{5,3},{6,4},{7,5},{8,14},{9,15},{10,... | collective-permute-start | bytes 552968 | tf_op jit(solution)/shard_map/ppermute | solution.py:620
  57.2 8.8 %collective-permute-start.12 = (bf16[144,640]{1,0:T(8,128)(2,1)S(1)}, bf16[144,640]{1,0:T(8,128)(2,1)S(1)}, u32[]{:S(2)}, u32[]{:S(2)}) collective-permute-start(bf16[144,640]{1,0:T(8,128)(2,1)S(1)} %get-tuple-element.61.refs_6_), channel_id=1, source_target_pairs={{0,2},{1,3},{2,4},{3,5},{4,6},{5,7},{6,0},{7,1},{8,10},{9,11},{10,... | collective-permute-start | bytes 552968 | tf_op jit(solution)/shard_map/ppermute | solution.py:620
  57.2 12.4 %collective-permute-start.11 = (bf16[144,640]{1,0:T(8,128)(2,1)S(1)}, bf16[144,640]{1,0:T(8,128)(2,1)S(1)}, u32[]{:S(2)}, u32[]{:S(2)}) collective-permute-start(bf16[144,640]{1,0:T(8,128)(2,1)S(1)} %get-tuple-element.61.refs_6_), channel_id=1, source_target_pairs={{0,4},{1,5},{2,6},{3,7},{4,0},{5,1},{6,2},{7,3},{8,12},{9,13},{10,... | collective-permute-start | bytes 552968 | tf_op jit(solution)/shard_map/ppermute | solution.py:620
  71.7 4.1 %collective-permute-start.15 = (bf16[4,256,640]{2,1,0:T(8,128)(2,1)S(1)}, bf16[4,256,640]{2,1,0:T(8,128)(2,1)S(1)}, u32[]{:S(2)}, u32[]{:S(2)}) collective-permute-start(bf16[4,256,640]{2,1,0:T(8,128)(2,1)S(1)} %get-tuple-element.65.refs_5_), channel_id=1, source_target_pairs={{0,1},{1,0},{2,3},{3,2},{4,5},{5,4},{6,7},{7,6},{8,9},{9,8},{10,11... | collective-permute-start | bytes 3932168 | tf_op jit(solution)/shard_map/ppermute | solution.py:620
  72.6 7.0 %collective-permute-start.16 = (bf16[4,256,640]{2,1,0:T(8,128)(2,1)S(1)}, bf16[4,256,640]{2,1,0:T(8,128)(2,1)S(1)}, u32[]{:S(2)}, u32[]{:S(2)}) collective-permute-start(bf16[4,256,640]{2,1,0:T(8,128)(2,1)S(1)} %get-tuple-element.70.refs_4_), channel_id=1, source_target_pairs={{0,1},{1,0},{2,3},{3,2},{4,5},{5,4},{6,7},{7,6},{8,9},{9,8},{10,11... | collective-permute-start | bytes 3932168 | tf_op jit(solution)/shard_map/ppermute | solution.py:620
  74.5 1.2 %copy-start.5 = (f32[5120]{0:T(1024)S(1)}, f32[5120]{0:T(1024)}, u32[]{:S(2)}) copy-start(f32[5120]{0:T(1024)} %param.25) | copy-start | bytes 61444

commit v4 on v3

--- a/solution.py
+++ b/solution.py
@@ -117,15 +117,21 @@
 
 
 def tables_kernel(
-    where_ref, keep_from, step_from, col_ref, rowt_ref, colt_ref, hcol_ref, keep_ref, step_ref, sems
+    where_ref, keep_from, step_from, x_from, w_from, col_ref, rowt_ref, colt_ref, hcol_ref, x_ref, w_ref,
+    keep_ref, step_ref, sems,
 ):
     copies = [
         pltpu.make_async_copy(keep_from, keep_ref, sems.at[0]),
         pltpu.make_async_copy(step_from, step_ref, sems.at[1]),
+        pltpu.make_async_copy(w_from, w_ref, sems.at[2]),
     ]
+    share = x_ref.shape[0] // 4
+    for at in range(4):
+        rows = pl.ds(at * share, share)
+        copies.append(pltpu.make_async_copy(x_from.at[rows], x_ref.at[rows], sems.at[3 + at]))
     for copy in copies:
         copy.start()
-    for copy in copies:
+    for copy in copies[:2]:
         copy.wait()
     place = lax.broadcasted_iota(jnp.int32, (8, 128), 0)
     stack = jnp.zeros((8, 128), F32)
@@ -137,6 +143,8 @@
     for pair in range(HEADS // 2):
         at = (pair % PAIRS) * 128
         hcol_ref[pair // PAIRS, :, at : at + 128] = spread(stack, pair)
+    for copy in copies[2:]:
+        copy.wait()
 
 
 def conv_columns(rows, hist, weight, bias):
@@ -175,23 +183,11 @@
 
 
 def sent_states_kernel(
-    where_ref, x_from, w_from, hist_ref, b_ref, rows_ref, colt_ref, hcol_ref,
-    acts_ref, kq_ref, keyt_ref, high_ref, msg_ref, x_ref, w_ref, weighted_ref, sems,
+    where_ref, x_ref, w_ref, hist_ref, b_ref, rows_ref, colt_ref, hcol_ref,
+    acts_ref, kq_ref, keyt_ref, high_ref, msg_ref, weighted_ref,
 ):
     half = 1 - where_ref[2]
-    kq_cols = pl.ds(D_INNER, 2 * STATE)
-    copies = [
-        pltpu.make_async_copy(w_from, w_ref, sems.at[0]),
-        pltpu.make_async_copy(x_from.at[:, kq_cols], x_ref.at[:, kq_cols], sems.at[1]),
-    ]
-    for at in range(4):
-        cols = pl.ds(pl.multiple_of((half * 4 + at) * SLAB, 128), SLAB)
-        copies.append(pltpu.make_async_copy(x_from.at[:, cols], x_ref.at[:, cols], sems.at[2 + at]))
-    for copy in copies:
-        copy.start()
     conv = convolver(where_ref, x_ref, hist_ref, w_ref, b_ref)
-    for copy in copies[:2]:
-        copy.wait()
     key = conv(slice(D_INNER, D_INNER + STATE))
     kq_ref[:, 0:STATE] = key
     kq_ref[:, STATE : 2 * STATE] = conv(slice(D_INNER + STATE, D_INNER + 2 * STATE))
@@ -199,8 +195,6 @@
 
     def body(at, carry):
         slab = half * 4 + at
-        cols = pl.ds(pl.multiple_of(slab * SLAB, 128), SLAB)
-        pltpu.make_async_copy(x_from.at[:, cols], x_ref.at[:, cols], sems.at[2 + at]).wait()
 
         def put(state):
             msg_ref[at, 0:STATE] = state.astype(BF16)
@@ -424,7 +418,7 @@
     return ref[0:STATE, cols].astype(F32) + along * factor[:, cols]
 
 
-def row_kernel(where_ref, r2, r0, r1, r3, out_ref, state_ref):
+def row_kernel(where_ref, r0, r1, r3, r2, out_ref, state_ref):
     refs = (r0, r1, r2, r3)
     places = [at_shift(where_ref[0], -i) for i in range(SIDE)]
     weights, through = weights_to(places, [decay_of(ref[STATE:]) for ref in refs], SIDE)
@@ -445,7 +439,7 @@
     out_ref[STATE:] = extra_rows(through, tail)
 
 
-def entering_kernel(where_ref, t2, t0, t1, t3, r2, r0, r1, r3, e0, e1, e2, e3, final_ref, tail_ref, state_ref):
+def entering_kernel(where_ref, t0, t1, t3, t2, r0, r1, r3, r2, e0, e1, e2, e3, final_ref, tail_ref, state_ref):
     x, y = where_ref[0], where_ref[1]
     refs, totals, outs = (r0, r1, r2, r3), (t0, t1, t2, t3), (e0, e1, e2, e3)
     rows = [at_shift(y, -i) for i in range(SIDE)]
@@ -491,7 +485,7 @@
 
 
 def cores_kernel(
-    where_ref, g2, g0, g1, g3, f2, f0, f1, f3, own_ref, recv_ref, hcol_ref, mine_ref, send_ref, final_ref
+    where_ref, g0, g1, g3, g2, f0, f1, f3, f2, own_ref, recv_ref, hcol_ref, mine_ref, send_ref, final_ref
 ):
     x, core = where_ref[0], where_ref[2]
     first = (core == 0).astype(F32)
@@ -512,7 +506,8 @@
             put_pair(send_ref, slab, cols, later * first + start * last)
 
 
-TILE = 64
+TILE = 128
+PART = 32
 
 
 def half_gated(query, held_ref, half, here, part_ref, gate_ref, put):
@@ -554,7 +549,7 @@
     core = where_ref[2]
 
     def copy_out(at):
-        here = pl.ds(pl.multiple_of(at * TILE, TILE), TILE)
+        here = pl.ds(pl.multiple_of(at * PART, PART), PART)
         return pltpu.make_async_copy(rows_ref.at[here], out_ref.at[here], sems.at[at])
 
     def body(at, carry):
@@ -569,22 +564,23 @@
         mean = jnp.sum(squares, axis=1, keepdims=True) * (1.0 / D_INNER)
         row = lax.broadcasted_iota(jnp.int32, (TILE, 1), 0) + start
         inv = jnp.where(row < where_ref[length_at], lax.rsqrt(mean + EPS), 0.0)
-        inv = jnp.broadcast_to(inv, (TILE, 128))
-        for s in range(4):
-            for half, value_of in (
-                (core, lambda cols: own_ref[s, here, cols]),
-                (1 - core, lambda cols: gated_ref[s, :, cols]),
-            ):
+        for part in range(TILE // PART):
+            inside = slice(part * PART, (part + 1) * PART)
+            there = pl.ds(pl.multiple_of(start + part * PART, PART), PART)
+            scale = jnp.broadcast_to(inv[inside], (PART, 128))
+            for s in range(4):
                 for cols in CHUNKS:
-                    wide = pl.ds(pl.multiple_of((half * 4 + s) * SLAB + cols.start, 128), 128)
-                    rows_ref[here, wide] = (value_of(cols) * inv * gain_ref[:, wide]).astype(BF16)
-        copy_out(at).start()
+                    wide = pl.ds(pl.multiple_of((core * 4 + s) * SLAB + cols.start, 128), 128)
+                    rows_ref[there, wide] = (own_ref[s, there, cols] * scale * gain_ref[:, wide]).astype(BF16)
+                    wide = pl.ds(pl.multiple_of((4 - core * 4 + s) * SLAB + cols.start, 128), 128)
+                    rows_ref[there, wide] = (gated_ref[s, inside, cols] * scale * gain_ref[:, wide]).astype(BF16)
+            copy_out(at * (TILE // PART) + part).start()
         return carry
 
     tiles = part_ref.shape[1] // TILE
     lax.fori_loop(0, tiles, body, 0)
     token_ref[...] = jnp.zeros_like(token_ref)
-    for at in range(tiles):
+    for at in range(tiles * (TILE // PART)):
         copy_out(at).wait()
 
 
@@ -597,7 +593,7 @@
         scratch_shapes=[
             pltpu.VMEM((4, TILE, SLAB), F32),
             pltpu.VMEM((rows, D_INNER), BF16),
-            pltpu.SemaphoreType.DMA((rows // TILE,)),
+            pltpu.SemaphoreType.DMA((rows // PART,)),
         ],
         out_shape=[jax.ShapeDtypeStruct((rows, D_INNER), BF16), jax.ShapeDtypeStruct((8, 128), F32)],
         compiler_params=params(),
@@ -630,17 +626,19 @@
 
 def round_x(here, to_next, to_opposite, to_last):
     opposite = along_x(to_opposite, 2)
-    return opposite, here, along_x(to_next, 1), along_x(to_last, 3)
+    return here, along_x(to_next, 1), along_x(to_last, 3), opposite
 
 
 def along_y(value, by):
     return moved(value, lambda y, x, core: (y + by, x, core))
 
 
-def make_tables(where, keep, step):
+def make_tables(where, keep, step, xbc, weight):
     shapes = [((2, HEADS, BLOCK), F32), ((2, BLOCK, 128), F32), ((2, BLOCK, 128), F32), ((SLABS, 8, SLAB), F32)]
-    scratch = [pltpu.VMEM(keep.shape, F32), pltpu.VMEM(step.shape, F32), pltpu.SemaphoreType.DMA((2,))]
-    return whole(tables_kernel, where, (keep, step), shapes, "tables", scratch=scratch, outside=2)
+    shapes += [(xbc.shape, BF16), (weight.shape, F32)]
+    scratch = [pltpu.VMEM(keep.shape, F32), pltpu.VMEM(step.shape, F32), pltpu.SemaphoreType.DMA((7,))]
+    arrays = (keep, step, xbc, weight)
+    return whole(tables_kernel, where, arrays, shapes, "tables", scratch=scratch, outside=4)
 
 
 def sent_states(where, xbc, weight, hist, bias, own_rows, colt, hcol):
@@ -652,14 +650,9 @@
         ((4, STATE, SLAB), BF16),
         ((4, STATE + EXTRA, SLAB), BF16),
     ]
-    scratch = [
-        pltpu.VMEM(xbc.shape, BF16),
-        pltpu.VMEM(weight.shape, F32),
-        pltpu.VMEM((rows, SLAB), BF16),
-        pltpu.SemaphoreType.DMA((6,)),
-    ]
+    scratch = [pltpu.VMEM((rows, SLAB), BF16)]
     arrays = (xbc, weight, hist, bias, own_rows, colt, hcol)
-    return whole(sent_states_kernel, where, arrays, shapes, "sent_states", scratch=scratch, outside=2)
+    return whole(sent_states_kernel, where, arrays, shapes, "sent_states", scratch=scratch)
 
 
 def kept_states(where, xbc, weight, hist, bias, keyt, colt, hcol, after):
@@ -713,13 +706,13 @@
     own_rows = prompt_xbc[rows - HIST :]
     count = 2 * SIDE * SIDE
     hist = lax.ppermute(own_rows, GROUP, [(i, i + 1) for i in range(count - 1)])
-    col, rowt, colt, hcol = make_tables(where, prompt_keep, prompt_step)
+    col, rowt, colt, hcol, xbc, taps = make_tables(where, prompt_keep, prompt_step, prompt_xbc, conv_weight)
     sent_acts, kq, keyt, sent_high, msg = sent_states(
-        where, prompt_xbc, conv_weight, hist, bias_row, own_rows, colt, hcol
+        where, xbc, taps, hist, bias_row, own_rows, colt, hcol
     )
     recv = swap_cores(msg)
     kept_acts, kept_high, own = kept_states(
-        where, prompt_xbc, conv_weight, hist, bias_row, keyt, colt, hcol, after=(msg,)
+        where, xbc, taps, hist, bias_row, keyt, colt, hcol, after=(msg,)
     )
     with_extra = ((STATE + EXTRA, SLAB), BF16)
     c0, c1, c2, c3 = whole(chip_kernel, where, (own, recv, hcol, own_rows), [with_extra] * 4, "chip")
@@ -730,7 +723,7 @@
     )
     (total,) = whole(row_kernel, where, pieces, [with_extra], "row", after=(part, gate), scratch=[pltpu.VMEM((STATE, SLAB), F32)])
     opposite = along_y(total, 2)
-    totals = (opposite, total, along_y(total, 1), along_y(total, 3))
+    totals = (total, along_y(total, 1), along_y(total, 3), opposite)
     e0, e1, e2, e3, final, tail = whole(
         entering_kernel, where, totals + pieces, [with_extra] * 5 + [((EXTRA, SLAB), BF16)], "entering", after=(part, gate),
         scratch=[pltpu.VMEM((SIDE + 1, STATE, SLAB), F32)],

time: 83.2 us -> 79.5 us (0.956)
  Pallas kernels: 38.1 us -> 35.2 us
  waiting for transfers between devices: 15.3 us -> 16.3 us
  starting transfers between devices: 26 us -> 25.1 us
    pallas_call x11, Pallas kernels: 31.2 us -> 29.2 us  [whole(): pl.pallas_call(ordered(kernel, 1 + len(arrays), len(after)), in_specs=[SM...]
    ppermute x16, waiting for transfers between devices: 15.2 us -> 16.3 us  [moved(): return lax.ppermute(value, GROUP, pairs)]
    ppermute x16, starting transfers between devices: 21.5 us -> 20.6 us  [moved(): return lax.ppermute(value, GROUP, pairs)]
    pallas_call x2, Pallas kernels: 6.97 us -> 6.03 us  [finish(): pl.pallas_call(ordered(functools.partial(finish_kernel, length_at), 8, le...]
  transfers between devices with their start and end apart: 17 -> 17, of which waited for: 6 -> 7; matrix products, arithmetic and copies ran while one was open for 1% -> 0% of each run, Pallas kernels for 28% -> 28%
where the time goes in v4:
time: 79.5 us; the launch traced here: 79.3 us
  Pallas kernels  35.2 us (44%)
  starting transfers between devices  25.1 us (32%)
  waiting for transfers between devices  16.3 us (21%)
  between operations  1.71 us (2%)
  local copies, waits for them, and re-layouts  1.05 us (1%)
    pallas_call x11, Pallas kernels, whole(): pl.pallas_call(ordered(kernel, 1 + len(arrays), len(after)), in_specs=[SM...  29.2 us
    ppermute x16, starting transfers between devices, moved(): return lax.ppermute(value, GROUP, pairs)  20.6 us
    ppermute x16, waiting for transfers between devices, moved(): return lax.ppermute(value, GROUP, pairs)  16.3 us
    pallas_call x2, Pallas kernels, finish(): pl.pallas_call(ordered(functools.partial(finish_kernel, length_at), 8, le...  6.03 us
    ppermute x1, starting transfers between devices, shards(): hist = lax.ppermute(own_rows, GROUP, [(i, i + 1) for i in range(count - 1)])  4.5 us
  transfers between devices with their start and end apart: 17, of which 7 were waited for; matrix products, arithmetic and copies ran while one was open for 0% of the time, Pallas kernels for 28%

profile of v4, /device:TPU:1, one launch (start us, length us, event | category | flops | bytes accessed | tf_op | source)
XLA Modules:
  0.0 79.3 jit_solution(6689930772090538248)
XLA Ops:
  0.6 0.9 %slice.3.refs_5_.refs_4_ = bf16[8,5376]{1,0:T(8,128)(2,1)S(1)} slice(bf16[256,5376]{1,0:T(8,128)(2,1)} %refs_3_.2), slice={[248:256], [0:5376]} | slice | bytes 172032 | tf_op jit(solution)/shard_map/slice | solution.py:706
  1.5 4.5 %collective-permute-start = (bf16[8,5376]{1,0:T(8,128)(2,1)S(1)}, bf16[8,5376]{1,0:T(8,128)(2,1)S(1)}, u32[]{:S(2)}, u32[]{:S(2)}) collective-permute-start(bf16[8,5376]{1,0:T(8,128)(2,1)S(1)} %slice.3.refs_5_.refs_4_), channel_id=1, source_target_pairs={{0,1},{1,2},{2,3},{3,4},{4,5},{5,6},{6,7},{7,8},{8,9},{9,10},{10,1... | collective-permute-start | bytes 258056 | tf_op jit(solution)/shard_map/ppermute | solution.py:708
  6.7 0.1 stack.19.refs_0_
  6.8 2.5 %tables.1 = (f32[2,80,128]{2,1,0:T(8,128)S(1)}, f32[2,128,128]{2,1,0:T(8,128)S(1)}, f32[2,128,128]{2,1,0:T(8,128)S(1)}, f32[8,8,640]{2,1,0:T(8,128)S(1)}, bf16[2...) custom-call(s32[6]{0:T(128)S(1)} %stack.19.refs_0_, f32[80,256]{1,0:T(8,128)} %refs_1_.1, f32[80,256]{1,0:T(8,128)} %refs_2_.1, ...), custom_call_target="tpu_custom_call" | custom-call | flops 1 | bytes 1 | tf_op jit(solution)/shard_map/tables/pallas_call | solution.py:49
  9.3 0.0 copy-done.8
  9.3 0.0 collective-permute-done.refs_3_
  9.3 4.2 %sent_states.1 = (bf16[4,256,640]{2,1,0:T(8,128)(2,1)S(1)}, bf16[256,256]{1,0:T(8,128)(2,1)S(1)}, bf16[128,256]{1,0:T(8,128)(2,1)S(1)}, bf16[4,128,640]{2,1,0:T(8,128)(2,1)S(1)}, bf16[4,144,640]{2,1,0:T(8,128)(2,1)S(1)}) custom-call(s32[6]{0:T(128)S(1)} %stack.19.refs_0_, bf16[256,5376]{1,0:T(8,128)(2,1)S(1)} %get-tuple-element.41.refs_1_, ...), custom_call_target="tpu_custom_call" | custom-call | flops 1 | bytes 1 | tf_op jit(solution)/shard_map/sent_states/pallas_call | solution.py:49
  13.5 0.1 collective-permute-start.1
  13.6 3.9 %kept_states.1 = (bf16[4,256,640]{2,1,0:T(8,128)(2,1)S(1)}, bf16[4,128,640]{2,1,0:T(8,128)(2,1)S(1)}, f32[4,128,640]{2,1,0:T(8,128)S(1)}) custom-call(s32[6]{0:T(128)S(1)} %stack.19.refs_0_, bf16[256,5376]{1,0:T(8,128)(2,1)S(1)} %get-tuple-element.41.refs_1_, f32[4,5376]{1,0:T(4,128)S(1)} %get-tuple-element.42.refs_2_, ...), custom_call_target="tpu_custom_call" | custom-call | flops 1 | bytes 1 | tf_op jit(solution)/shard_map/kept_states/pallas_call | solution.py:49
  17.5 0.0 copy-start.7
  17.5 0.0 collective-permute-done.1.refs_2_.refs_10_
  17.5 0.9 %chip.1 = (bf16[144,640]{1,0:T(8,128)(2,1)S(1)}, bf16[144,640]{1,0:T(8,128)(2,1)S(1)}, bf16[144,640]{1,0:T(8,128)(2,1)S(1)}, bf16[144,640]{1,0:T(8,128)(2,1)S(1)}) custom-call(s32[6]{0:T(128)S(1)} %stack.19.refs_0_, f32[4,128,640]{2,1,0:T(8,128)S(1)} %get-tuple-element.54.refs_1_.refs_9_, bf16[4,144,640]{2,1,0:T(8,128)(2,1)S(1)} %collective-permute-done.1.refs_2_.refs_10_, ...), custom_call_target="tpu_custom_call" | custom-call | flops 1 | bytes 1 | tf_op jit(solution)/shard_map/chip/pallas_call | solution.py:49
  18.4 1.3 %collective-permute-start.2 = (bf16[144,640]{1,0:T(8,128)(2,1)S(1)}, bf16[144,640]{1,0:T(8,128)(2,1)S(1)}, u32[]{:S(2)}, u32[]{:S(2)}) collective-permute-start(bf16[144,640]{1,0:T(8,128)(2,1)S(1)} %get-tuple-element.55.refs_11_), channel_id=1, source_target_pairs={{0,2},{1,3},{2,4},{3,5},{4,6},{5,7},{6,0},{7,1},{8,10},{9,11},{10,... | collective-permute-start | bytes 552968 | tf_op jit(solution)/shard_map/ppermute | solution.py:616
  19.7 2.5 %collective-permute-start.4 = (bf16[144,640]{1,0:T(8,128)(2,1)S(1)}, bf16[144,640]{1,0:T(8,128)(2,1)S(1)}, u32[]{:S(2)}, u32[]{:S(2)}) collective-permute-start(bf16[144,640]{1,0:T(8,128)(2,1)S(1)} %get-tuple-element.56.refs_12_), channel_id=1, source_target_pairs={{0,4},{1,5},{2,6},{3,7},{4,0},{5,1},{6,2},{7,3},{8,12},{9,13},{10,... | collective-permute-start | bytes 552968 | tf_op jit(solution)/shard_map/ppermute | solution.py:616
  22.2 0.9 %collective-permute-start.3 = (bf16[144,640]{1,0:T(8,128)(2,1)S(1)}, bf16[144,640]{1,0:T(8,128)(2,1)S(1)}, u32[]{:S(2)}, u32[]{:S(2)}) collective-permute-start(bf16[144,640]{1,0:T(8,128)(2,1)S(1)} %get-tuple-element.57.refs_13_), channel_id=1, source_target_pairs={{0,6},{1,7},{2,0},{3,1},{4,2},{5,3},{6,4},{7,5},{8,14},{9,15},{10,... | collective-permute-start | bytes 552968 | tf_op jit(solution)/shard_map/ppermute | solution.py:616
  23.0 0.0 copy-done
  23.0 0.0 copy-done.7
  23.0 5.2 %prompt_within.1 = (f32[8,256,640]{2,1,0:T(8,128)S(1)}, f32[8,256,640]{2,1,0:T(8,128)S(1)}) custom-call(s32[6]{0:T(128)S(1)} %stack.19.refs_0_, bf16[4,256,640]{2,1,0:T(8,128)(2,1)S(1)} %get-tuple-element.45.refs_1_, bf16[4,256,640]{2,1,0:T(8,128)(2,1)S(1)} %get-tuple-element.48.refs_2_, bf16[256,5120]{1,0:T(8,128)(2,1)S(1)} %copy-done, ...), custom_call_target="tpu_custom_call" | custom-call | flops 1 | bytes 1 | tf_op jit(solution)/shard_map/prompt_within/pallas_call | solution.py:49
  28.2 0.0 collective-permute-done.2.refs_2_.refs_6_
  28.3 2.1 %collective-permute-done.4.refs_4_.refs_8_ = bf16[144,640]{1,0:T(8,128)(2,1)S(1)} collective-permute-done((bf16[144,640]{1,0:T(8,128)(2,1)S(1)}, bf16[144,640]{1,0:T(8,128)(2,1)S(1)}, u32[]{:S(2)}, u32[]{:S(2)}) %collective-permute-start.4) | collective-permute-done | bytes 184352 | tf_op jit(solution)/shard_map/ppermute | solution.py:616
  30.4 0.0 collective-permute-done.3.refs_3_.refs_7_
  30.4 1.1 %row.1.refs_1_ = bf16[144,640]{1,0:T(8,128)(2,1)S(1)} custom-call(s32[6]{0:T(128)S(1)} %stack.19.refs_0_, bf16[144,640]{1,0:T(8,128)(2,1)S(1)} %get-tuple-element.60.refs_1_.refs_5_, bf16[144,640]{1,0:T(8,128)(2,1)S(1)} %collective-permute-done.2.refs_2_.refs_6_, bf16[144,640]{1,0:T(8,128)(2,1)S(1)} %collective-permute-done.3.refs_3_.refs_7_, ...), custom_call_target="tpu_custom_call" | custom-call | flops 1 | bytes 1 | tf_op jit(solution)/shard_map/row/pallas_call | solution.py:49
  31.5 0.0 copy-start.1
  31.5 0.0 copy-start.2
  31.5 0.0 copy-start.3
  31.5 0.0 copy-start.5
  31.5 0.0 copy-start.6
  31.5 4.4 %collective-permute-start.7 = (bf16[144,640]{1,0:T(8,128)(2,1)S(1)}, bf16[144,640]{1,0:T(8,128)(2,1)S(1)}, u32[]{:S(2)}, u32[]{:S(2)}) collective-permute-start(bf16[144,640]{1,0:T(8,128)(2,1)S(1)} %row.1.refs_1_), channel_id=1, source_target_pairs={{0,16},{1,17},{2,18},{3,19},{4,20},{5,21},{6,22},{7,23},{8,24},{9,... | collective-permute-start | bytes 552968 | tf_op jit(solution)/shard_map/ppermute | solution.py:616
  35.9 0.8 collective-permute-start.6
  36.7 0.7 collective-permute-start.5
  37.4 2.4 %collective-permute-done.7.refs_4_ = bf16[144,640]{1,0:T(8,128)(2,1)S(1)} collective-permute-done((bf16[144,640]{1,0:T(8,128)(2,1)S(1)}, bf16[144,640]{1,0:T(8,128)(2,1)S(1)}, u32[]{:S(2)}, u32[]{:S(2)}) %collective-permute-start.7) | collective-permute-done | bytes 184352 | tf_op jit(solution)/shard_map/ppermute | solution.py:616
  39.8 4.6 %collective-permute-done.6.refs_3_ = bf16[144,640]{1,0:T(8,128)(2,1)S(1)} collective-permute-done((bf16[144,640]{1,0:T(8,128)(2,1)S(1)}, bf16[144,640]{1,0:T(8,128)(2,1)S(1)}, u32[]{:S(2)}, u32[]{:S(2)}) %collective-permute-start.6) | collective-permute-done | bytes 184352 | tf_op jit(solution)/shard_map/ppermute | solution.py:616
  44.3 0.0 collective-permute-done.5.refs_2_
  44.3 2.2 %entering.1 = (bf16[144,640]{1,0:T(8,128)(2,1)S(1)}, bf16[144,640]{1,0:T(8,128)(2,1)S(1)}, bf16[144,640]{1,0:T(8,128)(2,1)S(1)}, bf16[144,640]{1,0:T(8,128)(2,1)...) custom-call(s32[6]{0:T(128)S(1)} %stack.19.refs_0_, bf16[144,640]{1,0:T(8,128)(2,1)S(1)} %row.1.refs_1_, ...), custom_call_target="tpu_custom_call" | custom-call | flops 1 | bytes 1 | tf_op jit(solution)/shard_map/entering/pallas_call | solution.py:49
  46.6 1.2 %collective-permute-start.8 = (bf16[144,640]{1,0:T(8,128)(2,1)S(1)}, bf16[144,640]{1,0:T(8,128)(2,1)S(1)}, u32[]{:S(2)}, u32[]{:S(2)}) collective-permute-start(bf16[144,640]{1,0:T(8,128)(2,1)S(1)} %get-tuple-element.62.refs_10_), channel_id=1, source_target_pairs={{0,2},{1,3},{2,4},{3,5},{4,6},{5,7},{6,0},{7,1},{8,10},{9,11},{10,... | collective-permute-start | bytes 552968 | tf_op jit(solution)/shard_map/ppermute | solution.py:616
  47.7 1.6 %collective-permute-start.14 = (bf16[16,640]{1,0:T(8,128)(2,1)S(1)}, bf16[16,640]{1,0:T(8,128)(2,1)S(1)}, u32[]{:S(2)}, u32[]{:S(2)}) collective-permute-start(bf16[16,640]{1,0:T(8,128)(2,1)S(1)} %get-tuple-element.66.refs_2_), channel_id=1, source_target_pairs={{0,1},{1,0},{2,3},{3,2},{4,5},{5,4},{6,7},{7,6},{8,9},{9,8},{10,11... | collective-permute-start | bytes 61448 | tf_op jit(solution)/shard_map/ppermute | solution.py:616
  49.3 2.1 %collective-permute-start.9 = (bf16[144,640]{1,0:T(8,128)(2,1)S(1)}, bf16[144,640]{1,0:T(8,128)(2,1)S(1)}, u32[]{:S(2)}, u32[]{:S(2)}) collective-permute-start(bf16[144,640]{1,0:T(8,128)(2,1)S(1)} %get-tuple-element.63.refs_12_), channel_id=1, source_target_pairs={{0,6},{1,7},{2,0},{3,1},{4,2},{5,3},{6,4},{7,5},{8,14},{9,15},{10,... | collective-permute-start | bytes 552968 | tf_op jit(solution)/shard_map/ppermute | solution.py:616
  51.4 1.2 %collective-permute-start.10 = (bf16[144,640]{1,0:T(8,128)(2,1)S(1)}, bf16[144,640]{1,0:T(8,128)(2,1)S(1)}, u32[]{:S(2)}, u32[]{:S(2)}) collective-permute-start(bf16[144,640]{1,0:T(8,128)(2,1)S(1)} %get-tuple-element.64.refs_11_), channel_id=1, source_target_pairs={{0,4},{1,5},{2,6},{3,7},{4,0},{5,1},{6,2},{7,3},{8,12},{9,13},{10,... | collective-permute-start | bytes 552968 | tf_op jit(solution)/shard_map/ppermute | solution.py:616
  52.6 1.8 %collective-permute-start.13 = (bf16[144,640]{1,0:T(8,128)(2,1)S(1)}, bf16[144,640]{1,0:T(8,128)(2,1)S(1)}, u32[]{:S(2)}, u32[]{:S(2)}) collective-permute-start(bf16[144,640]{1,0:T(8,128)(2,1)S(1)} %get-tuple-element.65.refs_5_), channel_id=1, source_target_pairs={{0,4},{1,5},{2,6},{3,7},{4,0},{5,1},{6,2},{7,3},{8,12},{9,13},{10,... | collective-permute-start | bytes 552968 | tf_op jit(solution)/shard_map/ppermute | solution.py:616
  54.4 0.0 collective-permute-done.14.refs_3_
  54.4 1.5 %collective-permute-start.12 = (bf16[144,640]{1,0:T(8,128)(2,1)S(1)}, bf16[144,640]{1,0:T(8,128)(2,1)S(1)}, u32[]{:S(2)}, u32[]{:S(2)}) collective-permute-start(bf16[144,640]{1,0:T(8,128)(2,1)S(1)} %get-tuple-element.65.refs_5_), channel_id=1, source_target_pairs={{0,6},{1,7},{2,0},{3,1},{4,2},{5,3},{6,4},{7,5},{8,14},{9,15},{10,... | collective-permute-start | bytes 552968 | tf_op jit(solution)/shard_map/ppermute | solution.py:616
  55.8 0.0 collective-permute-done.8.refs_2_
  55.8 0.0 collective-permute-start.11
  55.8 0.0 copy-done.1
  55.8 0.0 copy-done.2
  55.9 0.0 copy-done.3
  55.9 0.0 copy-done.5
  55.9 0.0 copy-done.6
  55.9 5.0 %resp_within.1 = (f32[8,128,640]{2,1,0:T(8,128)S(1)}, f32[8,128,640]{2,1,0:T(8,128)S(1)}, bf16[128,256]{1,0:T(8,128)(2,1)S(1)}) custom-call(s32[6]{0:T(128)S(1)} %stack.19.refs_0_, bf16[128,5376]{1,0:T(8,128)(2,1)S(1)} %bitcast.11, bf16[16,640]{1,0:T(8,128)(2,1)S(1)} %get-tuple-element.66.refs_2_, bf16[16,640]{1,0:T(8,128)(2,1)S(1)} %collective-permute-done.14.refs_3_, ...), custom_call_target="tpu_custom_call" | custom-call | flops 1 | bytes 1 | tf_op jit(solution)/shard_map/resp_within/pallas_call | solution.py:49
  60.9 0.0 collective-permute-done.9.refs_3_
  60.9 0.0 collective-permute-done.10.refs_4_
  60.9 2.7 %collective-permute-done.13.refs_8_ = bf16[144,640]{1,0:T(8,128)(2,1)S(1)} collective-permute-done((bf16[144,640]{1,0:T(8,128)(2,1)S(1)}, bf16[144,640]{1,0:T(8,128)(2,1)S(1)}, u32[]{:S(2)}, u32[]{:S(2)}) %collective-permute-start.13) | collective-permute-done | bytes 184352 | tf_op jit(solution)/shard_map/ppermute | solution.py:616
  63.6 3.9 %collective-permute-done.12.refs_7_ = bf16[144,640]{1,0:T(8,128)(2,1)S(1)} collective-permute-done((bf16[144,640]{1,0:T(8,128)(2,1)S(1)}, bf16[144,640]{1,0:T(8,128)(2,1)S(1)}, u32[]{:S(2)}, u32[]{:S(2)}) %collective-permute-start.12) | collective-permute-done | bytes 184352 | tf_op jit(solution)/shard_map/ppermute | solution.py:616
  67.5 0.3 collective-permute-done.11.refs_6_
  67.8 2.0 %cores.1 = (bf16[4,256,640]{2,1,0:T(8,128)(2,1)S(1)}, bf16[4,256,640]{2,1,0:T(8,128)(2,1)S(1)}, bf16[4,256,640]{2,1,0:T(8,128)(2,1)S(1)}) custom-call(s32[6]{0:T(128)S(1)} %stack.19.refs_0_, bf16[144,640]{1,0:T(8,128)(2,1)S(1)} %get-tuple-element.61.refs_1_, bf16[144,640]{1,0:T(8,128)(2,1)S(1)} %collective-permute-done.8.refs_2_, ...), custom_call_target="tpu_custom_call" | custom-call | flops 1 | bytes 1 | tf_op jit(solution)/shard_map/cores/pallas_call | solution.py:49
  69.9 0.6 collective-permute-start.15
  70.4 0.1 collective-permute-start.16
  70.5 1.3 %prompt_own_half.1 = (f32[4,256,640]{2,1,0:T(8,128)S(1)}, f32[256,128]{1,0:T(8,128)S(1)}) custom-call(s32[6]{0:T(128)S(1)} %stack.19.refs_0_, f32[8,256,640]{2,1,0:T(8,128)S(1)} %get-tuple-element.58.refs_5_.refs_9_.refs_14_.refs_1_, f32[8,256,640]{2,1,0:T(8,128)S(1)} %get-tuple-element.59.refs_6_.refs_10_.refs_15_.refs_2_, ...), custom_call_target="tpu_custom_call" | custom-call | flops 1 | bytes 1 | tf_op jit(solution)/shard_map/prompt_own_half/pallas_call | solution.py:49
  71.9 0.0 copy-start.4
  71.9 0.9 %resp_own_half.1 = (f32[4,128,640]{2,1,0:T(8,128)S(1)}, f32[128,128]{1,0:T(8,128)S(1)}) custom-call(s32[6]{0:T(128)S(1)} %stack.19.refs_0_, f32[8,128,640]{2,1,0:T(8,128)S(1)} %get-tuple-element.67.refs_12_.refs_1_, f32[8,128,640]{2,1,0:T(8,128)S(1)} %get-tuple-element.68.refs_13_.refs_2_, bf16[128,256]{1,0:T(8,128)(2,1)S(1)} %get-tuple-element.73.refs_3_, ...), custom_call_target="tpu_custom_call" | custom-call | flops 1 | bytes 1 | tf_op jit(solution)/shard_map/resp_own_half/pallas_call | solution.py:49
  72.8 0.3 collective-permute-done.15.refs_4_
  73.1 3.2 %prompt_finish.1 = (bf16[256,5120]{1,0:T(8,128)(2,1)}, f32[8,128]{1,0:T(8,128)S(1)}) custom-call(s32[6]{0:T(128)S(1)} %stack.19.refs_0_, f32[8,256,640]{2,1,0:T(8,128)S(1)} %get-tuple-element.58.refs_5_.refs_9_.refs_14_.refs_1_, f32[8,256,640]{2,1,0:T(8,128)S(1)} %get-tuple-element.59.refs_6_.refs_10_.refs_15_.refs_2_, ...), custom_call_target="tpu_custom_call" | custom-call | flops 1 | bytes 1 | tf_op jit(solution)/shard_map/prompt_finish/pallas_call | solution.py:589
  76.3 0.0 collective-permute-done.16.refs_4_
  76.3 2.9 %resp_finish.1 = (bf16[128,5120]{1,0:T(8,128)(2,1)}, f32[8,128]{1,0:T(8,128)}) custom-call(s32[6]{0:T(128)S(1)} %stack.19.refs_0_, f32[8,128,640]{2,1,0:T(8,128)S(1)} %get-tuple-element.67.refs_12_.refs_1_, f32[8,128,640]{2,1,0:T(8,128)S(1)} %get-tuple-element.68.refs_13_.refs_2_, bf16[128,256]{1,0:T(8,128)(2,1)S(1)} %get-tuple-element.73.refs_3_, ...), custom_call_target="tpu_custom_call" | custom-call | flops 1 | bytes 1 | tf_op jit(solution)/shard_map/resp_finish/pallas_call | solution.py:589
  (4 shorter events, 0.0 us)
Async XLA Ops:
  1.5 7.8 %collective-permute-start = (bf16[8,5376]{1,0:T(8,128)(2,1)S(1)}, bf16[8,5376]{1,0:T(8,128)(2,1)S(1)}, u32[]{:S(2)}, u32[]{:S(2)}) collective-permute-start(bf16[8,5376]{1,0:T(8,128)(2,1)S(1)} %slice.3.refs_5_.refs_4_), channel_id=1, source_target_pairs={{0,1},{1,2},{2,3},{3,4},{4,5},{5,6},{6,7},{7,8},{8,9},{9,10},{10,1... | collective-permute-start | bytes 258056 | tf_op jit(solution)/shard_map/ppermute | solution.py:708
  6.8 2.5 %copy-start.8 = (f32[5376]{0:T(1024)S(1)}, f32[5376]{0:T(1024)}, u32[]{:S(2)}) copy-start(f32[5376]{0:T(1024)} %param.23) | copy-start | bytes 64516
  13.5 4.0 %collective-permute-start.1 = (bf16[4,144,640]{2,1,0:T(8,128)(2,1)S(1)}, bf16[4,144,640]{2,1,0:T(8,128)(2,1)S(1)}, u32[]{:S(2)}, u32[]{:S(2)}) collective-permute-start(bf16[4,144,640]{2,1,0:T(8,128)(2,1)S(1)} %get-tuple-element.47.refs_8_), channel_id=1, source_target_pairs={{0,1},{1,0},{2,3},{3,2},{4,5},{5,4},{6,7},{7,6},{8,9},{9,8},{10,11... | collective-permute-start | bytes 2211848 | tf_op jit(solution)/shard_map/ppermute | solution.py:616
  13.6 9.4 %copy-start = (bf16[256,5120]{1,0:T(8,128)(2,1)S(1)}, bf16[256,5120]{1,0:T(8,128)(2,1)}, u32[]{:S(2)}) copy-start(bf16[256,5120]{1,0:T(8,128)(2,1)} %refs_3_.3) | copy-start | bytes 7864324
  17.5 5.5 %copy-start.7 = (f32[80]{0:T(128)S(1)}, f32[80]{0:T(128)}, u32[]{:S(2)}) copy-start(f32[80]{0:T(128)} %param.24) | copy-start | bytes 964
  18.4 9.8 %collective-permute-start.2 = (bf16[144,640]{1,0:T(8,128)(2,1)S(1)}, bf16[144,640]{1,0:T(8,128)(2,1)S(1)}, u32[]{:S(2)}, u32[]{:S(2)}) collective-permute-start(bf16[144,640]{1,0:T(8,128)(2,1)S(1)} %get-tuple-element.55.refs_11_), channel_id=1, source_target_pairs={{0,2},{1,3},{2,4},{3,5},{4,6},{5,7},{6,0},{7,1},{8,10},{9,11},{10,... | collective-permute-start | bytes 552968 | tf_op jit(solution)/shard_map/ppermute | solution.py:616
  19.7 10.7 %collective-permute-start.4 = (bf16[144,640]{1,0:T(8,128)(2,1)S(1)}, bf16[144,640]{1,0:T(8,128)(2,1)S(1)}, u32[]{:S(2)}, u32[]{:S(2)}) collective-permute-start(bf16[144,640]{1,0:T(8,128)(2,1)S(1)} %get-tuple-element.56.refs_12_), channel_id=1, source_target_pairs={{0,4},{1,5},{2,6},{3,7},{4,0},{5,1},{6,2},{7,3},{8,12},{9,13},{10,... | collective-permute-start | bytes 552968 | tf_op jit(solution)/shard_map/ppermute | solution.py:616
  22.2 8.2 %collective-permute-start.3 = (bf16[144,640]{1,0:T(8,128)(2,1)S(1)}, bf16[144,640]{1,0:T(8,128)(2,1)S(1)}, u32[]{:S(2)}, u32[]{:S(2)}) collective-permute-start(bf16[144,640]{1,0:T(8,128)(2,1)S(1)} %get-tuple-element.57.refs_13_), channel_id=1, source_target_pairs={{0,6},{1,7},{2,0},{3,1},{4,2},{5,3},{6,4},{7,5},{8,14},{9,15},{10,... | collective-permute-start | bytes 552968 | tf_op jit(solution)/shard_map/ppermute | solution.py:616
  31.5 24.4 %copy-start.1 = (bf16[1,128,5376]{2,1,0:T(8,128)(2,1)S(1)}, bf16[1,128,5376]{2,1,0:T(8,128)(2,1)}, u32[]{:S(2)}) copy-start(bf16[1,128,5376]{2,1,0:T(8,128)(2,1)} %param.17) | copy-start | bytes 4128772
  31.5 24.4 %copy-start.2 = (bf16[1,128,5120]{2,1,0:T(8,128)(2,1)S(1)}, bf16[1,128,5120]{2,1,0:T(8,128)(2,1)}, u32[]{:S(2)}) copy-start(bf16[1,128,5120]{2,1,0:T(8,128)(2,1)} %param.18) | copy-start | bytes 3932164
  31.5 24.4 %copy-start.3 = (f32[4,5376]{1,0:T(4,128)S(1)}, f32[4,5376]{1,0:T(4,128)}, u32[]{:S(2)}) copy-start(f32[4,5376]{1,0:T(4,128)} %refs_4_.3) | copy-start | bytes 258052
  31.5 24.4 %copy-start.5 = (f32[80,1,128]{2,1,0:T(1,128)S(1)}, f32[80,1,128]{2,1,0:T(1,128)}, u32[]{:S(2)}) copy-start(f32[80,1,128]{2,1,0:T(1,128)} %param.20) | copy-start | bytes 122884
  31.5 24.4 %copy-start.6 = (f32[80,1,128]{2,1,0:T(1,128)S(1)}, f32[80,1,128]{2,1,0:T(1,128)}, u32[]{:S(2)}) copy-start(f32[80,1,128]{2,1,0:T(1,128)} %param.19) | copy-start | bytes 122884
  31.5 8.3 %collective-permute-start.7 = (bf16[144,640]{1,0:T(8,128)(2,1)S(1)}, bf16[144,640]{1,0:T(8,128)(2,1)S(1)}, u32[]{:S(2)}, u32[]{:S(2)}) collective-permute-start(bf16[144,640]{1,0:T(8,128)(2,1)S(1)} %row.1.refs_1_), channel_id=1, source_target_pairs={{0,16},{1,17},{2,18},{3,19},{4,20},{5,21},{6,22},{7,23},{8,24},{9,... | collective-permute-start | bytes 552968 | tf_op jit(solution)/shard_map/ppermute | solution.py:616
  35.9 8.4 %collective-permute-start.6 = (bf16[144,640]{1,0:T(8,128)(2,1)S(1)}, bf16[144,640]{1,0:T(8,128)(2,1)S(1)}, u32[]{:S(2)}, u32[]{:S(2)}) collective-permute-start(bf16[144,640]{1,0:T(8,128)(2,1)S(1)} %row.1.refs_1_), channel_id=1, source_target_pairs={{0,24},{1,25},{2,26},{3,27},{4,28},{5,29},{6,30},{7,31},{8,0},{9,1... | collective-permute-start | bytes 552968 | tf_op jit(solution)/shard_map/ppermute | solution.py:616
  36.7 7.6 %collective-permute-start.5 = (bf16[144,640]{1,0:T(8,128)(2,1)S(1)}, bf16[144,640]{1,0:T(8,128)(2,1)S(1)}, u32[]{:S(2)}, u32[]{:S(2)}) collective-permute-start(bf16[144,640]{1,0:T(8,128)(2,1)S(1)} %row.1.refs_1_), channel_id=1, source_target_pairs={{0,8},{1,9},{2,10},{3,11},{4,12},{5,13},{6,14},{7,15},{8,16},{9,17... | collective-permute-start | bytes 552968 | tf_op jit(solution)/shard_map/ppermute | solution.py:616
  46.6 9.3 %collective-permute-start.8 = (bf16[144,640]{1,0:T(8,128)(2,1)S(1)}, bf16[144,640]{1,0:T(8,128)(2,1)S(1)}, u32[]{:S(2)}, u32[]{:S(2)}) collective-permute-start(bf16[144,640]{1,0:T(8,128)(2,1)S(1)} %get-tuple-element.62.refs_10_), channel_id=1, source_target_pairs={{0,2},{1,3},{2,4},{3,5},{4,6},{5,7},{6,0},{7,1},{8,10},{9,11},{10,... | collective-permute-start | bytes 552968 | tf_op jit(solution)/shard_map/ppermute | solution.py:616
  47.7 6.7 %collective-permute-start.14 = (bf16[16,640]{1,0:T(8,128)(2,1)S(1)}, bf16[16,640]{1,0:T(8,128)(2,1)S(1)}, u32[]{:S(2)}, u32[]{:S(2)}) collective-permute-start(bf16[16,640]{1,0:T(8,128)(2,1)S(1)} %get-tuple-element.66.refs_2_), channel_id=1, source_target_pairs={{0,1},{1,0},{2,3},{3,2},{4,5},{5,4},{6,7},{7,6},{8,9},{9,8},{10,11... | collective-permute-start | bytes 61448 | tf_op jit(solution)/shard_map/ppermute | solution.py:616
  49.3 11.5 %collective-permute-start.9 = (bf16[144,640]{1,0:T(8,128)(2,1)S(1)}, bf16[144,640]{1,0:T(8,128)(2,1)S(1)}, u32[]{:S(2)}, u32[]{:S(2)}) collective-permute-start(bf16[144,640]{1,0:T(8,128)(2,1)S(1)} %get-tuple-element.63.refs_12_), channel_id=1, source_target_pairs={{0,6},{1,7},{2,0},{3,1},{4,2},{5,3},{6,4},{7,5},{8,14},{9,15},{10,... | collective-permute-start | bytes 552968 | tf_op jit(solution)/shard_map/ppermute | solution.py:616
  51.4 9.5 %collective-permute-start.10 = (bf16[144,640]{1,0:T(8,128)(2,1)S(1)}, bf16[144,640]{1,0:T(8,128)(2,1)S(1)}, u32[]{:S(2)}, u32[]{:S(2)}) collective-permute-start(bf16[144,640]{1,0:T(8,128)(2,1)S(1)} %get-tuple-element.64.refs_11_), channel_id=1, source_target_pairs={{0,4},{1,5},{2,6},{3,7},{4,0},{5,1},{6,2},{7,3},{8,12},{9,13},{10,... | collective-permute-start | bytes 552968 | tf_op jit(solution)/shard_map/ppermute | solution.py:616
  52.6 11.0 %collective-permute-start.13 = (bf16[144,640]{1,0:T(8,128)(2,1)S(1)}, bf16[144,640]{1,0:T(8,128)(2,1)S(1)}, u32[]{:S(2)}, u32[]{:S(2)}) collective-permute-start(bf16[144,640]{1,0:T(8,128)(2,1)S(1)} %get-tuple-element.65.refs_5_), channel_id=1, source_target_pairs={{0,4},{1,5},{2,6},{3,7},{4,0},{5,1},{6,2},{7,3},{8,12},{9,13},{10,... | collective-permute-start | bytes 552968 | tf_op jit(solution)/shard_map/ppermute | solution.py:616
  54.4 13.1 %collective-permute-start.12 = (bf16[144,640]{1,0:T(8,128)(2,1)S(1)}, bf16[144,640]{1,0:T(8,128)(2,1)S(1)}, u32[]{:S(2)}, u32[]{:S(2)}) collective-permute-start(bf16[144,640]{1,0:T(8,128)(2,1)S(1)} %get-tuple-element.65.refs_5_), channel_id=1, source_target_pairs={{0,6},{1,7},{2,0},{3,1},{4,2},{5,3},{6,4},{7,5},{8,14},{9,15},{10,... | collective-permute-start | bytes 552968 | tf_op jit(solution)/shard_map/ppermute | solution.py:616
  55.8 12.0 %collective-permute-start.11 = (bf16[144,640]{1,0:T(8,128)(2,1)S(1)}, bf16[144,640]{1,0:T(8,128)(2,1)S(1)}, u32[]{:S(2)}, u32[]{:S(2)}) collective-permute-start(bf16[144,640]{1,0:T(8,128)(2,1)S(1)} %get-tuple-element.65.refs_5_), channel_id=1, source_target_pairs={{0,2},{1,3},{2,4},{3,5},{4,6},{5,7},{6,0},{7,1},{8,10},{9,11},{10,... | collective-permute-start | bytes 552968 | tf_op jit(solution)/shard_map/ppermute | solution.py:616
  69.9 3.2 %collective-permute-start.15 = (bf16[4,256,640]{2,1,0:T(8,128)(2,1)S(1)}, bf16[4,256,640]{2,1,0:T(8,128)(2,1)S(1)}, u32[]{:S(2)}, u32[]{:S(2)}) collective-permute-start(bf16[4,256,640]{2,1,0:T(8,128)(2,1)S(1)} %get-tuple-element.69.refs_5_), channel_id=1, source_target_pairs={{0,1},{1,0},{2,3},{3,2},{4,5},{5,4},{6,7},{7,6},{8,9},{9,8},{10,11... | collective-permute-start | bytes 3932168 | tf_op jit(solution)/shard_map/ppermute | solution.py:616
  70.4 5.9 %collective-permute-start.16 = (bf16[4,256,640]{2,1,0:T(8,128)(2,1)S(1)}, bf16[4,256,640]{2,1,0:T(8,128)(2,1)S(1)}, u32[]{:S(2)}, u32[]{:S(2)}) collective-permute-start(bf16[4,256,640]{2,1,0:T(8,128)(2,1)S(1)} %get-tuple-element.74.refs_4_), channel_id=1, source_target_pairs={{0,1},{1,0},{2,3},{3,2},{4,5},{5,4},{6,7},{7,6},{8,9},{9,8},{10,11... | collective-permute-start | bytes 3932168 | tf_op jit(solution)/shard_map/ppermute | solution.py:616
  71.9 1.2 %copy-start.4 = (f32[5120]{0:T(1024)S(1)}, f32[5120]{0:T(1024)}, u32[]{:S(2)}) copy-start(f32[5120]{0:T(1024)} %param.25) | copy-start | bytes 61444

commit v5 on v4

--- a/solution.py
+++ b/solution.py
@@ -485,25 +485,31 @@
 
 
 def cores_kernel(
-    where_ref, g0, g1, g3, g2, f0, f1, f3, f2, own_ref, recv_ref, hcol_ref, mine_ref, send_ref, final_ref
+    where_ref, g0, g1, g3, g2, own_ref, recv_ref, hcol_ref, mine_ref, send_ref
 ):
     x, core = where_ref[0], where_ref[2]
     first = (core == 0).astype(F32)
     last = 1.0 - first
-    for i, (ref, passed_ref) in enumerate(zip((g0, g1, g2, g3), (f0, f1, f2, f3))):
+    for i, ref in enumerate((g0, g1, g2, g3)):
         slab = at_shift(x, -i)
         half = hcol_ref[core * 4 + slab]
         mine = (half[0:1] * half[1:2]) ** 2
         decay = mine * first + decay_of(recv_ref[slab, STATE:, :]) * last
         along, factor = uncoded(ref)
-        final_along, final_factor = uncoded(passed_ref)
         for cols in CHUNKS:
-            put_pair(final_ref, slab, cols, joined(passed_ref, final_along, final_factor, cols))
             earlier = own_ref[slab, :, cols] * first + recv_ref[slab, 0:STATE, cols].astype(F32) * last
             start = joined(ref, along, factor, cols)
             later = decay[:, cols] * start + earlier
             put_pair(mine_ref, slab, cols, start * first + later * last)
             put_pair(send_ref, slab, cols, later * first + start * last)
+
+
+def final_kernel(where_ref, f0, f1, f3, f2, final_ref):
+    for i, ref in enumerate((f0, f1, f2, f3)):
+        slab = at_shift(where_ref[0], -i)
+        along, factor = uncoded(ref)
+        for cols in CHUNKS:
+            put_pair(final_ref, slab, cols, joined(ref, along, factor, cols))
 
 
 TILE = 128
@@ -736,21 +742,18 @@
         resp_keep.reshape(HEADS, BLOCK), resp_step.reshape(HEADS, BLOCK), skip_row, after=(e1, e2, e3),
     )
     four = ((4, 2 * STATE, SLAB), BF16)
-    mine, send, final_mine = whole(
-        cores_kernel,
-        where,
-        back + finals + (own, recv, hcol),
-        [four] * 3,
-        "cores",
-        after=(resp_part, resp_gate, part, gate),
-    )
-    other, final_other = swap_cores(send), swap_cores(final_mine)
+    mine, send = whole(
+        cores_kernel, where, back + (own, recv, hcol), [four] * 2, "cores", after=(resp_part, resp_gate, part, gate)
+    )
+    other = swap_cores(send)
     gated, squares = own_half(where, part, gate, kq, mine, "prompt_own_half", after=(send,))
+    (final_mine,) = whole(final_kernel, where, finals, [four], "final", after=(squares,))
+    final_other = swap_cores(final_mine)
+    prompt_out, token = finish(
+        where, part, gate, kq, other, gated, squares, gain_row, 4, "prompt_finish", after=(final_mine,)
+    )
     resp_gated, resp_squares = own_half(
-        where, resp_part, resp_gate, resp_kq, final_mine, "resp_own_half", after=(squares,)
-    )
-    prompt_out, token = finish(
-        where, part, gate, kq, other, gated, squares, gain_row, 4, "prompt_finish", after=(resp_squares,)
+        where, resp_part, resp_gate, resp_kq, final_mine, "resp_own_half", after=(token,)
     )
     resp_out, _ = finish(
         where, resp_part, resp_gate, resp_kq, final_other, resp_gated, resp_squares, gain_row, 5, "resp_finish",

time: 79.5 us -> 76.7 us (0.965)
  waiting for transfers between devices: 16.3 us -> 9.28 us
  starting transfers between devices: 25.1 us -> 28.7 us
    ppermute x16, waiting for transfers between devices: 16.3 us -> 9.28 us  [moved(): return lax.ppermute(value, GROUP, pairs)]
    ppermute x16, starting transfers between devices: 20.6 us -> 24.2 us  [moved(): return lax.ppermute(value, GROUP, pairs)]
    pallas_call x11 -> x12, Pallas kernels: 29.2 us -> 29.8 us  [whole(): pl.pallas_call(ordered(kernel, 1 + len(arrays), len(after)), in_specs=[SM...]
  transfers between devices with their start and end apart: 17 -> 17, of which waited for: 7 -> 4; matrix products, arithmetic and copies ran while one was open for 0% -> 0% of each run, Pallas kernels for 28% -> 32%
where the time goes in v5:
time: 76.7 us; the launch traced here: 76.6 us
  Pallas kernels  35.8 us (47%)
  starting transfers between devices  28.7 us (37%)
  waiting for transfers between devices  9.28 us (12%)
  between operations  1.73 us (2%)
  local copies, waits for them, and re-layouts  1.05 us (1%)
    pallas_call x12, Pallas kernels, whole(): pl.pallas_call(ordered(kernel, 1 + len(arrays), len(after)), in_specs=[SM...  29.8 us
    ppermute x16, starting transfers between devices, moved(): return lax.ppermute(value, GROUP, pairs)  24.2 us
    ppermute x16, waiting for transfers between devices, moved(): return lax.ppermute(value, GROUP, pairs)  9.28 us
    pallas_call x2, Pallas kernels, finish(): pl.pallas_call(ordered(functools.partial(finish_kernel, length_at), 8, le...  6.06 us
    ppermute x1, starting transfers between devices, shards(): hist = lax.ppermute(own_rows, GROUP, [(i, i + 1) for i in range(count - 1)])  4.5 us
  transfers between devices with their start and end apart: 17, of which 4 were waited for; matrix products, arithmetic and copies ran while one was open for 0% of the time, Pallas kernels for 32%

profile of v5, /device:TPU:1, one launch (start us, length us, event | category | flops | bytes accessed | tf_op | source)
XLA Modules:
  0.0 76.6 jit_solution(10861545142240841952)
XLA Ops:
  0.6 0.9 %slice.3.refs_5_.refs_4_ = bf16[8,5376]{1,0:T(8,128)(2,1)S(1)} slice(bf16[256,5376]{1,0:T(8,128)(2,1)} %refs_3_.2), slice={[248:256], [0:5376]} | slice | bytes 172032 | tf_op jit(solution)/shard_map/slice | solution.py:712
  1.5 4.5 %collective-permute-start = (bf16[8,5376]{1,0:T(8,128)(2,1)S(1)}, bf16[8,5376]{1,0:T(8,128)(2,1)S(1)}, u32[]{:S(2)}, u32[]{:S(2)}) collective-permute-start(bf16[8,5376]{1,0:T(8,128)(2,1)S(1)} %slice.3.refs_5_.refs_4_), channel_id=1, source_target_pairs={{0,1},{1,2},{2,3},{3,4},{4,5},{5,6},{6,7},{7,8},{8,9},{9,10},{10,1... | collective-permute-start | bytes 258056 | tf_op jit(solution)/shard_map/ppermute | solution.py:714
  6.7 0.1 stack.19.refs_0_
  6.8 2.5 %tables.1 = (f32[2,80,128]{2,1,0:T(8,128)S(1)}, f32[2,128,128]{2,1,0:T(8,128)S(1)}, f32[2,128,128]{2,1,0:T(8,128)S(1)}, f32[8,8,640]{2,1,0:T(8,128)S(1)}, bf16[2...) custom-call(s32[6]{0:T(128)S(1)} %stack.19.refs_0_, f32[80,256]{1,0:T(8,128)} %refs_1_.1, f32[80,256]{1,0:T(8,128)} %refs_2_.1, ...), custom_call_target="tpu_custom_call" | custom-call | flops 1 | bytes 1 | tf_op jit(solution)/shard_map/tables/pallas_call | solution.py:49
  9.3 0.0 copy-done.8
  9.3 0.0 collective-permute-done.refs_3_
  9.3 4.2 %sent_states.1 = (bf16[4,256,640]{2,1,0:T(8,128)(2,1)S(1)}, bf16[256,256]{1,0:T(8,128)(2,1)S(1)}, bf16[128,256]{1,0:T(8,128)(2,1)S(1)}, bf16[4,128,640]{2,1,0:T(8,128)(2,1)S(1)}, bf16[4,144,640]{2,1,0:T(8,128)(2,1)S(1)}) custom-call(s32[6]{0:T(128)S(1)} %stack.19.refs_0_, bf16[256,5376]{1,0:T(8,128)(2,1)S(1)} %get-tuple-element.40.refs_1_, ...), custom_call_target="tpu_custom_call" | custom-call | flops 1 | bytes 1 | tf_op jit(solution)/shard_map/sent_states/pallas_call | solution.py:49
  13.5 0.1 collective-permute-start.1
  13.6 3.9 %kept_states.1 = (bf16[4,256,640]{2,1,0:T(8,128)(2,1)S(1)}, bf16[4,128,640]{2,1,0:T(8,128)(2,1)S(1)}, f32[4,128,640]{2,1,0:T(8,128)S(1)}) custom-call(s32[6]{0:T(128)S(1)} %stack.19.refs_0_, bf16[256,5376]{1,0:T(8,128)(2,1)S(1)} %get-tuple-element.40.refs_1_, f32[4,5376]{1,0:T(4,128)S(1)} %get-tuple-element.41.refs_2_, ...), custom_call_target="tpu_custom_call" | custom-call | flops 1 | bytes 1 | tf_op jit(solution)/shard_map/kept_states/pallas_call | solution.py:49
  17.5 0.0 copy-start.7
  17.5 0.0 collective-permute-done.1.refs_2_.refs_6_
  17.5 0.9 %chip.1 = (bf16[144,640]{1,0:T(8,128)(2,1)S(1)}, bf16[144,640]{1,0:T(8,128)(2,1)S(1)}, bf16[144,640]{1,0:T(8,128)(2,1)S(1)}, bf16[144,640]{1,0:T(8,128)(2,1)S(1)}) custom-call(s32[6]{0:T(128)S(1)} %stack.19.refs_0_, f32[4,128,640]{2,1,0:T(8,128)S(1)} %get-tuple-element.53.refs_1_.refs_5_, bf16[4,144,640]{2,1,0:T(8,128)(2,1)S(1)} %collective-permute-done.1.refs_2_.refs_6_, ...), custom_call_target="tpu_custom_call" | custom-call | flops 1 | bytes 1 | tf_op jit(solution)/shard_map/chip/pallas_call | solution.py:49
  18.4 1.3 %collective-permute-start.2 = (bf16[144,640]{1,0:T(8,128)(2,1)S(1)}, bf16[144,640]{1,0:T(8,128)(2,1)S(1)}, u32[]{:S(2)}, u32[]{:S(2)}) collective-permute-start(bf16[144,640]{1,0:T(8,128)(2,1)S(1)} %get-tuple-element.54.refs_11_), channel_id=1, source_target_pairs={{0,2},{1,3},{2,4},{3,5},{4,6},{5,7},{6,0},{7,1},{8,10},{9,11},{10,... | collective-permute-start | bytes 552968 | tf_op jit(solution)/shard_map/ppermute | solution.py:622
  19.7 2.5 %collective-permute-start.4 = (bf16[144,640]{1,0:T(8,128)(2,1)S(1)}, bf16[144,640]{1,0:T(8,128)(2,1)S(1)}, u32[]{:S(2)}, u32[]{:S(2)}) collective-permute-start(bf16[144,640]{1,0:T(8,128)(2,1)S(1)} %get-tuple-element.55.refs_12_), channel_id=1, source_target_pairs={{0,4},{1,5},{2,6},{3,7},{4,0},{5,1},{6,2},{7,3},{8,12},{9,13},{10,... | collective-permute-start | bytes 552968 | tf_op jit(solution)/shard_map/ppermute | solution.py:622
  22.2 0.9 %collective-permute-start.3 = (bf16[144,640]{1,0:T(8,128)(2,1)S(1)}, bf16[144,640]{1,0:T(8,128)(2,1)S(1)}, u32[]{:S(2)}, u32[]{:S(2)}) collective-permute-start(bf16[144,640]{1,0:T(8,128)(2,1)S(1)} %get-tuple-element.56.refs_13_), channel_id=1, source_target_pairs={{0,6},{1,7},{2,0},{3,1},{4,2},{5,3},{6,4},{7,5},{8,14},{9,15},{10,... | collective-permute-start | bytes 552968 | tf_op jit(solution)/shard_map/ppermute | solution.py:622
  23.0 0.0 copy-done
  23.0 0.0 copy-done.7
  23.0 5.2 %prompt_within.1 = (f32[8,256,640]{2,1,0:T(8,128)S(1)}, f32[8,256,640]{2,1,0:T(8,128)S(1)}) custom-call(s32[6]{0:T(128)S(1)} %stack.19.refs_0_, bf16[4,256,640]{2,1,0:T(8,128)(2,1)S(1)} %get-tuple-element.44.refs_1_, bf16[4,256,640]{2,1,0:T(8,128)(2,1)S(1)} %get-tuple-element.47.refs_2_, bf16[256,5120]{1,0:T(8,128)(2,1)S(1)} %copy-done, ...), custom_call_target="tpu_custom_call" | custom-call | flops 1 | bytes 1 | tf_op jit(solution)/shard_map/prompt_within/pallas_call | solution.py:49
  28.3 0.0 collective-permute-done.2.refs_2_.refs_6_
  28.3 2.1 %collective-permute-done.4.refs_4_.refs_8_ = bf16[144,640]{1,0:T(8,128)(2,1)S(1)} collective-permute-done((bf16[144,640]{1,0:T(8,128)(2,1)S(1)}, bf16[144,640]{1,0:T(8,128)(2,1)S(1)}, u32[]{:S(2)}, u32[]{:S(2)}) %collective-permute-start.4) | collective-permute-done | bytes 184352 | tf_op jit(solution)/shard_map/ppermute | solution.py:622
  30.4 0.0 collective-permute-done.3.refs_3_.refs_7_
  30.4 1.1 %row.1.refs_1_ = bf16[144,640]{1,0:T(8,128)(2,1)S(1)} custom-call(s32[6]{0:T(128)S(1)} %stack.19.refs_0_, bf16[144,640]{1,0:T(8,128)(2,1)S(1)} %get-tuple-element.59.refs_1_.refs_5_, bf16[144,640]{1,0:T(8,128)(2,1)S(1)} %collective-permute-done.2.refs_2_.refs_6_, bf16[144,640]{1,0:T(8,128)(2,1)S(1)} %collective-permute-done.3.refs_3_.refs_7_, ...), custom_call_target="tpu_custom_call" | custom-call | flops 1 | bytes 1 | tf_op jit(solution)/shard_map/row/pallas_call | solution.py:49
  31.5 0.0 copy-start.1
  31.5 0.0 copy-start.2
  31.5 0.0 copy-start.3
  31.5 0.0 copy-start.5
  31.5 0.0 copy-start.6
  31.5 4.4 %collective-permute-start.7 = (bf16[144,640]{1,0:T(8,128)(2,1)S(1)}, bf16[144,640]{1,0:T(8,128)(2,1)S(1)}, u32[]{:S(2)}, u32[]{:S(2)}) collective-permute-start(bf16[144,640]{1,0:T(8,128)(2,1)S(1)} %row.1.refs_1_), channel_id=1, source_target_pairs={{0,16},{1,17},{2,18},{3,19},{4,20},{5,21},{6,22},{7,23},{8,24},{9,... | collective-permute-start | bytes 552968 | tf_op jit(solution)/shard_map/ppermute | solution.py:622
  35.9 0.8 %collective-permute-start.6 = (bf16[144,640]{1,0:T(8,128)(2,1)S(1)}, bf16[144,640]{1,0:T(8,128)(2,1)S(1)}, u32[]{:S(2)}, u32[]{:S(2)}) collective-permute-start(bf16[144,640]{1,0:T(8,128)(2,1)S(1)} %row.1.refs_1_), channel_id=1, source_target_pairs={{0,24},{1,25},{2,26},{3,27},{4,28},{5,29},{6,30},{7,31},{8,0},{9,1... | collective-permute-start | bytes 552968 | tf_op jit(solution)/shard_map/ppermute | solution.py:622
  36.7 0.7 collective-permute-start.5
  37.4 2.4 %collective-permute-done.7.refs_4_ = bf16[144,640]{1,0:T(8,128)(2,1)S(1)} collective-permute-done((bf16[144,640]{1,0:T(8,128)(2,1)S(1)}, bf16[144,640]{1,0:T(8,128)(2,1)S(1)}, u32[]{:S(2)}, u32[]{:S(2)}) %collective-permute-start.7) | collective-permute-done | bytes 184352 | tf_op jit(solution)/shard_map/ppermute | solution.py:622
  39.8 4.6 %collective-permute-done.6.refs_3_ = bf16[144,640]{1,0:T(8,128)(2,1)S(1)} collective-permute-done((bf16[144,640]{1,0:T(8,128)(2,1)S(1)}, bf16[144,640]{1,0:T(8,128)(2,1)S(1)}, u32[]{:S(2)}, u32[]{:S(2)}) %collective-permute-start.6) | collective-permute-done | bytes 184352 | tf_op jit(solution)/shard_map/ppermute | solution.py:622
  44.3 0.0 collective-permute-done.5.refs_2_
  44.3 2.2 %entering.1 = (bf16[144,640]{1,0:T(8,128)(2,1)S(1)}, bf16[144,640]{1,0:T(8,128)(2,1)S(1)}, bf16[144,640]{1,0:T(8,128)(2,1)S(1)}, bf16[144,640]{1,0:T(8,128)(2,1)...) custom-call(s32[6]{0:T(128)S(1)} %stack.19.refs_0_, bf16[144,640]{1,0:T(8,128)(2,1)S(1)} %row.1.refs_1_, ...), custom_call_target="tpu_custom_call" | custom-call | flops 1 | bytes 1 | tf_op jit(solution)/shard_map/entering/pallas_call | solution.py:49
  46.6 1.2 %collective-permute-start.8 = (bf16[144,640]{1,0:T(8,128)(2,1)S(1)}, bf16[144,640]{1,0:T(8,128)(2,1)S(1)}, u32[]{:S(2)}, u32[]{:S(2)}) collective-permute-start(bf16[144,640]{1,0:T(8,128)(2,1)S(1)} %get-tuple-element.61.refs_10_), channel_id=1, source_target_pairs={{0,2},{1,3},{2,4},{3,5},{4,6},{5,7},{6,0},{7,1},{8,10},{9,11},{10,... | collective-permute-start | bytes 552968 | tf_op jit(solution)/shard_map/ppermute | solution.py:622
  47.7 1.6 %collective-permute-start.11 = (bf16[16,640]{1,0:T(8,128)(2,1)S(1)}, bf16[16,640]{1,0:T(8,128)(2,1)S(1)}, u32[]{:S(2)}, u32[]{:S(2)}) collective-permute-start(bf16[16,640]{1,0:T(8,128)(2,1)S(1)} %get-tuple-element.64.refs_2_), channel_id=1, source_target_pairs={{0,1},{1,0},{2,3},{3,2},{4,5},{5,4},{6,7},{7,6},{8,9},{9,8},{10,11... | collective-permute-start | bytes 61448 | tf_op jit(solution)/shard_map/ppermute | solution.py:622
  49.3 2.1 %collective-permute-start.9 = (bf16[144,640]{1,0:T(8,128)(2,1)S(1)}, bf16[144,640]{1,0:T(8,128)(2,1)S(1)}, u32[]{:S(2)}, u32[]{:S(2)}) collective-permute-start(bf16[144,640]{1,0:T(8,128)(2,1)S(1)} %get-tuple-element.62.refs_12_), channel_id=1, source_target_pairs={{0,6},{1,7},{2,0},{3,1},{4,2},{5,3},{6,4},{7,5},{8,14},{9,15},{10,... | collective-permute-start | bytes 552968 | tf_op jit(solution)/shard_map/ppermute | solution.py:622
  51.4 1.2 %collective-permute-start.10 = (bf16[144,640]{1,0:T(8,128)(2,1)S(1)}, bf16[144,640]{1,0:T(8,128)(2,1)S(1)}, u32[]{:S(2)}, u32[]{:S(2)}) collective-permute-start(bf16[144,640]{1,0:T(8,128)(2,1)S(1)} %get-tuple-element.63.refs_11_), channel_id=1, source_target_pairs={{0,4},{1,5},{2,6},{3,7},{4,0},{5,1},{6,2},{7,3},{8,12},{9,13},{10,... | collective-permute-start | bytes 552968 | tf_op jit(solution)/shard_map/ppermute | solution.py:622
  52.6 1.8 %collective-permute-start.15 = (bf16[144,640]{1,0:T(8,128)(2,1)S(1)}, bf16[144,640]{1,0:T(8,128)(2,1)S(1)}, u32[]{:S(2)}, u32[]{:S(2)}) collective-permute-start(bf16[144,640]{1,0:T(8,128)(2,1)S(1)} %get-tuple-element.71.refs_1_), channel_id=1, source_target_pairs={{0,4},{1,5},{2,6},{3,7},{4,0},{5,1},{6,2},{7,3},{8,12},{9,13},{10,... | collective-permute-start | bytes 552968 | tf_op jit(solution)/shard_map/ppermute | solution.py:622
  54.4 0.0 collective-permute-done.11.refs_3_
  54.4 1.5 %collective-permute-start.14 = (bf16[144,640]{1,0:T(8,128)(2,1)S(1)}, bf16[144,640]{1,0:T(8,128)(2,1)S(1)}, u32[]{:S(2)}, u32[]{:S(2)}) collective-permute-start(bf16[144,640]{1,0:T(8,128)(2,1)S(1)} %get-tuple-element.71.refs_1_), channel_id=1, source_target_pairs={{0,6},{1,7},{2,0},{3,1},{4,2},{5,3},{6,4},{7,5},{8,14},{9,15},{10,... | collective-permute-start | bytes 552968 | tf_op jit(solution)/shard_map/ppermute | solution.py:622
  55.8 0.0 collective-permute-done.8.refs_2_
  55.8 0.0 collective-permute-start.13
  55.8 0.0 copy-done.1
  55.8 0.0 copy-done.2
  55.9 0.0 copy-done.3
  55.9 0.0 copy-done.5
  55.9 5.0 %resp_within.1 = (f32[8,128,640]{2,1,0:T(8,128)S(1)}, f32[8,128,640]{2,1,0:T(8,128)S(1)}, bf16[128,256]{1,0:T(8,128)(2,1)S(1)}) custom-call(s32[6]{0:T(128)S(1)} %stack.19.refs_0_, bf16[128,5376]{1,0:T(8,128)(2,1)S(1)} %bitcast.11, bf16[16,640]{1,0:T(8,128)(2,1)S(1)} %get-tuple-element.64.refs_2_, bf16[16,640]{1,0:T(8,128)(2,1)S(1)} %collective-permute-done.11.refs_3_, ...), custom_call_target="tpu_custom_call" | custom-call | flops 1 | bytes 1 | tf_op jit(solution)/shard_map/resp_within/pallas_call | solution.py:49
  60.9 0.0 collective-permute-done.9.refs_3_
  60.9 0.0 collective-permute-done.10.refs_4_
  60.9 1.7 %cores.1 = (bf16[4,256,640]{2,1,0:T(8,128)(2,1)S(1)}, bf16[4,256,640]{2,1,0:T(8,128)(2,1)S(1)}) custom-call(s32[6]{0:T(128)S(1)} %stack.19.refs_0_, bf16[144,640]{1,0:T(8,128)(2,1)S(1)} %get-tuple-element.60.refs_1_, bf16[144,640]{1,0:T(8,128)(2,1)S(1)} %collective-permute-done.8.refs_2_, bf16[144,640]{1,0:T(8,128)(2,1)S(1)} %collective-permute-done.9.refs_3_, ...), custom_call_target="tpu_custom_call" | custom-call | flops 1 | bytes 1 | tf_op jit(solution)/shard_map/cores/pallas_call | solution.py:49
  62.6 3.7 %collective-permute-start.12 = (bf16[4,256,640]{2,1,0:T(8,128)(2,1)S(1)}, bf16[4,256,640]{2,1,0:T(8,128)(2,1)S(1)}, u32[]{:S(2)}, u32[]{:S(2)}) collective-permute-start(bf16[4,256,640]{2,1,0:T(8,128)(2,1)S(1)} %get-tuple-element.67.refs_5_), channel_id=1, source_target_pairs={{0,1},{1,0},{2,3},{3,2},{4,5},{5,4},{6,7},{7,6},{8,9},{9,8},{10,11... | collective-permute-start | bytes 3932168 | tf_op jit(solution)/shard_map/ppermute | solution.py:622
  66.3 1.3 %prompt_own_half.1 = (f32[4,256,640]{2,1,0:T(8,128)S(1)}, f32[256,128]{1,0:T(8,128)S(1)}) custom-call(s32[6]{0:T(128)S(1)} %stack.19.refs_0_, f32[8,256,640]{2,1,0:T(8,128)S(1)} %get-tuple-element.57.refs_5_.refs_9_.refs_10_.refs_1_, f32[8,256,640]{2,1,0:T(8,128)S(1)} %get-tuple-element.58.refs_6_.refs_10_.refs_11_.refs_2_, ...), custom_call_target="tpu_custom_call" | custom-call | flops 1 | bytes 1 | tf_op jit(solution)/shard_map/prompt_own_half/pallas_call | solution.py:49
  67.6 0.0 copy-start.4
  67.6 0.0 collective-permute-done.15.refs_4_
  67.6 0.0 collective-permute-done.14.refs_3_
  67.6 0.2 collective-permute-done.13.refs_2_
  67.8 0.9 %final.1.refs_8_.refs_4_ = bf16[4,256,640]{2,1,0:T(8,128)(2,1)S(1)} custom-call(s32[6]{0:T(128)S(1)} %stack.19.refs_0_, bf16[144,640]{1,0:T(8,128)(2,1)S(1)} %get-tuple-element.71.refs_1_, bf16[144,640]{1,0:T(8,128)(2,1)S(1)} %collective-permute-done.13.refs_2_, bf16[144,640]{1,0:T(8,128)(2,1)S(1)} %collective-permute-done.14.refs_3_, ...), custom_call_target="tpu_custom_call" | custom-call | flops 1 | bytes 1 | tf_op jit(solution)/shard_map/final/pallas_call | solution.py:49
  68.8 0.6 collective-permute-start.16
  69.4 0.0 collective-permute-done.12.refs_4_
  69.4 3.2 %prompt_finish.1 = (bf16[256,5120]{1,0:T(8,128)(2,1)}, f32[8,128]{1,0:T(8,128)S(1)}) custom-call(s32[6]{0:T(128)S(1)} %stack.19.refs_0_, f32[8,256,640]{2,1,0:T(8,128)S(1)} %get-tuple-element.57.refs_5_.refs_9_.refs_10_.refs_1_, f32[8,256,640]{2,1,0:T(8,128)S(1)} %get-tuple-element.58.refs_6_.refs_10_.refs_11_.refs_2_, ...), custom_call_target="tpu_custom_call" | custom-call | flops 1 | bytes 1 | tf_op jit(solution)/shard_map/prompt_finish/pallas_call | solution.py:595
  72.6 0.9 %resp_own_half.1 = (f32[4,128,640]{2,1,0:T(8,128)S(1)}, f32[128,128]{1,0:T(8,128)S(1)}) custom-call(s32[6]{0:T(128)S(1)} %stack.19.refs_0_, f32[8,128,640]{2,1,0:T(8,128)S(1)} %get-tuple-element.65.refs_8_.refs_1_, f32[8,128,640]{2,1,0:T(8,128)S(1)} %get-tuple-element.66.refs_9_.refs_2_, bf16[128,256]{1,0:T(8,128)(2,1)S(1)} %get-tuple-element.73.refs_3_, ...), custom_call_target="tpu_custom_call" | custom-call | flops 1 | bytes 1 | tf_op jit(solution)/shard_map/resp_own_half/pallas_call | solution.py:49
  73.5 0.0 collective-permute-done.16.refs_4_
  73.5 2.9 %resp_finish.1 = (bf16[128,5120]{1,0:T(8,128)(2,1)}, f32[8,128]{1,0:T(8,128)}) custom-call(s32[6]{0:T(128)S(1)} %stack.19.refs_0_, f32[8,128,640]{2,1,0:T(8,128)S(1)} %get-tuple-element.65.refs_8_.refs_1_, f32[8,128,640]{2,1,0:T(8,128)S(1)} %get-tuple-element.66.refs_9_.refs_2_, bf16[128,256]{1,0:T(8,128)(2,1)S(1)} %get-tuple-element.73.refs_3_, ...), custom_call_target="tpu_custom_call" | custom-call | flops 1 | bytes 1 | tf_op jit(solution)/shard_map/resp_finish/pallas_call | solution.py:595
  (5 shorter events, 0.0 us)
Async XLA Ops:
  1.5 7.8 %collective-permute-start = (bf16[8,5376]{1,0:T(8,128)(2,1)S(1)}, bf16[8,5376]{1,0:T(8,128)(2,1)S(1)}, u32[]{:S(2)}, u32[]{:S(2)}) collective-permute-start(bf16[8,5376]{1,0:T(8,128)(2,1)S(1)} %slice.3.refs_5_.refs_4_), channel_id=1, source_target_pairs={{0,1},{1,2},{2,3},{3,4},{4,5},{5,6},{6,7},{7,8},{8,9},{9,10},{10,1... | collective-permute-start | bytes 258056 | tf_op jit(solution)/shard_map/ppermute | solution.py:714
  6.8 2.5 %copy-start.8 = (f32[5376]{0:T(1024)S(1)}, f32[5376]{0:T(1024)}, u32[]{:S(2)}) copy-start(f32[5376]{0:T(1024)} %param.23) | copy-start | bytes 64516
  13.5 4.0 %collective-permute-start.1 = (bf16[4,144,640]{2,1,0:T(8,128)(2,1)S(1)}, bf16[4,144,640]{2,1,0:T(8,128)(2,1)S(1)}, u32[]{:S(2)}, u32[]{:S(2)}) collective-permute-start(bf16[4,144,640]{2,1,0:T(8,128)(2,1)S(1)} %get-tuple-element.46.refs_8_), channel_id=1, source_target_pairs={{0,1},{1,0},{2,3},{3,2},{4,5},{5,4},{6,7},{7,6},{8,9},{9,8},{10,11... | collective-permute-start | bytes 2211848 | tf_op jit(solution)/shard_map/ppermute | solution.py:622
  13.6 9.4 %copy-start = (bf16[256,5120]{1,0:T(8,128)(2,1)S(1)}, bf16[256,5120]{1,0:T(8,128)(2,1)}, u32[]{:S(2)}) copy-start(bf16[256,5120]{1,0:T(8,128)(2,1)} %refs_3_.3) | copy-start | bytes 7864324
  17.5 5.5 %copy-start.7 = (f32[80]{0:T(128)S(1)}, f32[80]{0:T(128)}, u32[]{:S(2)}) copy-start(f32[80]{0:T(128)} %param.24) | copy-start | bytes 964
  18.4 9.8 %collective-permute-start.2 = (bf16[144,640]{1,0:T(8,128)(2,1)S(1)}, bf16[144,640]{1,0:T(8,128)(2,1)S(1)}, u32[]{:S(2)}, u32[]{:S(2)}) collective-permute-start(bf16[144,640]{1,0:T(8,128)(2,1)S(1)} %get-tuple-element.54.refs_11_), channel_id=1, source_target_pairs={{0,2},{1,3},{2,4},{3,5},{4,6},{5,7},{6,0},{7,1},{8,10},{9,11},{10,... | collective-permute-start | bytes 552968 | tf_op jit(solution)/shard_map/ppermute | solution.py:622
  19.7 10.7 %collective-permute-start.4 = (bf16[144,640]{1,0:T(8,128)(2,1)S(1)}, bf16[144,640]{1,0:T(8,128)(2,1)S(1)}, u32[]{:S(2)}, u32[]{:S(2)}) collective-permute-start(bf16[144,640]{1,0:T(8,128)(2,1)S(1)} %get-tuple-element.55.refs_12_), channel_id=1, source_target_pairs={{0,4},{1,5},{2,6},{3,7},{4,0},{5,1},{6,2},{7,3},{8,12},{9,13},{10,... | collective-permute-start | bytes 552968 | tf_op jit(solution)/shard_map/ppermute | solution.py:622
  22.2 8.2 %collective-permute-start.3 = (bf16[144,640]{1,0:T(8,128)(2,1)S(1)}, bf16[144,640]{1,0:T(8,128)(2,1)S(1)}, u32[]{:S(2)}, u32[]{:S(2)}) collective-permute-start(bf16[144,640]{1,0:T(8,128)(2,1)S(1)} %get-tuple-element.56.refs_13_), channel_id=1, source_target_pairs={{0,6},{1,7},{2,0},{3,1},{4,2},{5,3},{6,4},{7,5},{8,14},{9,15},{10,... | collective-permute-start | bytes 552968 | tf_op jit(solution)/shard_map/ppermute | solution.py:622
  31.5 24.4 %copy-start.1 = (bf16[1,128,5376]{2,1,0:T(8,128)(2,1)S(1)}, bf16[1,128,5376]{2,1,0:T(8,128)(2,1)}, u32[]{:S(2)}) copy-start(bf16[1,128,5376]{2,1,0:T(8,128)(2,1)} %param.17) | copy-start | bytes 4128772
  31.5 24.4 %copy-start.2 = (bf16[1,128,5120]{2,1,0:T(8,128)(2,1)S(1)}, bf16[1,128,5120]{2,1,0:T(8,128)(2,1)}, u32[]{:S(2)}) copy-start(bf16[1,128,5120]{2,1,0:T(8,128)(2,1)} %param.18) | copy-start | bytes 3932164
  31.5 24.4 %copy-start.3 = (f32[4,5376]{1,0:T(4,128)S(1)}, f32[4,5376]{1,0:T(4,128)}, u32[]{:S(2)}) copy-start(f32[4,5376]{1,0:T(4,128)} %refs_4_.3) | copy-start | bytes 258052
  31.5 24.4 %copy-start.5 = (f32[80,1,128]{2,1,0:T(1,128)S(1)}, f32[80,1,128]{2,1,0:T(1,128)}, u32[]{:S(2)}) copy-start(f32[80,1,128]{2,1,0:T(1,128)} %param.20) | copy-start | bytes 122884
  31.5 24.4 %copy-start.6 = (f32[80,1,128]{2,1,0:T(1,128)S(1)}, f32[80,1,128]{2,1,0:T(1,128)}, u32[]{:S(2)}) copy-start(f32[80,1,128]{2,1,0:T(1,128)} %param.19) | copy-start | bytes 122884
  31.5 8.3 %collective-permute-start.7 = (bf16[144,640]{1,0:T(8,128)(2,1)S(1)}, bf16[144,640]{1,0:T(8,128)(2,1)S(1)}, u32[]{:S(2)}, u32[]{:S(2)}) collective-permute-start(bf16[144,640]{1,0:T(8,128)(2,1)S(1)} %row.1.refs_1_), channel_id=1, source_target_pairs={{0,16},{1,17},{2,18},{3,19},{4,20},{5,21},{6,22},{7,23},{8,24},{9,... | collective-permute-start | bytes 552968 | tf_op jit(solution)/shard_map/ppermute | solution.py:622
  35.9 8.4 %collective-permute-start.6 = (bf16[144,640]{1,0:T(8,128)(2,1)S(1)}, bf16[144,640]{1,0:T(8,128)(2,1)S(1)}, u32[]{:S(2)}, u32[]{:S(2)}) collective-permute-start(bf16[144,640]{1,0:T(8,128)(2,1)S(1)} %row.1.refs_1_), channel_id=1, source_target_pairs={{0,24},{1,25},{2,26},{3,27},{4,28},{5,29},{6,30},{7,31},{8,0},{9,1... | collective-permute-start | bytes 552968 | tf_op jit(solution)/shard_map/ppermute | solution.py:622
  36.7 7.6 %collective-permute-start.5 = (bf16[144,640]{1,0:T(8,128)(2,1)S(1)}, bf16[144,640]{1,0:T(8,128)(2,1)S(1)}, u32[]{:S(2)}, u32[]{:S(2)}) collective-permute-start(bf16[144,640]{1,0:T(8,128)(2,1)S(1)} %row.1.refs_1_), channel_id=1, source_target_pairs={{0,8},{1,9},{2,10},{3,11},{4,12},{5,13},{6,14},{7,15},{8,16},{9,17... | collective-permute-start | bytes 552968 | tf_op jit(solution)/shard_map/ppermute | solution.py:622
  46.6 9.3 %collective-permute-start.8 = (bf16[144,640]{1,0:T(8,128)(2,1)S(1)}, bf16[144,640]{1,0:T(8,128)(2,1)S(1)}, u32[]{:S(2)}, u32[]{:S(2)}) collective-permute-start(bf16[144,640]{1,0:T(8,128)(2,1)S(1)} %get-tuple-element.61.refs_10_), channel_id=1, source_target_pairs={{0,2},{1,3},{2,4},{3,5},{4,6},{5,7},{6,0},{7,1},{8,10},{9,11},{10,... | collective-permute-start | bytes 552968 | tf_op jit(solution)/shard_map/ppermute | solution.py:622
  47.7 6.7 %collective-permute-start.11 = (bf16[16,640]{1,0:T(8,128)(2,1)S(1)}, bf16[16,640]{1,0:T(8,128)(2,1)S(1)}, u32[]{:S(2)}, u32[]{:S(2)}) collective-permute-start(bf16[16,640]{1,0:T(8,128)(2,1)S(1)} %get-tuple-element.64.refs_2_), channel_id=1, source_target_pairs={{0,1},{1,0},{2,3},{3,2},{4,5},{5,4},{6,7},{7,6},{8,9},{9,8},{10,11... | collective-permute-start | bytes 61448 | tf_op jit(solution)/shard_map/ppermute | solution.py:622
  49.3 11.5 %collective-permute-start.9 = (bf16[144,640]{1,0:T(8,128)(2,1)S(1)}, bf16[144,640]{1,0:T(8,128)(2,1)S(1)}, u32[]{:S(2)}, u32[]{:S(2)}) collective-permute-start(bf16[144,640]{1,0:T(8,128)(2,1)S(1)} %get-tuple-element.62.refs_12_), channel_id=1, source_target_pairs={{0,6},{1,7},{2,0},{3,1},{4,2},{5,3},{6,4},{7,5},{8,14},{9,15},{10,... | collective-permute-start | bytes 552968 | tf_op jit(solution)/shard_map/ppermute | solution.py:622
  51.4 9.5 %collective-permute-start.10 = (bf16[144,640]{1,0:T(8,128)(2,1)S(1)}, bf16[144,640]{1,0:T(8,128)(2,1)S(1)}, u32[]{:S(2)}, u32[]{:S(2)}) collective-permute-start(bf16[144,640]{1,0:T(8,128)(2,1)S(1)} %get-tuple-element.63.refs_11_), channel_id=1, source_target_pairs={{0,4},{1,5},{2,6},{3,7},{4,0},{5,1},{6,2},{7,3},{8,12},{9,13},{10,... | collective-permute-start | bytes 552968 | tf_op jit(solution)/shard_map/ppermute | solution.py:622
  52.6 15.0 %collective-permute-start.15 = (bf16[144,640]{1,0:T(8,128)(2,1)S(1)}, bf16[144,640]{1,0:T(8,128)(2,1)S(1)}, u32[]{:S(2)}, u32[]{:S(2)}) collective-permute-start(bf16[144,640]{1,0:T(8,128)(2,1)S(1)} %get-tuple-element.71.refs_1_), channel_id=1, source_target_pairs={{0,4},{1,5},{2,6},{3,7},{4,0},{5,1},{6,2},{7,3},{8,12},{9,13},{10,... | collective-permute-start | bytes 552968 | tf_op jit(solution)/shard_map/ppermute | solution.py:622
  54.4 13.2 %collective-permute-start.14 = (bf16[144,640]{1,0:T(8,128)(2,1)S(1)}, bf16[144,640]{1,0:T(8,128)(2,1)S(1)}, u32[]{:S(2)}, u32[]{:S(2)}) collective-permute-start(bf16[144,640]{1,0:T(8,128)(2,1)S(1)} %get-tuple-element.71.refs_1_), channel_id=1, source_target_pairs={{0,6},{1,7},{2,0},{3,1},{4,2},{5,3},{6,4},{7,5},{8,14},{9,15},{10,... | collective-permute-start | bytes 552968 | tf_op jit(solution)/shard_map/ppermute | solution.py:622
  55.8 12.0 %collective-permute-start.13 = (bf16[144,640]{1,0:T(8,128)(2,1)S(1)}, bf16[144,640]{1,0:T(8,128)(2,1)S(1)}, u32[]{:S(2)}, u32[]{:S(2)}) collective-permute-start(bf16[144,640]{1,0:T(8,128)(2,1)S(1)} %get-tuple-element.71.refs_1_), channel_id=1, source_target_pairs={{0,2},{1,3},{2,4},{3,5},{4,6},{5,7},{6,0},{7,1},{8,10},{9,11},{10,... | collective-permute-start | bytes 552968 | tf_op jit(solution)/shard_map/ppermute | solution.py:622
  62.6 6.8 %collective-permute-start.12 = (bf16[4,256,640]{2,1,0:T(8,128)(2,1)S(1)}, bf16[4,256,640]{2,1,0:T(8,128)(2,1)S(1)}, u32[]{:S(2)}, u32[]{:S(2)}) collective-permute-start(bf16[4,256,640]{2,1,0:T(8,128)(2,1)S(1)} %get-tuple-element.67.refs_5_), channel_id=1, source_target_pairs={{0,1},{1,0},{2,3},{3,2},{4,5},{5,4},{6,7},{7,6},{8,9},{9,8},{10,11... | collective-permute-start | bytes 3932168 | tf_op jit(solution)/shard_map/ppermute | solution.py:622
  67.6 1.8 %copy-start.4 = (f32[5120]{0:T(1024)S(1)}, f32[5120]{0:T(1024)}, u32[]{:S(2)}) copy-start(f32[5120]{0:T(1024)} %param.25) | copy-start | bytes 61444
  68.8 4.8 %collective-permute-start.16 = (bf16[4,256,640]{2,1,0:T(8,128)(2,1)S(1)}, bf16[4,256,640]{2,1,0:T(8,128)(2,1)S(1)}, u32[]{:S(2)}, u32[]{:S(2)}) collective-permute-start(bf16[4,256,640]{2,1,0:T(8,128)(2,1)S(1)} %final.1.refs_8_.refs_4_), channel_id=1, source_target_pairs={{0,1},{1,0},{2,3},{3,2},{4,5},{5,4},{6,7},{7,6},{8,9},{9,8},{10,11... | collective-permute-start | bytes 3932168 | tf_op jit(solution)/shard_map/ppermute | solution.py:622
